TPU v7x, 512 devices: a whole 4x8x8 slice. The times are simulated.
512 devices in a mesh: dp: 128 (over y, z, core), space: 4 (over x).
Axes of the slice: x: 4, y: 8, z: 8, core: 2. Of those that a mesh axis runs over, the one named last changes fastest.
Arguments:
- clips: bfloat16 [256, 4, 16, 32, 128], P('dp', None, 'space'), may hold values from -6 to 6
- lengths: int32 [256], P('dp'), may hold values from 1 to 2
- partner: int32 [1], replicated, may hold values from 1 to 127
- kernel: bfloat16 [3, 3, 3, 128, 128], replicated, may hold values from -0.109375 to 0.109375
- cot_stay: bfloat16 [128, 2, 16, 32, 128], P('dp', None, 'space'), may hold values from -6 to 6
- cot_guest: bfloat16 [128, 2, 16, 32, 128], P('dp', None, 'space'), may hold values from -6 to 6
Outputs:
- stay_out: bfloat16 [128, 2, 16, 32, 128], P('dp', None, 'space')
- guest_out: bfloat16 [128, 2, 16, 32, 128], P('dp', None, 'space')
- slab_grad: bfloat16 [256, 4, 16, 32, 128], P('dp', None, 'space')
- weight_grad: float32 [3, 3, 3, 128, 128], replicated
Inputs may be any that keep to these rules, and one draw needn't show every extreme that they name: `partner`: one offset for the whole mesh.
All inputs are finite; a program needn't handle non-finite values.
Results may differ from a plain program's by a relative error of at most 0.0049.
Values may be sent and summed in bfloat16 or wider, within the bound.
No kernel may reach another device: no remote copies, remote signals or barrier semaphores. Data moves between devices by JAX's collectives and lax.ppermute only.
A program may use at most 64 MiB of HBM per device.

v0:
```python
import math

import jax
import jax.numpy as jnp
from jax import lax
from jax.sharding import PartitionSpec as P


def extended(block, sides, width):
    for axis, dim in sides:
        count = lax.axis_size(axis)
        forward = [(i, i + 1) for i in range(count - 1)]
        backward = [(target, source) for source, target in forward]
        low = lax.ppermute(
            lax.slice_in_dim(block, block.shape[dim] - width, None, axis=dim), axis, forward
        )
        high = lax.ppermute(lax.slice_in_dim(block, 0, width, axis=dim), axis, backward)
        block = jnp.concatenate([low, block, high], axis=dim)
    return block


def for_sending(shard):

    def short(part):
        return part.astype(jnp.bfloat16) if part.dtype == jnp.float32 else part

    return jax.tree.map(short, shard)


def partner_2(value, axis, stride):
    mask = 2**stride
    pairs = [(source, source ^ mask) for source in range(lax.axis_size(axis))]
    return lax.ppermute(value, axis, pairs)


def block_pass(stack, masks, cots, kernel):
    frames = cots.shape[1]
    rows = stack.shape[2]
    width = stack.shape[3]
    channels = stack.shape[4]
    padded = extended(stack, (("space", 2),), 1)
    z_val = lax.conv_general_dilated(
        padded,
        kernel,
        (1, 1, 1),
        ((0, 0), (0, 0), (1, 1)),
        dimension_numbers=("NDHWC", "DHWIO", "NDHWC"),
        preferred_element_type=jnp.float32,
    )
    valid = masks[:, :, None, None, None]
    sig = jax.nn.sigmoid(z_val)
    outputs = (valid * z_val * sig).astype(jnp.bfloat16)
    dz_val = (valid * cots.astype(jnp.float32) * sig * (1.0 + z_val * (1.0 - sig))).astype(
        jnp.bfloat16
    )
    dz_rows = extended(dz_val, (("space", 2),), 1)
    flipped = jnp.transpose(kernel[::-1, ::-1, ::-1], (0, 1, 2, 4, 3))
    grads = lax.conv_general_dilated(
        dz_rows,
        flipped,
        (1, 1, 1),
        ((2, 2), (0, 0), (1, 1)),
        dimension_numbers=("NDHWC", "DHWIO", "NDHWC"),
        preferred_element_type=jnp.float32,
    ).astype(jnp.bfloat16)
    wide = jnp.pad(padded, ((0, 0), (0, 0), (0, 0), (1, 1), (0, 0)))
    taps = []
    for tap_t in range(3):
        for tap_h in range(3):
            for tap_w in range(3):
                window = wide[
                    :, tap_t : tap_t + frames, tap_h : tap_h + rows, tap_w : tap_w + width
                ]
                taps.append(
                    jnp.einsum(
                        "nthwc,nthwo->co", window, dz_val, preferred_element_type=jnp.float32
                    )
                )
    kernel_part = jnp.stack(taps).reshape(3, 3, 3, channels, channels)
    return (outputs, grads, kernel_part)


def shards(clips, lengths, partner, kernel, cot_stay, cot_guest):
    frames = cot_stay.shape[1]
    rows = clips.shape[2]
    width = clips.shape[3]
    levels = lax.axis_size("dp").bit_length() - 1
    offset = partner[0]

    def route(payload, mover):
        for level in range(levels):
            flag = jnp.bitwise_and(jnp.right_shift(offset, level), 1) == 1
            other = mover(payload, level)
            payload = jax.tree.map(
                lambda mine, theirs: jnp.where(flag, theirs, mine), payload, other
            )
        return payload

    valid = (jnp.arange(frames, dtype=jnp.int32)[None, :] < lengths[:, None]).astype(jnp.float32)
    moved, moved_valid = route(
        (clips[1], valid[1].astype(jnp.bfloat16)),
        lambda item, level: jax.tree.map(
            lambda part, own: part.astype(own.dtype),
            partner_2(for_sending(item), "dp", level),
            item,
        ),
    )
    stack = jnp.stack([clips[0], moved])
    masks = jnp.stack([valid[0], moved_valid.astype(jnp.float32)])
    cots = jnp.concatenate([cot_stay, cot_guest], axis=0)
    outputs, grads, kernel_part = block_pass(stack, masks, cots, kernel)
    returned = route(
        grads[1],
        lambda item, level: jax.tree.map(
            lambda part, own: part.astype(own.dtype),
            partner_2(for_sending(item), "dp", level),
            item,
        ),
    )
    stay_out = outputs[0:1]
    guest_out = outputs[1:2]
    slab_grad = jnp.stack([grads[0], returned])
    positions = lax.axis_size("dp") * 2 * frames * lax.axis_size("space") * rows * width
    weight_grad = lax.psum(kernel_part, ("dp", "space")) / math.sqrt(positions)
    return (stay_out, guest_out, slab_grad, weight_grad)


def solution(mesh):
    placed = (
        P("dp", None, "space", None, None),
        P("dp"),
        P(),
        P(),
        P("dp", None, "space", None, None),
        P("dp", None, "space", None, None),
    )
    return jax.shard_map(
        shards,
        mesh=mesh,
        in_specs=placed,
        out_specs=(
            P("dp", None, "space", None, None),
            P("dp", None, "space", None, None),
            P("dp", None, "space", None, None),
            P(),
        ),
        check_vma=False,
    )
```

profile of v0, /device:TPU:1, one launch (start us, length us, event | category | flops | bytes accessed | tf_op | source)
XLA Modules:
  0.0 428.0 jit_solution(17350311426370947572)
XLA Ops:
  8.3 8.8 %collective-permute-start.7 = (bf16[4,4,32,128]{3,2,0,1:T(8,128)(2,1)S(1)}, bf16[4,4,32,128]{3,2,0,1:T(8,128)(2,1)S(1)}, u32[]{:S(2)}, u32[]{:S(2)}) collective-permute-start(bf16[4,4,32,128]{3,2,0,1:T(8,128)(2,1)S(1)} %bitcast.298), channel_id=1, source_target_pairs={{0,4},{4,0},{8,12},{12,8},{16,20},{20,16},{24,28},{28,24},{32,36},... | collective-permute-start | bytes 393224 | tf_op jit(solution)/shard_map/ppermute | solution.py:33
  22.8 3.4 collective-permute-start.8
  32.4 7.3 %collective-permute-start.3 = (bf16[2]{0:T(256)(128)(2,1)S(1)}, bf16[2]{0:T(256)(128)(2,1)S(1)}, u32[]{:S(2)}, u32[]{:S(2)}) collective-permute-start(bf16[2]{0:T(256)(128)(2,1)S(1)} %broadcast_select_fusion.14), channel_id=1, source_target_pairs={{0,32},{4,36},{8,40},{12,44},{16,48},{20,52},{24,56},{28,60},{32,0... | collective-permute-start | bytes 20 | tf_op jit(solution)/shard_map/ppermute | solution.py:33
  39.8 6.2 %collective-permute-start.10 = (bf16[4,4,32,128]{3,2,0,1:T(8,128)(2,1)S(1)}, bf16[4,4,32,128]{3,2,0,1:T(8,128)(2,1)S(1)}, u32[]{:S(2)}, u32[]{:S(2)}) collective-permute-start(bf16[4,4,32,128]{3,2,0,1:T(8,128)(2,1)S(1)} %broadcast_select_fusion.5), channel_id=1, source_target_pairs={{0,32},{4,36},{8,40},{12,44},{16,48},{20,52},{24,56},{28,60},{32,0... | collective-permute-start | bytes 393224 | tf_op jit(solution)/shard_map/ppermute | solution.py:33
  46.1 3.2 collective-permute-start.4
  51.2 3.3 collective-permute-start.11
  54.6 4.2 collective-permute-start.5
  61.3 6.1 %collective-permute-start.6 = (bf16[2]{0:T(256)(128)(2,1)S(1)}, bf16[2]{0:T(256)(128)(2,1)S(1)}, u32[]{:S(2)}, u32[]{:S(2)}) collective-permute-start(bf16[2]{0:T(256)(128)(2,1)S(1)} %broadcast_select_fusion.17), channel_id=1, source_target_pairs={{0,256},{4,260},{8,264},{12,268},{16,272},{20,276},{24,280},{28,28... | collective-permute-start | bytes 20 | tf_op jit(solution)/shard_map/ppermute | solution.py:33
  67.4 5.1 %collective-permute-start.13 = (bf16[4,4,32,128]{3,2,0,1:T(8,128)(2,1)S(1)}, bf16[4,4,32,128]{3,2,0,1:T(8,128)(2,1)S(1)}, u32[]{:S(2)}, u32[]{:S(2)}) collective-permute-start(bf16[4,4,32,128]{3,2,0,1:T(8,128)(2,1)S(1)} %broadcast_select_fusion.11), channel_id=1, source_target_pairs={{0,256},{4,260},{8,264},{12,268},{16,272},{20,276},{24,280},{28,28... | collective-permute-start | bytes 393224 | tf_op jit(solution)/shard_map/ppermute | solution.py:33
  72.6 5.9 %collective-permute-done.13 = bf16[4,4,32,128]{3,2,0,1:T(8,128)(2,1)S(1)} collective-permute-done((bf16[4,4,32,128]{3,2,0,1:T(8,128)(2,1)S(1)}, bf16[4,4,32,128]{3,2,0,1:T(8,128)(2,1)S(1)}, u32[]{:S(2)}, u32[]{:S(2)}) %collective-permute-start.13) | collective-permute-done | bytes 131104 | tf_op jit(solution)/shard_map/ppermute | solution.py:33
  78.5 3.1 collective-permute-start.14
  83.0 3.6 collective-permute-done.15
  96.0 3.1 collective-permute-start.16
  100.7 3.1 collective-permute-done.17
  107.4 10.1 %collective-permute-start.18 = (bf16[4,4,32,128]{3,2,0,1:T(8,128)(2,1)S(1)}, bf16[4,4,32,128]{3,2,0,1:T(8,128)(2,1)S(1)}, u32[]{:S(2)}, u32[]{:S(2)}) collective-permute-start(bf16[4,4,32,128]{3,2,0,1:T(8,128)(2,1)S(1)} %get-tuple-element.22), channel_id=1, source_target_pairs={{0,4},{4,0},{8,12},{12,8},{16,20},{20,16},{24,28},{28,24},{32,36},... | collective-permute-start | bytes 393224 | tf_op jit(solution)/shard_map/ppermute | solution.py:33
  120.6 4.4 %collective-permute-done.19 = bf16[4,4,32,128]{3,2,0,1:T(8,128)(2,1)S(1)} collective-permute-done((bf16[4,4,32,128]{3,2,0,1:T(8,128)(2,1)S(1)}, bf16[4,4,32,128]{3,2,0,1:T(8,128)(2,1)S(1)}, u32[]{:S(2)}, u32[]{:S(2)}) %collective-permute-start.19) | collective-permute-done | bytes 131104 | tf_op jit(solution)/shard_map/ppermute | solution.py:33
  127.2 8.4 %collective-permute-done.20 = bf16[4,4,32,128]{3,2,0,1:T(8,128)(2,1)S(1)} collective-permute-done((bf16[4,4,32,128]{3,2,0,1:T(8,128)(2,1)S(1)}, bf16[4,4,32,128]{3,2,0,1:T(8,128)(2,1)S(1)}, u32[]{:S(2)}, u32[]{:S(2)}) %collective-permute-start.20) | collective-permute-done | bytes 131104 | tf_op jit(solution)/shard_map/ppermute | solution.py:33
  135.7 6.2 %collective-permute-start.21 = (bf16[4,4,32,128]{3,2,0,1:T(8,128)(2,1)S(1)}, bf16[4,4,32,128]{3,2,0,1:T(8,128)(2,1)S(1)}, u32[]{:S(2)}, u32[]{:S(2)}) collective-permute-start(bf16[4,4,32,128]{3,2,0,1:T(8,128)(2,1)S(1)} %broadcast_select_fusion.4), channel_id=1, source_target_pairs={{0,32},{4,36},{8,40},{12,44},{16,48},{20,52},{24,56},{28,60},{32,0... | collective-permute-start | bytes 393224 | tf_op jit(solution)/shard_map/ppermute | solution.py:33
  143.4 5.2 %collective-permute-done.21 = bf16[4,4,32,128]{3,2,0,1:T(8,128)(2,1)S(1)} collective-permute-done((bf16[4,4,32,128]{3,2,0,1:T(8,128)(2,1)S(1)}, bf16[4,4,32,128]{3,2,0,1:T(8,128)(2,1)S(1)}, u32[]{:S(2)}, u32[]{:S(2)}) %collective-permute-start.21) | collective-permute-done | bytes 131104 | tf_op jit(solution)/shard_map/ppermute | solution.py:33
  151.4 3.4 collective-permute-done.22
  154.9 4.7 %collective-permute-start.23 = (bf16[4,4,32,128]{3,2,0,1:T(8,128)(2,1)S(1)}, bf16[4,4,32,128]{3,2,0,1:T(8,128)(2,1)S(1)}, u32[]{:S(2)}, u32[]{:S(2)}) collective-permute-start(bf16[4,4,32,128]{3,2,0,1:T(8,128)(2,1)S(1)} %broadcast_select_fusion.8), channel_id=1, source_target_pairs={{0,128},{4,132},{8,136},{12,140},{16,144},{20,148},{24,152},{28,15... | collective-permute-start | bytes 393224 | tf_op jit(solution)/shard_map/ppermute | solution.py:33
  160.9 5.0 %collective-permute-done.23 = bf16[4,4,32,128]{3,2,0,1:T(8,128)(2,1)S(1)} collective-permute-done((bf16[4,4,32,128]{3,2,0,1:T(8,128)(2,1)S(1)}, bf16[4,4,32,128]{3,2,0,1:T(8,128)(2,1)S(1)}, u32[]{:S(2)}, u32[]{:S(2)}) %collective-permute-start.23) | collective-permute-done | bytes 131104 | tf_op jit(solution)/shard_map/ppermute | solution.py:33
  165.9 3.6 collective-permute-start.24
  169.6 247.9 %all-reduce.3.cloned.1.call-done = f32[3,3,3,128,128]{4,3,2,1,0:T(8,128)} async-done(((f32[3,3,3,128,128]{4,3,2,1,0:T(8,128)}), f32[3,3,3,128,128]{4,3,2,1,0:T(8,128)}) %all-reduce.3.cloned.1.call-update) | async-done | bytes 1769488 | tf_op jit(solution)/shard_map/psum | solution.py:124
  (126 shorter events, 46.9 us)
Async XLA Ops:
  7.2 410.3 %all-reduce.3.cloned.1.call-start = ((), (), s32[]{:S(2)}) async-start(), calls=%async_computation | async-start | bytes 3538944 | tf_op jit(solution)/shard_map/psum | solution.py:124
  8.3 14.5 %collective-permute-start.7 = (bf16[4,4,32,128]{3,2,0,1:T(8,128)(2,1)S(1)}, bf16[4,4,32,128]{3,2,0,1:T(8,128)(2,1)S(1)}, u32[]{:S(2)}, u32[]{:S(2)}) collective-permute-start(bf16[4,4,32,128]{3,2,0,1:T(8,128)(2,1)S(1)} %bitcast.298), channel_id=1, source_target_pairs={{0,4},{4,0},{8,12},{12,8},{16,20},{20,16},{24,28},{28,24},{32,36},... | collective-permute-start | bytes 393224 | tf_op jit(solution)/shard_map/ppermute | solution.py:33
  20.8 5.3 %collective-permute-start.1 = (bf16[2]{0:T(256)(128)(2,1)S(1)}, bf16[2]{0:T(256)(128)(2,1)S(1)}, u32[]{:S(2)}, u32[]{:S(2)}) collective-permute-start(bf16[2]{0:T(256)(128)(2,1)S(1)} %broadcast_select_fusion.12), channel_id=1, source_target_pairs={{0,8},{4,12},{8,0},{12,4},{16,24},{20,28},{24,16},{28,20},{32,40},... | collective-permute-start | bytes 20 | tf_op jit(solution)/shard_map/ppermute | solution.py:33
  22.8 6.8 %collective-permute-start.8 = (bf16[4,4,32,128]{3,2,0,1:T(8,128)(2,1)S(1)}, bf16[4,4,32,128]{3,2,0,1:T(8,128)(2,1)S(1)}, u32[]{:S(2)}, u32[]{:S(2)}) collective-permute-start(bf16[4,4,32,128]{3,2,0,1:T(8,128)(2,1)S(1)} %broadcast_select_fusion.1), channel_id=1, source_target_pairs={{0,8},{4,12},{8,0},{12,4},{16,24},{20,28},{24,16},{28,20},{32,40},... | collective-permute-start | bytes 393224 | tf_op jit(solution)/shard_map/ppermute | solution.py:33
  26.2 6.2 %collective-permute-start.2 = (bf16[2]{0:T(256)(128)(2,1)S(1)}, bf16[2]{0:T(256)(128)(2,1)S(1)}, u32[]{:S(2)}, u32[]{:S(2)}) collective-permute-start(bf16[2]{0:T(256)(128)(2,1)S(1)} %broadcast_select_fusion.13), channel_id=1, source_target_pairs={{0,16},{4,20},{8,24},{12,28},{16,0},{20,4},{24,8},{28,12},{32,48},... | collective-permute-start | bytes 20 | tf_op jit(solution)/shard_map/ppermute | solution.py:33
  29.6 10.2 %collective-permute-start.9 = (bf16[4,4,32,128]{3,2,0,1:T(8,128)(2,1)S(1)}, bf16[4,4,32,128]{3,2,0,1:T(8,128)(2,1)S(1)}, u32[]{:S(2)}, u32[]{:S(2)}) collective-permute-start(bf16[4,4,32,128]{3,2,0,1:T(8,128)(2,1)S(1)} %broadcast_select_fusion.3), channel_id=1, source_target_pairs={{0,16},{4,20},{8,24},{12,28},{16,0},{20,4},{24,8},{28,12},{32,48},... | collective-permute-start | bytes 393224 | tf_op jit(solution)/shard_map/ppermute | solution.py:33
  32.4 13.6 %collective-permute-start.3 = (bf16[2]{0:T(256)(128)(2,1)S(1)}, bf16[2]{0:T(256)(128)(2,1)S(1)}, u32[]{:S(2)}, u32[]{:S(2)}) collective-permute-start(bf16[2]{0:T(256)(128)(2,1)S(1)} %broadcast_select_fusion.14), channel_id=1, source_target_pairs={{0,32},{4,36},{8,40},{12,44},{16,48},{20,52},{24,56},{28,60},{32,0... | collective-permute-start | bytes 20 | tf_op jit(solution)/shard_map/ppermute | solution.py:33
  39.8 11.4 %collective-permute-start.10 = (bf16[4,4,32,128]{3,2,0,1:T(8,128)(2,1)S(1)}, bf16[4,4,32,128]{3,2,0,1:T(8,128)(2,1)S(1)}, u32[]{:S(2)}, u32[]{:S(2)}) collective-permute-start(bf16[4,4,32,128]{3,2,0,1:T(8,128)(2,1)S(1)} %broadcast_select_fusion.5), channel_id=1, source_target_pairs={{0,32},{4,36},{8,40},{12,44},{16,48},{20,52},{24,56},{28,60},{32,0... | collective-permute-start | bytes 393224 | tf_op jit(solution)/shard_map/ppermute | solution.py:33
  46.1 8.5 %collective-permute-start.4 = (bf16[2]{0:T(256)(128)(2,1)S(1)}, bf16[2]{0:T(256)(128)(2,1)S(1)}, u32[]{:S(2)}, u32[]{:S(2)}) collective-permute-start(bf16[2]{0:T(256)(128)(2,1)S(1)} %broadcast_select_fusion.15), channel_id=1, source_target_pairs={{0,64},{4,68},{8,72},{12,76},{16,80},{20,84},{24,88},{28,92},{32,9... | collective-permute-start | bytes 20 | tf_op jit(solution)/shard_map/ppermute | solution.py:33
  51.2 7.6 %collective-permute-start.11 = (bf16[4,4,32,128]{3,2,0,1:T(8,128)(2,1)S(1)}, bf16[4,4,32,128]{3,2,0,1:T(8,128)(2,1)S(1)}, u32[]{:S(2)}, u32[]{:S(2)}) collective-permute-start(bf16[4,4,32,128]{3,2,0,1:T(8,128)(2,1)S(1)} %broadcast_select_fusion.7), channel_id=1, source_target_pairs={{0,64},{4,68},{8,72},{12,76},{16,80},{20,84},{24,88},{28,92},{32,9... | collective-permute-start | bytes 393224 | tf_op jit(solution)/shard_map/ppermute | solution.py:33
  54.6 6.7 %collective-permute-start.5 = (bf16[2]{0:T(256)(128)(2,1)S(1)}, bf16[2]{0:T(256)(128)(2,1)S(1)}, u32[]{:S(2)}, u32[]{:S(2)}) collective-permute-start(bf16[2]{0:T(256)(128)(2,1)S(1)} %broadcast_select_fusion.16), channel_id=1, source_target_pairs={{0,128},{4,132},{8,136},{12,140},{16,144},{20,148},{24,152},{28,15... | collective-permute-start | bytes 20 | tf_op jit(solution)/shard_map/ppermute | solution.py:33
  58.8 8.6 %collective-permute-start.12 = (bf16[4,4,32,128]{3,2,0,1:T(8,128)(2,1)S(1)}, bf16[4,4,32,128]{3,2,0,1:T(8,128)(2,1)S(1)}, u32[]{:S(2)}, u32[]{:S(2)}) collective-permute-start(bf16[4,4,32,128]{3,2,0,1:T(8,128)(2,1)S(1)} %broadcast_select_fusion.9), channel_id=1, source_target_pairs={{0,128},{4,132},{8,136},{12,140},{16,144},{20,148},{24,152},{28,15... | collective-permute-start | bytes 393224 | tf_op jit(solution)/shard_map/ppermute | solution.py:33
  61.3 11.3 %collective-permute-start.6 = (bf16[2]{0:T(256)(128)(2,1)S(1)}, bf16[2]{0:T(256)(128)(2,1)S(1)}, u32[]{:S(2)}, u32[]{:S(2)}) collective-permute-start(bf16[2]{0:T(256)(128)(2,1)S(1)} %broadcast_select_fusion.17), channel_id=1, source_target_pairs={{0,256},{4,260},{8,264},{12,268},{16,272},{20,276},{24,280},{28,28... | collective-permute-start | bytes 20 | tf_op jit(solution)/shard_map/ppermute | solution.py:33
  67.4 11.0 %collective-permute-start.13 = (bf16[4,4,32,128]{3,2,0,1:T(8,128)(2,1)S(1)}, bf16[4,4,32,128]{3,2,0,1:T(8,128)(2,1)S(1)}, u32[]{:S(2)}, u32[]{:S(2)}) collective-permute-start(bf16[4,4,32,128]{3,2,0,1:T(8,128)(2,1)S(1)} %broadcast_select_fusion.11), channel_id=1, source_target_pairs={{0,256},{4,260},{8,264},{12,268},{16,272},{20,276},{24,280},{28,28... | collective-permute-start | bytes 393224 | tf_op jit(solution)/shard_map/ppermute | solution.py:33
  81.6 5.0 %collective-permute-start.15 = (bf16[2,4,1,32,128]{4,3,1,0,2:T(8,128)(2,1)S(1)}, bf16[2,4,1,32,128]{4,3,1,0,2:T(8,128)(2,1)S(1)}, u32[]{:S(2)}, u32[]{:S(2)}) collective-permute-start(bf16[2,4,1,32,128]{4,3,1,0,2:T(8,128)(2,1)S(1)} %get-tuple-element.24), channel_id=1, source_target_pairs={{1,0},{2,1},{3,2},{5,4},{6,5},{7,6},{9,8},{10,9},{11,10},{13,12},{... | collective-permute-start | bytes 196616 | tf_op jit(solution)/shard_map/ppermute | solution.py:17
  96.0 4.7 %collective-permute-start.16 = (bf16[2,2,1,32,128]{4,3,2,1,0:T(8,128)(2,1)S(1)}, bf16[2,2,1,32,128]{4,3,2,1,0:T(8,128)(2,1)S(1)}, u32[]{:S(2)}, u32[]{:S(2)}) collective-permute-start(bf16[2,2,1,32,128]{4,3,2,1,0:T(8,128)(2,1)S(1)} %get-tuple-element.27), channel_id=1, source_target_pairs={{0,1},{1,2},{2,3},{4,5},{5,6},{6,7},{8,9},{9,10},{10,11},{12,13},{... | collective-permute-start | bytes 98312 | tf_op jit(solution)/shard_map/ppermute | solution.py:14
  99.1 4.7 %collective-permute-start.17 = (bf16[2,2,1,32,128]{4,3,2,1,0:T(8,128)(2,1)S(1)}, bf16[2,2,1,32,128]{4,3,2,1,0:T(8,128)(2,1)S(1)}, u32[]{:S(2)}, u32[]{:S(2)}) collective-permute-start(bf16[2,2,1,32,128]{4,3,2,1,0:T(8,128)(2,1)S(1)} %get-tuple-element.28), channel_id=1, source_target_pairs={{1,0},{2,1},{3,2},{5,4},{6,5},{7,6},{9,8},{10,9},{11,10},{13,12},{... | collective-permute-start | bytes 98312 | tf_op jit(solution)/shard_map/ppermute | solution.py:17
  107.4 11.0 %collective-permute-start.18 = (bf16[4,4,32,128]{3,2,0,1:T(8,128)(2,1)S(1)}, bf16[4,4,32,128]{3,2,0,1:T(8,128)(2,1)S(1)}, u32[]{:S(2)}, u32[]{:S(2)}) collective-permute-start(bf16[4,4,32,128]{3,2,0,1:T(8,128)(2,1)S(1)} %get-tuple-element.22), channel_id=1, source_target_pairs={{0,4},{4,0},{8,12},{12,8},{16,20},{20,16},{24,28},{28,24},{32,36},... | collective-permute-start | bytes 393224 | tf_op jit(solution)/shard_map/ppermute | solution.py:33
  118.4 6.6 %collective-permute-start.19 = (bf16[4,4,32,128]{3,2,0,1:T(8,128)(2,1)S(1)}, bf16[4,4,32,128]{3,2,0,1:T(8,128)(2,1)S(1)}, u32[]{:S(2)}, u32[]{:S(2)}) collective-permute-start(bf16[4,4,32,128]{3,2,0,1:T(8,128)(2,1)S(1)} %broadcast_select_fusion), channel_id=1, source_target_pairs={{0,8},{4,12},{8,0},{12,4},{16,24},{20,28},{24,16},{28,20},{32,40},... | collective-permute-start | bytes 393224 | tf_op jit(solution)/shard_map/ppermute | solution.py:33
  125.0 10.6 %collective-permute-start.20 = (bf16[4,4,32,128]{3,2,0,1:T(8,128)(2,1)S(1)}, bf16[4,4,32,128]{3,2,0,1:T(8,128)(2,1)S(1)}, u32[]{:S(2)}, u32[]{:S(2)}) collective-permute-start(bf16[4,4,32,128]{3,2,0,1:T(8,128)(2,1)S(1)} %broadcast_select_fusion.2), channel_id=1, source_target_pairs={{0,16},{4,20},{8,24},{12,28},{16,0},{20,4},{24,8},{28,12},{32,48},... | collective-permute-start | bytes 393224 | tf_op jit(solution)/shard_map/ppermute | solution.py:33
  135.7 13.0 %collective-permute-start.21 = (bf16[4,4,32,128]{3,2,0,1:T(8,128)(2,1)S(1)}, bf16[4,4,32,128]{3,2,0,1:T(8,128)(2,1)S(1)}, u32[]{:S(2)}, u32[]{:S(2)}) collective-permute-start(bf16[4,4,32,128]{3,2,0,1:T(8,128)(2,1)S(1)} %broadcast_select_fusion.4), channel_id=1, source_target_pairs={{0,32},{4,36},{8,40},{12,44},{16,48},{20,52},{24,56},{28,60},{32,0... | collective-permute-start | bytes 393224 | tf_op jit(solution)/shard_map/ppermute | solution.py:33
  148.7 6.2 %collective-permute-start.22 = (bf16[4,4,32,128]{3,2,0,1:T(8,128)(2,1)S(1)}, bf16[4,4,32,128]{3,2,0,1:T(8,128)(2,1)S(1)}, u32[]{:S(2)}, u32[]{:S(2)}) collective-permute-start(bf16[4,4,32,128]{3,2,0,1:T(8,128)(2,1)S(1)} %broadcast_select_fusion.6), channel_id=1, source_target_pairs={{0,64},{4,68},{8,72},{12,76},{16,80},{20,84},{24,88},{28,92},{32,9... | collective-permute-start | bytes 393224 | tf_op jit(solution)/shard_map/ppermute | solution.py:33
  154.9 11.0 %collective-permute-start.23 = (bf16[4,4,32,128]{3,2,0,1:T(8,128)(2,1)S(1)}, bf16[4,4,32,128]{3,2,0,1:T(8,128)(2,1)S(1)}, u32[]{:S(2)}, u32[]{:S(2)}) collective-permute-start(bf16[4,4,32,128]{3,2,0,1:T(8,128)(2,1)S(1)} %broadcast_select_fusion.8), channel_id=1, source_target_pairs={{0,128},{4,132},{8,136},{12,140},{16,144},{20,148},{24,152},{28,15... | collective-permute-start | bytes 393224 | tf_op jit(solution)/shard_map/ppermute | solution.py:33
  165.9 254.4 %collective-permute-start.24 = (bf16[4,4,32,128]{3,2,0,1:T(8,128)(2,1)S(1)}, bf16[4,4,32,128]{3,2,0,1:T(8,128)(2,1)S(1)}, u32[]{:S(2)}, u32[]{:S(2)}) collective-permute-start(bf16[4,4,32,128]{3,2,0,1:T(8,128)(2,1)S(1)} %broadcast_select_fusion.10), channel_id=1, source_target_pairs={{0,256},{4,260},{8,264},{12,268},{16,272},{20,276},{24,280},{28,28... | collective-permute-start | bytes 393224 | tf_op jit(solution)/shard_map/ppermute | solution.py:33
  (7 other events, 93.3 us)
Sparse Core Ops, SparseCore 0:
  143.5 273.9 all-reduce.2
where the time goes:
time: 429 us; the launch traced here: 428 us
  waiting for transfers between devices  292 us (68%)
  starting transfers between devices  98.6 us (23%)
  between operations  15.6 us (4%)
  matrix products  10.1 us (2%)
  local copies, waits for them, and re-layouts  7.11 us (2%)
  other arithmetic  5.03 us (1%)
    psum x1, waiting for transfers between devices, shards(): weight_grad = lax.psum(kernel_part, ('dp', 'space')) / math.sqrt(positions)  248 us
    ppermute x21, starting transfers between devices, partner_2(): return lax.ppermute(value, axis, pairs)  89.8 us
    ppermute x21, waiting for transfers between devices, partner_2(): return lax.ppermute(value, axis, pairs)  37 us
  transfers between devices with their start and end apart: 26, of which 13 were waited for; matrix products, arithmetic and copies ran while one was open for 2% of the time, Pallas kernels for 0%

commit v1 on v0

v1 whole, which is shorter than its diff:
```python
import functools
import math

import jax
import jax.numpy as jnp
from jax import lax
from jax.experimental import pallas as pl
from jax.experimental.pallas import tpu as pltpu
from jax.sharding import Mesh
from jax.sharding import PartitionSpec as P

BF = jnp.bfloat16
F32 = jnp.float32
TAPS = 27
PADDED_TAPS = 32


def shifted_columns(rows, width):
    count = rows.shape[0]
    column = lax.broadcasted_iota(jnp.int32, rows.shape, 0) % width
    before = jnp.where(column == 0, 0.0, pltpu.roll(rows, 1, 0))
    after = jnp.where(column == width - 1, 0.0, pltpu.roll(rows, count - 1, 0))
    return before, after


def forward_kernel(lengths, core, clips, low, high, kernel, cot_stay, cot_guest,
                   y_stay, y_guest, dz_out, dz_first, dz_last, mine, other, wide, sums):
    slabs, frames, rows, width, chans = clips.shape
    out_frames = frames - 2
    x = jnp.concatenate([low[...], clips[...], high[...]], axis=2).reshape(-1, chans)
    shape = (slabs, frames, rows + 2, width, chans)
    before, after = shifted_columns(x.astype(F32), width)
    wide[:, :, :, :, 0:chans] = before.astype(BF).reshape(shape)
    wide[:, :, :, :, chans : 2 * chans] = x.reshape(shape)
    wide[:, :, :, :, 2 * chans :] = after.astype(BF).reshape(shape)
    places = slabs * out_frames * rows * width

    def window(tap_t, tap_h):
        return wide[:, tap_t : tap_t + out_frames, tap_h : tap_h + rows].reshape(places, 3 * chans)

    z = jnp.zeros((places, chans), F32)
    for tap in range(9):
        z = z + jnp.dot(window(tap // 3, tap % 3), kernel[tap], preferred_element_type=F32)
    sig = 1.0 / (1.0 + jnp.exp(-z))
    per = rows * width
    y = z * sig
    slope = sig * (1.0 + z * (1.0 - sig))
    parts = []
    for slab, (cot, out) in enumerate(((cot_stay, y_stay), (cot_guest, y_guest))):
        for frame in range(out_frames):
            valid = jnp.where(lengths[slab] > frame, 1.0, 0.0)
            at = (slab * out_frames + frame) * per
            out[frame] = (valid * y[at : at + per]).astype(BF).reshape(rows, width, chans)
            grad = cot[frame].reshape(per, chans).astype(F32)
            dz = (valid * grad * slope[at : at + per]).astype(BF)
            parts.append(dz)
            dz = dz.reshape(rows, width, chans)
            dz_out[slab, frame] = dz
            dz_first[slab, frame] = dz[0:1]
            dz_last[slab, frame] = dz[rows - 1 : rows]
    dz_all = jnp.concatenate(parts, axis=0)
    for tap in range(9):
        term = lax.dot_general(window(tap // 3, tap % 3), dz_all, (((0,), (0,)), ((), ())), preferred_element_type=F32)
        sums[3 * tap : 3 * tap + 3] = term.reshape(3, chans, chans)
    half = chans // 2
    own = core[0]
    mine[...] = sums[:, pl.ds(pl.multiple_of(own * half, half), half), :]
    other[...] = sums[:, pl.ds(pl.multiple_of((1 - own) * half, half), half), :].astype(BF)


def backward_kernel(dz, low, high, kernel, grads, wide):
    slabs, frames, rows, width, chans = dz.shape
    x = jnp.concatenate([low[...], dz[...], high[...]], axis=2).reshape(-1, chans)
    shape = (slabs, frames, rows + 2, width, chans)
    before, after = shifted_columns(x.astype(F32), width)
    wide[:, :, :, :, 0:chans] = after.astype(BF).reshape(shape)
    wide[:, :, :, :, chans : 2 * chans] = x.reshape(shape)
    wide[:, :, :, :, 2 * chans :] = before.astype(BF).reshape(shape)
    per = rows * width
    planes = []
    for tap_t in range(3):
        total = jnp.zeros((slabs * frames * per, chans), F32)
        for tap_h in range(3):
            rows_in = wide[:, :, 2 - tap_h : 2 - tap_h + rows].reshape(slabs * frames * per, 3 * chans)
            at = 3 * (3 * tap_t + tap_h)
            weights = jnp.concatenate([kernel[at], kernel[at + 1], kernel[at + 2]], axis=1)
            total = total + lax.dot_general(rows_in, weights, (((1,), (1,)), ((), ())), preferred_element_type=F32)
        planes.append(total)
    for slab in range(slabs):
        for frame in range(frames + 2):
            total = None
            for tap_t in range(3):
                source = frame - tap_t
                if 0 <= source < frames:
                    at = (slab * frames + source) * per
                    term = planes[tap_t][at : at + per]
                    total = term if total is None else total + term
            grads[slab, frame] = total.astype(BF).reshape(rows, width, chans)


def vmem(count):
    return [pl.BlockSpec(memory_space=pltpu.VMEM)] * count


def smem(count):
    return [pl.BlockSpec(memory_space=pltpu.SMEM)] * count


def forward_call(lengths, core, clips, low, high, kernel, cot_stay, cot_guest):
    slabs, frames, rows, width, chans = clips.shape
    out_frames = frames - 2
    one = (out_frames, rows, width, chans)
    edge = (slabs, out_frames, 1, width, chans)
    half = (TAPS, chans // 2, chans)
    return pl.pallas_call(
        forward_kernel,
        out_shape=(
            jax.ShapeDtypeStruct(one, BF),
            jax.ShapeDtypeStruct(one, BF),
            jax.ShapeDtypeStruct((slabs,) + one, BF),
            jax.ShapeDtypeStruct(edge, BF),
            jax.ShapeDtypeStruct(edge, BF),
            jax.ShapeDtypeStruct(half, F32),
            jax.ShapeDtypeStruct(half, BF),
        ),
        in_specs=smem(2) + vmem(6),
        out_specs=tuple(vmem(7)),
        scratch_shapes=[
            pltpu.VMEM((slabs, frames, rows + 2, width, 3 * chans), BF),
            pltpu.VMEM((TAPS, chans, chans), F32),
        ],
        compiler_params=pltpu.CompilerParams(vmem_limit_bytes=32 * 2**20),
        name="forward",
    )(lengths, core, clips, low, high, kernel, cot_stay, cot_guest)


def backward_call(dz, low, high, kernel):
    slabs, frames, rows, width, chans = dz.shape
    return pl.pallas_call(
        backward_kernel,
        out_shape=jax.ShapeDtypeStruct((slabs, frames + 2, rows, width, chans), BF),
        in_specs=vmem(4),
        out_specs=vmem(1)[0],
        scratch_shapes=[pltpu.VMEM((slabs, frames, rows + 2, width, 3 * chans), BF)],
        compiler_params=pltpu.CompilerParams(vmem_limit_bytes=32 * 2**20),
        name="backward",
    )(dz, low, high, kernel)


def by_xor(value, axes, count, offset):
    def branch(mask):
        pairs = [(source, source ^ mask) for source in range(count)]
        return lambda item: lax.ppermute(item, axes, pairs)

    return lax.switch(offset, [branch(mask) for mask in range(count)], value)


def route(value, offset, ny, nz):
    low = 2 * nz
    value = by_xor(value, ("z", "c"), low, jnp.bitwise_and(offset, low - 1))
    return by_xor(value, "y", ny, offset // low)


def swap_cores(value):
    return lax.ppermute(value, "c", [(0, 1), (1, 0)])


def spread(value, count):
    return jnp.broadcast_to(value[None], (count,) + value.shape)


def added(parts):
    return jnp.sum(parts.astype(F32), axis=0).astype(BF)


def summed(mine, other, scale, ny, nz, nx):
    core = lax.axis_index("c")
    half = mine + swap_cores(other).astype(F32)
    half = jnp.pad(half, ((0, PADDED_TAPS - TAPS), (0, 0), (0, 0))).astype(BF)
    held = half.shape
    parts = half.reshape((nz * nx, -1, held[2]))
    one = added(lax.all_to_all(parts, ("z", "x"), 0, 0))
    one = added(lax.all_to_all(spread(one, ny), "y", 0, 0))
    whole = lax.all_to_all(spread(one, nz * nx), ("z", "x"), 0, 0).reshape(held)
    theirs = swap_cores(whole)
    first = jnp.where(core == 0, whole, theirs)[:TAPS]
    second = jnp.where(core == 0, theirs, whole)[:TAPS]
    return jnp.concatenate([first, second], axis=1).astype(F32) * scale


def shards(ny, nz, nx, scale, clips, lengths, partner, kernel, cot_stay, cot_guest):
    rows = clips.shape[2]
    chans = clips.shape[4]
    offset = partner[0]
    up = [(i, i + 1) for i in range(nx - 1)]
    down = [(i + 1, i) for i in range(nx - 1)]

    def edges(first, last):
        return lax.ppermute(last, "x", up), lax.ppermute(first, "x", down)

    low, high = edges(clips[:, :, :1], clips[:, :, rows - 1 :])
    cot_here = route(cot_guest[0], offset, ny, nz)
    core = lax.axis_index("c").astype(jnp.int32).reshape(1)
    y_stay, y_guest, dz, dz_first, dz_last, mine, other = forward_call(
        lengths, core, clips, low, high, kernel.reshape(9, 3 * chans, chans), cot_stay[0], cot_here
    )
    dz_low, dz_high = edges(dz_first, dz_last)
    slab_grad = backward_call(dz, dz_low, dz_high, kernel.reshape(TAPS, chans, chans))
    guest_out = route(y_guest, offset, ny, nz)
    weight_grad = summed(mine, other, scale, ny, nz, nx).reshape(kernel.shape)
    return y_stay[None], guest_out[None], slab_grad, weight_grad


def solution(mesh):
    nx = mesh.shape["space"]
    ny = nz = math.isqrt(mesh.shape["dp"] // 2)
    fine = Mesh(mesh.devices.reshape(ny, nz, 2, nx), ("y", "z", "c", "x"))
    block = P(("y", "z", "c"), None, "x", None, None)

    def whole(clips, lengths, partner, kernel, cot_stay, cot_guest):
        slabs, _, height, width, _ = clips.shape
        scale = 1.0 / math.sqrt(slabs * cot_stay.shape[1] * height * width)
        return jax.shard_map(
            functools.partial(shards, ny, nz, nx, scale),
            mesh=fine,
            in_specs=(block, P(("y", "z", "c")), P(), P(), block, block),
            out_specs=(block, block, block, P()),
            check_vma=False,
        )(clips, lengths, partner, kernel, cot_stay, cot_guest)

    return whole
```

time: 429 us -> 128 us (0.30)
  the two profiles are of different devices: /device:TPU:1 before, /device:TPU:2 now
where the time goes in v1:
time: 128 us; the launch traced here: 127 us
  blocking collectives  63.1 us (49%)
  starting transfers between devices  31.7 us (25%)
  waiting for transfers between devices  18.1 us (14%)
  local copies, waits for them, and re-layouts  6.16 us (5%)
  Pallas kernels  5.08 us (4%)
  other arithmetic  1.7 us (1%)
  between operations  1.43 us (1%)
    all_to_all x1, blocking collectives, summed(): one = added(lax.all_to_all(parts, ('z', 'x'), 0, 0))  27.3 us
    all_to_all x1, blocking collectives, summed(): whole = lax.all_to_all(spread(one, nz * nx), ('z', 'x'), 0, 0).reshape(held)  19.9 us
    ppermute x4, waiting for transfers between devices, branch(): return lambda item: lax.ppermute(item, axes, pairs)  16.4 us
    all_to_all x1, blocking collectives, summed(): one = added(lax.all_to_all(spread(one, ny), 'y', 0, 0))  16 us
    ppermute x4, starting transfers between devices, edges(): return (lax.ppermute(last, 'x', up), lax.ppermute(first, 'x', down))  14.9 us
    ppermute x4, starting transfers between devices, branch(): return lambda item: lax.ppermute(item, axes, pairs)  12.9 us
    unnamed x11, local copies, waits for them, and re-layouts  5.09 us
    ppermute x2, starting transfers between devices, swap_cores(): return lax.ppermute(value, 'c', [(0, 1), (1, 0)])  3.83 us
  transfers between devices with their start and end apart: 10, of which 5 were waited for; matrix products, arithmetic and copies ran while one was open for 0% of the time, Pallas kernels for 1%

profile of v1, /device:TPU:2, one launch (start us, length us, event | category | flops | bytes accessed | tf_op | source)
XLA Modules:
  0.0 127.4 jit_solution(10839098673214008383)
XLA Ops:
  1.5 3.4 %collective-permute-start.48 = (bf16[2,4,1,32,128]{4,3,2,1,0:T(8,128)(2,1)S(1)}, bf16[2,4,1,32,128]{4,3,2,1,0:T(8,128)(2,1)S(1)}, u32[]{:S(2)}, u32[]{:S(2)}) collective-permute-start(bf16[2,4,1,32,128]{4,3,2,1,0:T(8,128)(2,1)S(1)} %get-tuple-element.122), channel_id=1, source_target_pairs={{0,1},{1,2},{2,3},{4,5},{5,6},{6,7},{8,9},{9,10},{10,11},{12,13},{... | collective-permute-start | bytes 196616 | tf_op jit(solution)/shard_map/ppermute | solution.py:199
  4.9 5.7 %collective-permute-start.49 = (bf16[2,4,1,32,128]{4,3,2,1,0:T(8,128)(2,1)S(1)}, bf16[2,4,1,32,128]{4,3,2,1,0:T(8,128)(2,1)S(1)}, u32[]{:S(2)}, u32[]{:S(2)}) collective-permute-start(bf16[2,4,1,32,128]{4,3,2,1,0:T(8,128)(2,1)S(1)} %get-tuple-element.121), channel_id=1, source_target_pairs={{1,0},{2,1},{3,2},{5,4},{6,5},{7,6},{9,8},{10,9},{11,10},{13,12},{... | collective-permute-start | bytes 196616 | tf_op jit(solution)/shard_map/ppermute | solution.py:199
  11.3 8.3 %conditional.4 = (bf16[2,4,32,128]{3,2,1,0:T(8,128)(2,1)}) conditional(s32[]{:T(128)} %clamp.9, bf16[2,4,32,128]{3,2,1,0:T(8,128)(2,1)} %bitcast.27, bf16[2,4,32,128]{3,2,1,0:T(8,128)(2,1)} %bitcast.28, bf16[2,4,32,128]{3,2,1,0:T(8,128)(2,1)} %bitcast.29, bf16[2,4,32,128]{3,2,1,0:T(8,128)(2,1)} %bitcast.30, ...), branch_computations={%region_0.0_spmd, %region_1.0_spmd, %region_2.0_spmd, %region_3.0_... | conditional | bytes 262192 | solution.py:155
  11.4 4.6 %collective-permute-start.6 = (bf16[2,4,32,128]{3,2,1,0:T(8,128)(2,1)}, bf16[2,4,32,128]{3,2,1,0:T(8,128)(2,1)}, u32[]{:S(2)}, u32[]{:S(2)}) collective-permute-start(bf16[2,4,32,128]{3,2,1,0:T(8,128)(2,1)} %param.6), channel_id=1, source_target_pairs={{0,24},{4,28},{8,16},{12,20},{16,8},{20,12},{24,0},{28,4},{32,56},... | collective-permute-start | bytes 196616 | tf_op jit(solution)/shard_map/cond/branch_6_fun/ppermute | solution.py:153
  16.0 3.6 %collective-permute-done.6 = bf16[2,4,32,128]{3,2,1,0:T(8,128)(2,1)} collective-permute-done((bf16[2,4,32,128]{3,2,1,0:T(8,128)(2,1)}, bf16[2,4,32,128]{3,2,1,0:T(8,128)(2,1)}, u32[]{:S(2)}, u32[]{:S(2)}) %collective-permute-start.6) | collective-permute-done | bytes 65568 | tf_op jit(solution)/shard_map/cond/branch_6_fun/ppermute | solution.py:153
  19.6 6.5 %conditional.5 = (bf16[2,4,32,128]{3,2,1,0:T(8,128)(2,1)}) conditional(s32[]{:T(128)} %clamp.8, bf16[2,4,32,128]{3,2,1,0:T(8,128)(2,1)} %get-tuple-element.131, bf16[2,4,32,128]{3,2,1,0:T(8,128)(2,1)} %get-tuple-element.131, bf16[2,4,32,128]{3,2,1,0:T(8,128)(2,1)} %get-tuple-element.131, ...), branch_computations={%region_16.17_spmd, %region_17.18_spmd, %region_18.19_spmd, %regio... | conditional | bytes 262192 | solution.py:155
  19.6 2.4 %collective-permute-start.17 = (bf16[2,4,32,128]{3,2,1,0:T(8,128)(2,1)}, bf16[2,4,32,128]{3,2,1,0:T(8,128)(2,1)}, u32[]{:S(2)}, u32[]{:S(2)}) collective-permute-start(bf16[2,4,32,128]{3,2,1,0:T(8,128)(2,1)} %param.17), channel_id=1, source_target_pairs={{0,64},{64,0},{128,192},{192,128},{256,320},{320,256},{384,448},{4... | collective-permute-start | bytes 196616 | tf_op jit(solution)/shard_map/cond/branch_1_fun/ppermute | solution.py:153
  22.0 4.1 %collective-permute-done.17 = bf16[2,4,32,128]{3,2,1,0:T(8,128)(2,1)} collective-permute-done((bf16[2,4,32,128]{3,2,1,0:T(8,128)(2,1)}, bf16[2,4,32,128]{3,2,1,0:T(8,128)(2,1)}, u32[]{:S(2)}, u32[]{:S(2)}) %collective-permute-start.17) | collective-permute-done | bytes 65568 | tf_op jit(solution)/shard_map/cond/branch_1_fun/ppermute | solution.py:153
  29.7 3.3 %forward.1 = (bf16[2,4,32,128]{3,2,1,0:T(8,128)(2,1)}, bf16[2,4,32,128]{3,2,1,0:T(8,128)(2,1)S(1)}, bf16[2,2,4,32,128]{4,3,2,1,0:T(8,128)(2,1)S(1)}, bf16[2,2,1,...) custom-call(s32[2]{0:T(128)S(1)} %copy-done.4, ...), custom_call_target="tpu_custom_call" | custom-call | tf_op jit(solution)/shard_map/forward/pallas_call | solution.py:115
  33.0 1.9 %collective-permute-start.52 = (bf16[27,64,128]{2,1,0:T(8,128)(2,1)S(1)}, bf16[27,64,128]{2,1,0:T(8,128)(2,1)S(1)}, u32[]{:S(2)}, u32[]{:S(2)}) collective-permute-start(bf16[27,64,128]{2,1,0:T(8,128)(2,1)S(1)} %get-tuple-element.118), channel_id=1, source_target_pairs={{0,4},{4,0},{1,5},{5,1},{2,6},{6,2},{3,7},{7,3},{8,12},{12,8},{9,1... | collective-permute-start | bytes 1327112 | tf_op jit(solution)/shard_map/ppermute | solution.py:165
  34.9 1.8 %collective-permute-done.52 = bf16[27,64,128]{2,1,0:T(8,128)(2,1)S(1)} collective-permute-done((bf16[27,64,128]{2,1,0:T(8,128)(2,1)S(1)}, bf16[27,64,128]{2,1,0:T(8,128)(2,1)S(1)}, u32[]{:S(2)}, u32[]{:S(2)}) %collective-permute-start.52) | collective-permute-done | bytes 442400 | tf_op jit(solution)/shard_map/ppermute | solution.py:165
  36.9 27.3 %all_to_all.15 = bf16[32,64,128]{2,1,0:T(8,128)(2,1)S(1)} all-to-all(bf16[32,64,128]{2,1,0:T(8,128)(2,1)S(1)} %pad.5), channel_id=1, replica_groups=mesh['y'=8,'z'=8,'c'=2,'x'=4] {'z','x'}, dimensions={0} | all-to-all | bytes 1048576 | tf_op jit(solution)/shard_map/all_to_all | solution.py:182
  64.3 16.0 %all_to_all.16 = bf16[8,64,128]{2,1,0:T(8,128)(2,1)S(1)} all-to-all(bf16[8,64,128]{2,1,0:T(8,128)(2,1)S(1)} %broadcast_in_dim.41), channel_id=1, replica_groups=mesh['y'=8,'z'=8,'c'=2,'x'=4] {'y'}, dimensions={0} | all-to-all | bytes 262144 | tf_op jit(solution)/shard_map/all_to_all | solution.py:183
  80.4 19.9 %all_to_all.17 = bf16[32,64,128]{2,1,0:T(8,128)(2,1)S(1)} all-to-all(bf16[32,64,128]{2,1,0:T(8,128)(2,1)S(1)} %broadcast_in_dim.42), channel_id=1, replica_groups=mesh['y'=8,'z'=8,'c'=2,'x'=4] {'z','x'}, dimensions={0} | all-to-all | bytes 1048576 | tf_op jit(solution)/shard_map/all_to_all | solution.py:184
  100.3 1.9 %collective-permute-start.53 = (bf16[32,64,128]{2,1,0:T(8,128)(2,1)S(1)}, bf16[32,64,128]{2,1,0:T(8,128)(2,1)S(1)}, u32[]{:S(2)}, u32[]{:S(2)}) collective-permute-start(bf16[32,64,128]{2,1,0:T(8,128)(2,1)S(1)} %all_to_all.17), channel_id=1, source_target_pairs={{0,4},{4,0},{1,5},{5,1},{2,6},{6,2},{3,7},{7,3},{8,12},{12,8},{9,1... | collective-permute-start | bytes 1572872 | tf_op jit(solution)/shard_map/ppermute | solution.py:165
  102.2 3.4 %collective-permute-start.50 = (bf16[2,2,1,32,128]{4,3,2,1,0:T(8,128)(2,1)S(1)}, bf16[2,2,1,32,128]{4,3,2,1,0:T(8,128)(2,1)S(1)}, u32[]{:S(2)}, u32[]{:S(2)}) collective-permute-start(bf16[2,2,1,32,128]{4,3,2,1,0:T(8,128)(2,1)S(1)} %get-tuple-element.115), channel_id=1, source_target_pairs={{0,1},{1,2},{2,3},{4,5},{5,6},{6,7},{8,9},{9,10},{10,11},{12,13},{... | collective-permute-start | bytes 98312 | tf_op jit(solution)/shard_map/ppermute | solution.py:199
  105.6 2.5 %collective-permute-start.51 = (bf16[2,2,1,32,128]{4,3,2,1,0:T(8,128)(2,1)S(1)}, bf16[2,2,1,32,128]{4,3,2,1,0:T(8,128)(2,1)S(1)}, u32[]{:S(2)}, u32[]{:S(2)}) collective-permute-start(bf16[2,2,1,32,128]{4,3,2,1,0:T(8,128)(2,1)S(1)} %get-tuple-element.116), channel_id=1, source_target_pairs={{1,0},{2,1},{3,2},{5,4},{6,5},{7,6},{9,8},{10,9},{11,10},{13,12},{... | collective-permute-start | bytes 98312 | tf_op jit(solution)/shard_map/ppermute | solution.py:199
  108.1 8.1 %conditional.6 = (bf16[2,4,32,128]{3,2,1,0:T(8,128)(2,1)}) conditional(s32[]{:T(128)} %clamp.9, bf16[2,4,32,128]{3,2,1,0:T(8,128)(2,1)S(1)} %get-tuple-element.113, bf16[2,4,32,128]{3,2,1,0:T(8,128)(2,1)S(1)} %get-tuple-element.113, bf16[2,4,32,128]{3,2,1,0:T(8,128)(2,1)S(1)} %get-tuple-element.113, ...), branch_computations={%region_24.25_spmd, %region_25.26_spmd, %region_26.27_spmd, %regio... | conditional | bytes 262192 | solution.py:155
  108.1 3.3 %collective-permute-start.30 = (bf16[2,4,32,128]{3,2,1,0:T(8,128)(2,1)S(1)}, bf16[2,4,32,128]{3,2,1,0:T(8,128)(2,1)}, u32[]{:S(2)}, u32[]{:S(2)}) collective-permute-start(bf16[2,4,32,128]{3,2,1,0:T(8,128)(2,1)S(1)} %param.30), channel_id=1, source_target_pairs={{0,24},{4,28},{8,16},{12,20},{16,8},{20,12},{24,0},{28,4},{32,56},... | collective-permute-start | bytes 196616 | tf_op jit(solution)/shard_map/cond/branch_6_fun/ppermute | solution.py:153
  111.4 4.8 %collective-permute-done.30 = bf16[2,4,32,128]{3,2,1,0:T(8,128)(2,1)} collective-permute-done((bf16[2,4,32,128]{3,2,1,0:T(8,128)(2,1)S(1)}, bf16[2,4,32,128]{3,2,1,0:T(8,128)(2,1)}, u32[]{:S(2)}, u32[]{:S(2)}) %collective-permute-start.30) | collective-permute-done | bytes 65568 | tf_op jit(solution)/shard_map/cond/branch_6_fun/ppermute | solution.py:153
  116.2 6.5 %conditional.7 = (bf16[1,2,4,32,128]{4,3,2,1,0:T(8,128)(2,1)}) conditional(s32[]{:T(128)} %clamp.8, bf16[2,4,32,128]{3,2,1,0:T(8,128)(2,1)} %get-tuple-element.133, bf16[2,4,32,128]{3,2,1,0:T(8,128)(2,1)} %get-tuple-element.133, bf16[2,4,32,128]{3,2,1,0:T(8,128)(2,1)} %get-tuple-element.133, ...), branch_computations={%region_40.41_spmd, %region_41.42_spmd, %region_42.43_spmd, %regio... | conditional | bytes 262192 | solution.py:155
  116.2 2.6 %collective-permute-start.41 = (bf16[2,4,32,128]{3,2,1,0:T(8,128)(2,1)}, bf16[2,4,32,128]{3,2,1,0:T(8,128)(2,1)}, u32[]{:S(2)}, u32[]{:S(2)}) collective-permute-start(bf16[2,4,32,128]{3,2,1,0:T(8,128)(2,1)} %param.41), channel_id=1, source_target_pairs={{0,64},{64,0},{128,192},{192,128},{256,320},{320,256},{384,448},{4... | collective-permute-start | bytes 196616 | tf_op jit(solution)/shard_map/cond/branch_1_fun/ppermute | solution.py:153
  118.7 3.9 %collective-permute-done.41 = bf16[2,4,32,128]{3,2,1,0:T(8,128)(2,1)} collective-permute-done((bf16[2,4,32,128]{3,2,1,0:T(8,128)(2,1)}, bf16[2,4,32,128]{3,2,1,0:T(8,128)(2,1)}, u32[]{:S(2)}, u32[]{:S(2)}) %collective-permute-start.41) | collective-permute-done | bytes 65568 | tf_op jit(solution)/shard_map/cond/branch_1_fun/ppermute | solution.py:153
  122.6 1.8 %backward.1 = bf16[2,4,4,32,128]{4,3,2,1,0:T(8,128)(2,1)} custom-call(bf16[2,2,4,32,128]{4,3,2,1,0:T(8,128)(2,1)S(1)} %get-tuple-element.114.dz, bf16[2,2,1,32,128]{4,3,2,1,0:T(8,128)(2,1)S(1)} %collective-permute-done.50.low, bf16[2,2,1,32,128]{4,3,2,1,0:T(8,128)(2,1)S(1)} %collective-permute-done.51.high, bf16[27,128,128]{2,1,0:T(8,128)(2,1)S(1)} %bitcast.23), custom_call_target="tpu_custom_call" | custom-call | tf_op jit(solution)/shard_map/backward/pallas_call | solution.py:139
  (25 shorter events, 7.9 us)
Async XLA Ops:
  1.5 24.6 %collective-permute-start.48 = (bf16[2,4,1,32,128]{4,3,2,1,0:T(8,128)(2,1)S(1)}, bf16[2,4,1,32,128]{4,3,2,1,0:T(8,128)(2,1)S(1)}, u32[]{:S(2)}, u32[]{:S(2)}) collective-permute-start(bf16[2,4,1,32,128]{4,3,2,1,0:T(8,128)(2,1)S(1)} %get-tuple-element.122), channel_id=1, source_target_pairs={{0,1},{1,2},{2,3},{4,5},{5,6},{6,7},{8,9},{9,10},{10,11},{12,13},{... | collective-permute-start | bytes 196616 | tf_op jit(solution)/shard_map/ppermute | solution.py:199
  4.9 21.2 %collective-permute-start.49 = (bf16[2,4,1,32,128]{4,3,2,1,0:T(8,128)(2,1)S(1)}, bf16[2,4,1,32,128]{4,3,2,1,0:T(8,128)(2,1)S(1)}, u32[]{:S(2)}, u32[]{:S(2)}) collective-permute-start(bf16[2,4,1,32,128]{4,3,2,1,0:T(8,128)(2,1)S(1)} %get-tuple-element.121), channel_id=1, source_target_pairs={{1,0},{2,1},{3,2},{5,4},{6,5},{7,6},{9,8},{10,9},{11,10},{13,12},{... | collective-permute-start | bytes 196616 | tf_op jit(solution)/shard_map/ppermute | solution.py:199
  11.4 8.3 %collective-permute-start.6 = (bf16[2,4,32,128]{3,2,1,0:T(8,128)(2,1)}, bf16[2,4,32,128]{3,2,1,0:T(8,128)(2,1)}, u32[]{:S(2)}, u32[]{:S(2)}) collective-permute-start(bf16[2,4,32,128]{3,2,1,0:T(8,128)(2,1)} %param.6), channel_id=1, source_target_pairs={{0,24},{4,28},{8,16},{12,20},{16,8},{20,12},{24,0},{28,4},{32,56},... | collective-permute-start | bytes 196616 | tf_op jit(solution)/shard_map/cond/branch_6_fun/ppermute | solution.py:153
  19.6 6.5 %collective-permute-start.17 = (bf16[2,4,32,128]{3,2,1,0:T(8,128)(2,1)}, bf16[2,4,32,128]{3,2,1,0:T(8,128)(2,1)}, u32[]{:S(2)}, u32[]{:S(2)}) collective-permute-start(bf16[2,4,32,128]{3,2,1,0:T(8,128)(2,1)} %param.17), channel_id=1, source_target_pairs={{0,64},{64,0},{128,192},{192,128},{256,320},{320,256},{384,448},{4... | collective-permute-start | bytes 196616 | tf_op jit(solution)/shard_map/cond/branch_1_fun/ppermute | solution.py:153
  26.1 1.2 copy-start
  27.3 0.9 copy-start.2
  28.2 0.8 copy-start.3
  29.1 0.7 copy-start.4
  33.0 3.7 %collective-permute-start.52 = (bf16[27,64,128]{2,1,0:T(8,128)(2,1)S(1)}, bf16[27,64,128]{2,1,0:T(8,128)(2,1)S(1)}, u32[]{:S(2)}, u32[]{:S(2)}) collective-permute-start(bf16[27,64,128]{2,1,0:T(8,128)(2,1)S(1)} %get-tuple-element.118), channel_id=1, source_target_pairs={{0,4},{4,0},{1,5},{5,1},{2,6},{6,2},{3,7},{7,3},{8,12},{12,8},{9,1... | collective-permute-start | bytes 1327112 | tf_op jit(solution)/shard_map/ppermute | solution.py:165
  36.9 85.7 %copy-start.1 = (bf16[3,3,3,128,128]{4,3,2,1,0:T(8,128)(2,1)S(1)}, bf16[3,3,3,128,128]{4,3,2,1,0:T(8,128)(2,1)}, u32[]{:S(2)}) copy-start(bf16[3,3,3,128,128]{4,3,2,1,0:T(8,128)(2,1)} %param.57) | copy-start | bytes 2654212
  100.3 24.2 %collective-permute-start.53 = (bf16[32,64,128]{2,1,0:T(8,128)(2,1)S(1)}, bf16[32,64,128]{2,1,0:T(8,128)(2,1)S(1)}, u32[]{:S(2)}, u32[]{:S(2)}) collective-permute-start(bf16[32,64,128]{2,1,0:T(8,128)(2,1)S(1)} %all_to_all.17), channel_id=1, source_target_pairs={{0,4},{4,0},{1,5},{5,1},{2,6},{6,2},{3,7},{7,3},{8,12},{12,8},{9,1... | collective-permute-start | bytes 1572872 | tf_op jit(solution)/shard_map/ppermute | solution.py:165
  102.2 20.4 %collective-permute-start.50 = (bf16[2,2,1,32,128]{4,3,2,1,0:T(8,128)(2,1)S(1)}, bf16[2,2,1,32,128]{4,3,2,1,0:T(8,128)(2,1)S(1)}, u32[]{:S(2)}, u32[]{:S(2)}) collective-permute-start(bf16[2,2,1,32,128]{4,3,2,1,0:T(8,128)(2,1)S(1)} %get-tuple-element.115), channel_id=1, source_target_pairs={{0,1},{1,2},{2,3},{4,5},{5,6},{6,7},{8,9},{9,10},{10,11},{12,13},{... | collective-permute-start | bytes 98312 | tf_op jit(solution)/shard_map/ppermute | solution.py:199
  105.6 17.1 %collective-permute-start.51 = (bf16[2,2,1,32,128]{4,3,2,1,0:T(8,128)(2,1)S(1)}, bf16[2,2,1,32,128]{4,3,2,1,0:T(8,128)(2,1)S(1)}, u32[]{:S(2)}, u32[]{:S(2)}) collective-permute-start(bf16[2,2,1,32,128]{4,3,2,1,0:T(8,128)(2,1)S(1)} %get-tuple-element.116), channel_id=1, source_target_pairs={{1,0},{2,1},{3,2},{5,4},{6,5},{7,6},{9,8},{10,9},{11,10},{13,12},{... | collective-permute-start | bytes 98312 | tf_op jit(solution)/shard_map/ppermute | solution.py:199
  108.1 8.1 %collective-permute-start.30 = (bf16[2,4,32,128]{3,2,1,0:T(8,128)(2,1)S(1)}, bf16[2,4,32,128]{3,2,1,0:T(8,128)(2,1)}, u32[]{:S(2)}, u32[]{:S(2)}) collective-permute-start(bf16[2,4,32,128]{3,2,1,0:T(8,128)(2,1)S(1)} %param.30), channel_id=1, source_target_pairs={{0,24},{4,28},{8,16},{12,20},{16,8},{20,12},{24,0},{28,4},{32,56},... | collective-permute-start | bytes 196616 | tf_op jit(solution)/shard_map/cond/branch_6_fun/ppermute | solution.py:153
  116.2 6.5 %collective-permute-start.41 = (bf16[2,4,32,128]{3,2,1,0:T(8,128)(2,1)}, bf16[2,4,32,128]{3,2,1,0:T(8,128)(2,1)}, u32[]{:S(2)}, u32[]{:S(2)}) collective-permute-start(bf16[2,4,32,128]{3,2,1,0:T(8,128)(2,1)} %param.41), channel_id=1, source_target_pairs={{0,64},{64,0},{128,192},{192,128},{256,320},{320,256},{384,448},{4... | collective-permute-start | bytes 196616 | tf_op jit(solution)/shard_map/cond/branch_1_fun/ppermute | solution.py:153

commit v2 on v1

v2 whole, which is shorter than its diff:
```python
import functools
import math

import jax
import jax.numpy as jnp
from jax import lax
from jax.experimental import pallas as pl
from jax.experimental.pallas import tpu as pltpu
from jax.sharding import Mesh
from jax.sharding import PartitionSpec as P

BF = jnp.bfloat16
F32 = jnp.float32
TAPS = 27
PADDED_TAPS = 32


def widen(wide, block, first, mirrored):
    slabs, frames, rows, width, chans = block.shape
    flat = block.reshape(-1, chans).astype(F32)
    column = lax.broadcasted_iota(jnp.int32, flat.shape, 0) % width
    before = jnp.where(column == 0, 0.0, pltpu.roll(flat, 1, 0)).astype(BF).reshape(block.shape)
    after = jnp.where(column == width - 1, 0.0, pltpu.roll(flat, flat.shape[0] - 1, 0)).astype(BF).reshape(block.shape)
    for part, columns in enumerate((after, block, before) if mirrored else (before, block, after)):
        wide[:, :, first : first + rows, :, part * chans : (part + 1) * chans] = columns


def forward_kernel(lengths, low, high, clips, kernel_in, y_stay, y_guest, slope_out, held, kernel, wide, sems):
    slabs, frames, rows, width, chans = clips.shape
    out_frames = frames - 2
    loads = [
        pltpu.make_async_copy(low, held.at[:, :, 0:1], sems.at[0]),
        pltpu.make_async_copy(clips, held.at[:, :, 1 : rows + 1], sems.at[1]),
        pltpu.make_async_copy(high, held.at[:, :, rows + 1 : rows + 2], sems.at[2]),
    ]
    weights = [
        pltpu.make_async_copy(kernel_in.at[3 * k : 3 * k + 3], kernel.at[3 * k : 3 * k + 3], sems.at[3 + k])
        for k in range(3)
    ]
    for load in loads + weights:
        load.start()
    for load in loads:
        load.wait()
    widen(wide, held[...], 0, False)
    places = slabs * out_frames * rows * width
    z = jnp.zeros((places, chans), F32)
    for tap in range(9):
        if tap % 3 == 0:
            weights[tap // 3].wait()
        z = z + jnp.dot(window(wide, tap, rows), kernel[tap], preferred_element_type=F32)
    sig = 1.0 / (1.0 + jnp.exp(-z))
    per = rows * width
    y = z * sig
    slope = sig * (1.0 + z * (1.0 - sig))
    for slab, out in enumerate((y_stay, y_guest)):
        for frame in range(out_frames):
            valid = jnp.where(lengths[slab] > frame, 1.0, 0.0)
            at = (slab * out_frames + frame) * per
            out[frame] = (valid * y[at : at + per]).astype(BF).reshape(rows, width, chans)
            slope_out[at : at + per] = valid * slope[at : at + per]


def window(wide, tap, rows):
    frames = wide.shape[1] - 2
    block = wide[:, tap // 3 : tap // 3 + frames, tap % 3 : tap % 3 + rows]
    return block.reshape(-1, wide.shape[4])


def weight_kernel(core, low, high, slope_in, cot_guest_in, clips, cot_stay,
                  dz_out, dz_first, dz_last, mine, other, edge, slope, cot_guest, wide, sums, sems):
    slabs, frames, rows, width, chans = clips.shape
    out_frames = frames - 2
    per = rows * width
    loads = [
        pltpu.make_async_copy(low, edge.at[0], sems.at[0]),
        pltpu.make_async_copy(high, edge.at[1], sems.at[1]),
        pltpu.make_async_copy(slope_in, slope, sems.at[2]),
        pltpu.make_async_copy(cot_guest_in, cot_guest, sems.at[3]),
    ]
    for load in loads:
        load.start()
    widen(wide, clips[...], 1, False)
    for load in loads:
        load.wait()
    for place in range(2):
        widen(wide, edge[place], place * (rows + 1), False)
    parts = []
    for slab, cot in enumerate((cot_stay, cot_guest)):
        for frame in range(out_frames):
            at = (slab * out_frames + frame) * per
            grad = cot[frame].reshape(per, chans).astype(F32)
            dz = (grad * slope[at : at + per]).astype(BF)
            parts.append(dz)
            dz = dz.reshape(rows, width, chans)
            dz_out[slab, frame] = dz
            dz_first[slab, frame] = dz[0:1]
            dz_last[slab, frame] = dz[rows - 1 : rows]
    dz_all = jnp.concatenate(parts, axis=0)
    for tap in range(9):
        term = lax.dot_general(
            window(wide, tap, rows), dz_all, (((0,), (0,)), ((), ())), preferred_element_type=F32
        )
        sums[3 * tap : 3 * tap + 3] = term.reshape(3, chans, chans)
    half = chans // 2
    own = core[0]
    mine[...] = sums[:, pl.ds(pl.multiple_of(own * half, half), half), :]
    other[...] = sums[:, pl.ds(pl.multiple_of((1 - own) * half, half), half), :].astype(BF)


def backward_kernel(dz, low, high, kernel, grads, wide):
    slabs, frames, rows, width, chans = dz.shape
    widen(wide, low[...], 0, True)
    widen(wide, dz[...], 1, True)
    widen(wide, high[...], rows + 1, True)
    per = rows * width
    planes = []
    for tap_t in range(3):
        total = jnp.zeros((slabs * frames * per, chans), F32)
        for tap_h in range(3):
            rows_in = wide[:, :, 2 - tap_h : 2 - tap_h + rows].reshape(slabs * frames * per, 3 * chans)
            at = 3 * (3 * tap_t + tap_h)
            weights = jnp.concatenate([kernel[at], kernel[at + 1], kernel[at + 2]], axis=1)
            total = total + lax.dot_general(rows_in, weights, (((1,), (1,)), ((), ())), preferred_element_type=F32)
        planes.append(total)
    for slab in range(slabs):
        for frame in range(frames + 2):
            total = None
            for tap_t in range(3):
                source = frame - tap_t
                if 0 <= source < frames:
                    at = (slab * frames + source) * per
                    term = planes[tap_t][at : at + per]
                    total = term if total is None else total + term
            grads[slab, frame] = total.astype(BF).reshape(rows, width, chans)


def vmem(count):
    return [pl.BlockSpec(memory_space=pltpu.VMEM)] * count


def smem(count):
    return [pl.BlockSpec(memory_space=pltpu.SMEM)] * count


def anywhere(count):
    return [pl.BlockSpec(memory_space=pl.ANY)] * count


def forward_call(lengths, low, high, clips, kernel):
    slabs, frames, rows, width, chans = clips.shape
    one = (frames - 2, rows, width, chans)
    return pl.pallas_call(
        forward_kernel,
        out_shape=(
            jax.ShapeDtypeStruct(one, BF),
            jax.ShapeDtypeStruct(one, BF),
            jax.ShapeDtypeStruct((slabs * (frames - 2) * rows * width, chans), F32),
        ),
        in_specs=smem(1) + anywhere(4),
        out_specs=tuple(vmem(3)),
        scratch_shapes=[
            pltpu.VMEM((slabs, frames, rows + 2, width, chans), BF),
            pltpu.VMEM(kernel.shape, BF),
            pltpu.VMEM((slabs, frames, rows + 2, width, 3 * chans), BF),
            pltpu.SemaphoreType.DMA((6,)),
        ],
        compiler_params=pltpu.CompilerParams(vmem_limit_bytes=32 * 2**20),
        name="forward",
    )(lengths, low, high, clips, kernel)


def weight_call(core, low, high, slope, cot_guest, clips, cot_stay):
    slabs, frames, rows, width, chans = clips.shape
    one = cot_stay.shape
    edge = (slabs, frames - 2, 1, width, chans)
    half = (TAPS, chans // 2, chans)
    return pl.pallas_call(
        weight_kernel,
        out_shape=(
            jax.ShapeDtypeStruct((slabs,) + one, BF),
            jax.ShapeDtypeStruct(edge, BF),
            jax.ShapeDtypeStruct(edge, BF),
            jax.ShapeDtypeStruct(half, F32),
            jax.ShapeDtypeStruct(half, BF),
        ),
        in_specs=smem(1) + anywhere(4) + vmem(2),
        out_specs=tuple(vmem(5)),
        scratch_shapes=[
            pltpu.VMEM((2,) + low.shape, BF),
            pltpu.VMEM(slope.shape, F32),
            pltpu.VMEM(one, BF),
            pltpu.VMEM((slabs, frames, rows + 2, width, 3 * chans), BF),
            pltpu.VMEM((TAPS, chans, chans), F32),
            pltpu.SemaphoreType.DMA((4,)),
        ],
        compiler_params=pltpu.CompilerParams(vmem_limit_bytes=32 * 2**20),
        name="weights",
    )(core, low, high, slope, cot_guest, clips, cot_stay)


def backward_call(dz, low, high, kernel):
    slabs, frames, rows, width, chans = dz.shape
    return pl.pallas_call(
        backward_kernel,
        out_shape=jax.ShapeDtypeStruct((slabs, frames + 2, rows, width, chans), BF),
        in_specs=vmem(4),
        out_specs=vmem(1)[0],
        scratch_shapes=[pltpu.VMEM((slabs, frames, rows + 2, width, 3 * chans), BF)],
        compiler_params=pltpu.CompilerParams(vmem_limit_bytes=32 * 2**20),
        name="backward",
    )(dz, low, high, kernel)


def half_kernel(scale, groups, first, rows, passed, out, passed_out, buffer, held, sems):
    taps, half, _ = buffer.shape
    step = taps // groups
    place = pl.ds(pl.multiple_of(first[0] * half, half), half)
    load = pltpu.make_async_copy(passed, held, sems.at[groups])
    load.start()
    copies = [pltpu.make_async_copy(held, passed_out.at[0], sems.at[groups + 1])]
    for group in range(groups):
        at = slice(group * step, group * step + step)
        buffer[at] = rows[at].astype(F32) * scale
        copies.append(pltpu.make_async_copy(buffer.at[at], out.at[at, place, :], sems.at[group]))
        copies[-1].start()
    load.wait()
    copies[0].start()
    for copy in copies:
        copy.wait()


def half_call(first, rows, scale, passed):
    _, half, chans = rows.shape
    return pl.pallas_call(
        functools.partial(half_kernel, scale, 3),
        out_shape=(
            jax.ShapeDtypeStruct((TAPS, 2 * half, chans), F32),
            jax.ShapeDtypeStruct((1,) + passed.shape, passed.dtype),
        ),
        in_specs=smem(1) + vmem(1) + anywhere(1),
        out_specs=tuple(anywhere(2)),
        scratch_shapes=[
            pltpu.VMEM((TAPS, half, chans), F32),
            pltpu.VMEM(passed.shape, passed.dtype),
            pltpu.SemaphoreType.DMA((5,)),
        ],
        compiler_params=pltpu.CompilerParams(vmem_limit_bytes=32 * 2**20),
        name="own",
    )(first, rows, passed)


def rest_kernel(scale, groups, first, rows, _, out, buffer, sems):
    taps, half, _ = buffer.shape
    step = taps // groups
    place = pl.ds(pl.multiple_of(first[0] * half, half), half)
    copies = []
    for group in range(groups):
        at = slice(group * step, group * step + step)
        buffer[at] = rows[at].astype(F32) * scale
        copies.append(pltpu.make_async_copy(buffer.at[at], out.at[at, place, :], sems.at[group]))
        copies[-1].start()
    for copy in copies:
        copy.wait()


def rest_call(first, rows, scale, earlier):
    _, half, chans = rows.shape
    return pl.pallas_call(
        functools.partial(rest_kernel, scale, 3),
        out_shape=jax.ShapeDtypeStruct(earlier.shape, F32),
        in_specs=smem(1) + vmem(1) + anywhere(1),
        out_specs=anywhere(1)[0],
        scratch_shapes=[pltpu.VMEM((TAPS, half, chans), F32), pltpu.SemaphoreType.DMA((3,))],
        input_output_aliases={2: 0},
        compiler_params=pltpu.CompilerParams(vmem_limit_bytes=32 * 2**20),
        name="rest",
    )(first, rows, earlier)


def by_xor(value, axes, count, offset, beside=None, extra=()):
    def branch(mask):
        pairs = [(source, source ^ mask) for source in range(count)]

        def moved(item, *others):
            there = lax.ppermute(item, axes, pairs)
            return there if beside is None else (there, beside(*others))

        return moved

    return lax.switch(offset, [branch(mask) for mask in range(count)], value, *extra)


def swap_cores(value):
    return lax.ppermute(value, "c", [(0, 1), (1, 0)])


def spread(value, count):
    return jnp.broadcast_to(value[None], (count,) + value.shape)


def added(parts):
    return jnp.sum(parts.astype(F32), axis=0).astype(BF)


def shards(ny, nz, nx, scale, clips, lengths, partner, kernel, cot_stay, cot_guest):
    rows = clips.shape[2]
    chans = clips.shape[4]
    near, far = jnp.bitwise_and(partner[0], 2 * nz - 1), partner[0] // (2 * nz)
    up = [(i, i + 1) for i in range(nx - 1)]
    down = [(i + 1, i) for i in range(nx - 1)]

    def edges(first, last):
        return lax.ppermute(last, "x", up), lax.ppermute(first, "x", down)

    def clip_edges(whole):
        return edges(whole[:, :, :1], whole[:, :, rows - 1 :])

    core = lax.axis_index("c").astype(jnp.int32).reshape(1)
    cot_here, (low, high) = by_xor(cot_guest[0], ("z", "c"), 2 * nz, near, clip_edges, (clips,))
    cot_here, (y_stay, y_guest, slope) = by_xor(
        cot_here, "y", ny, far, forward_call, (lengths, low, high, clips, kernel.reshape(9, 3 * chans, chans))
    )
    dz, dz_first, dz_last, mine, other = weight_call(core, low, high, slope, cot_here, clips, cot_stay[0])
    half = mine + swap_cores(other).astype(F32)
    half = jnp.pad(half, ((0, PADDED_TAPS - TAPS), (0, 0), (0, 0))).astype(BF)
    held = half.shape
    parts = lax.all_to_all(half.reshape((nz * nx, -1, held[2])), ("z", "x"), 0, 0)

    guest, (dz_low, dz_high) = by_xor(y_guest, "y", ny, far, edges, (dz_first, dz_last))
    one, guest, dz_low, dz_high = lax.optimization_barrier((added(parts), guest, dz_low, dz_high))
    parts = lax.all_to_all(spread(one, ny), "y", 0, 0)
    slab_grad = backward_call(dz, dz_low, dz_high, kernel.reshape(TAPS, chans, chans))
    one, slab_grad = lax.optimization_barrier((added(parts), slab_grad))
    whole = lax.all_to_all(spread(one, nz * nx), ("z", "x"), 0, 0).reshape(held)
    guest = by_xor(guest, ("z", "c"), 2 * nz, near)
    whole, guest = lax.optimization_barrier((whole, guest))
    theirs = swap_cores(whole)
    weight_grad, guest = half_call(core, whole, scale, guest)
    weight_grad = rest_call(1 - core, theirs, scale, weight_grad).reshape(kernel.shape)
    return y_stay[None], guest, slab_grad, weight_grad


def solution(mesh):
    nx = mesh.shape["space"]
    ny = nz = math.isqrt(mesh.shape["dp"] // 2)
    fine = Mesh(mesh.devices.reshape(ny, nz, 2, nx), ("y", "z", "c", "x"))
    block = P(("y", "z", "c"), None, "x", None, None)

    def whole(clips, lengths, partner, kernel, cot_stay, cot_guest):
        slabs, _, height, width, _ = clips.shape
        scale = 1.0 / math.sqrt(slabs * cot_stay.shape[1] * height * width)
        return jax.shard_map(
            functools.partial(shards, ny, nz, nx, scale),
            mesh=fine,
            in_specs=(block, P(("y", "z", "c")), P(), P(), block, block),
            out_specs=(block, block, block, P()),
            check_vma=False,
        )(clips, lengths, partner, kernel, cot_stay, cot_guest)

    return whole
```

time: 128 us -> 109 us (0.85)
  the two profiles are of different devices: /device:TPU:2 before, /device:TPU:1 now
where the time goes in v2:
time: 109 us; the launch traced here: 108 us
  starting transfers between devices  65.2 us (60%)
  waiting for transfers between devices  24.6 us (23%)
  Pallas kernels  12.1 us (11%)
  local copies, waits for them, and re-layouts  3.34 us (3%)
  between operations  1.59 us (1%)
    ppermute x4, starting transfers between devices, moved(): there = lax.ppermute(item, axes, pairs)  17.2 us
    ppermute x2, starting transfers between devices, swap_cores(): return lax.ppermute(value, 'c', [(0, 1), (1, 0)])  15.1 us
    all_to_all x1, waiting for transfers between devices, shards(): whole = lax.all_to_all(spread(one, nz * nx), ('z', 'x'), 0, 0).reshape(held)  11.9 us
    ppermute x4, starting transfers between devices, edges(): return (lax.ppermute(last, 'x', up), lax.ppermute(first, 'x', down))  11.5 us
    all_to_all x1, starting transfers between devices, shards(): lax.all_to_all(half.reshape((nz * nx, -1, held[2])), ('z', 'x'), 0, 0)  10.8 us
    all_to_all x1, starting transfers between devices, shards(): parts = lax.all_to_all(spread(one, ny), 'y', 0, 0)  5.76 us
    all_to_all x1, waiting for transfers between devices, shards(): parts = lax.all_to_all(spread(one, ny), 'y', 0, 0)  5.46 us
    all_to_all x1, starting transfers between devices, shards(): whole = lax.all_to_all(spread(one, nz * nx), ('z', 'x'), 0, 0).reshape(held)  4.84 us
  transfers between devices with their start and end apart: 13, of which 6 were waited for; matrix products, arithmetic and copies ran while one was open for 1% of the time, Pallas kernels for 7%

profile of v2, /device:TPU:1, one launch (start us, length us, event | category | flops | bytes accessed | tf_op | source)
XLA Modules:
  0.0 107.6 jit_solution(2256979210814127948)
XLA Ops:
  1.3 9.7 %conditional.4 = (bf16[2,4,32,128]{3,2,1,0:T(8,128)(2,1)}, bf16[2,4,1,32,128]{4,3,2,1,0:T(8,128)(2,1)}, bf16[2,4,1,32,128]{4,3,2,1,0:T(8,128)(2,1)}) conditional(s32[]{:T(128)} %clamp.9, (bf16[2,4,32,128]{3,2,1,0:T(8,128)(2,1)}, bf16[2,4,4,32,128]{4,3,2,1,0:T(8,128)(2,1)}) %tuple.274, ...), branch_computations={%region_0.1_spmd, %region_1.2_spmd, %region_2.3_spmd, %region_3.4_... | conditional | bytes 1048720 | solution.py:290
  1.4 1.5 %collective-permute-start.48 = (bf16[2,4,32,128]{3,2,1,0:T(8,128)(2,1)}, bf16[2,4,32,128]{3,2,1,0:T(8,128)(2,1)}, u32[]{:S(2)}, u32[]{:S(2)}) collective-permute-start(bf16[2,4,32,128]{3,2,1,0:T(8,128)(2,1)} %get-tuple-element.241), channel_id=1, source_target_pairs={{0,0},{4,4},{8,8},{12,12},{16,16},{20,20},{24,24},{28,28},{32,32},... | collective-permute-start | bytes 196616 | tf_op jit(solution)/shard_map/cond/branch_0_fun/ppermute | solution.py:285
  5.1 5.2 %collective-permute-start.49 = (bf16[2,4,1,32,128]{4,3,2,1,0:T(8,128)(2,1)S(1)}, bf16[2,4,1,32,128]{4,3,2,1,0:T(8,128)(2,1)}, u32[]{:S(2)}, u32[]{:S(2)}) collective-permute-start(bf16[2,4,1,32,128]{4,3,2,1,0:T(8,128)(2,1)S(1)} %get-tuple-element.424), channel_id=1, source_target_pairs={{0,1},{1,2},{2,3},{4,5},{5,6},{6,7},{8,9},{9,10},{10,11},{12,13},{... | collective-permute-start | bytes 196616 | tf_op jit(solution)/shard_map/cond/branch_0_fun/ppermute | solution.py:313
  11.0 12.2 %conditional.5 = (bf16[2,4,32,128]{3,2,1,0:T(8,128)(2,1)}, bf16[2,4,32,128]{3,2,1,0:T(8,128)(2,1)}, bf16[2,4,32,128]{3,2,1,0:T(8,128)(2,1)S(1)}, f32[512,128]{1,0:T(8,128)S(1)}) conditional(s32[]{:T(128)} %clamp.8, (bf16[2,4,32,128]{3,2,1,0:T(8,128)(2,1)}, s32[2]{0:T(128)S(1)}, bf16[2,4,1,32,128]{4,3,2,1,0:T(8,128)(2,1)}, ...), branch_computations={%region_16.17_spmd, %region_17.18_spmd, %region_18.19_spmd, %regio... | conditional | bytes 262216 | solution.py:290
  11.0 7.8 %collective-permute-start.4 = (bf16[2,4,32,128]{3,2,1,0:T(8,128)(2,1)}, bf16[2,4,32,128]{3,2,1,0:T(8,128)(2,1)}, u32[]{:S(2)}, u32[]{:S(2)}) collective-permute-start(bf16[2,4,32,128]{3,2,1,0:T(8,128)(2,1)} %get-tuple-element.309), channel_id=1, source_target_pairs={{0,256},{64,320},{128,384},{192,448},{256,0},{320,64},{384,128},{4... | collective-permute-start | bytes 196616 | tf_op jit(solution)/shard_map/cond/branch_4_fun/ppermute | solution.py:285
  18.8 3.9 %forward.12 = (bf16[2,4,32,128]{3,2,1,0:T(8,128)(2,1)}, bf16[2,4,32,128]{3,2,1,0:T(8,128)(2,1)S(1)}, f32[512,128]{1,0:T(8,128)S(1)}) custom-call(s32[2]{0:T(128)S(1)} %get-tuple-element.310.lengths, bf16[2,4,1,32,128]{4,3,2,1,0:T(8,128)(2,1)} %get-tuple-element.311.low, bf16[2,4,1,32,128]{4,3,2,1,0:T(8,128)(2,1)} %get-tuple-element.312.high, ...), custom_call_target="tpu_custom_call" | custom-call | tf_op jit(solution)/shard_map/cond/branch_4_fun/forward/pallas_call | solution.py:152
  23.2 3.1 %weights.1 = (bf16[2,2,4,32,128]{4,3,2,1,0:T(8,128)(2,1)S(1)}, bf16[2,2,1,32,128]{4,3,2,1,0:T(8,128)(2,1)S(1)}, bf16[2,2,1,32,128]{4,3,2,1,0:T(8,128)(2,1)S(1)},...) custom-call(s32[1]{0:T(128)} %bitcast.4.core.first, bf16[2,4,1,32,128]{4,3,2,1,0:T(8,128)(2,1)} %get-tuple-element.399.low, ...), custom_call_target="tpu_custom_call" | custom-call | tf_op jit(solution)/shard_map/weights/pallas_call | solution.py:177
  26.3 7.6 %collective-permute-start.96 = (bf16[27,64,128]{2,1,0:T(8,128)(2,1)S(1)}, bf16[27,64,128]{2,1,0:T(8,128)(2,1)S(1)}, u32[]{:S(2)}, u32[]{:S(2)}) collective-permute-start(bf16[27,64,128]{2,1,0:T(8,128)(2,1)S(1)} %get-tuple-element.405), channel_id=1, source_target_pairs={{0,4},{4,0},{1,5},{5,1},{2,6},{6,2},{3,7},{7,3},{8,12},{12,8},{9,1... | collective-permute-start | bytes 1327112 | tf_op jit(solution)/shard_map/ppermute | solution.py:294
  34.0 1.4 %collective-permute-done.96 = bf16[27,64,128]{2,1,0:T(8,128)(2,1)S(1)} collective-permute-done((bf16[27,64,128]{2,1,0:T(8,128)(2,1)S(1)}, bf16[27,64,128]{2,1,0:T(8,128)(2,1)S(1)}, u32[]{:S(2)}, u32[]{:S(2)}) %collective-permute-start.96) | collective-permute-done | bytes 442400 | tf_op jit(solution)/shard_map/ppermute | solution.py:294
  36.4 10.8 %all-to-all-start = ((bf16[32,64,128]{2,1,0:T(8,128)(2,1)}), bf16[32,64,128]{2,1,0:T(8,128)(2,1)S(1)}, u32[]{:S(2)}, u32[]{:S(2)}) async-start(bf16[32,64,128]{2,1,0:T(8,128)(2,1)} %pad.5), calls=%async_computation | async-start | bytes 1048576 | tf_op jit(solution)/shard_map/all_to_all | solution.py:327
  47.1 15.1 %conditional.6 = (bf16[2,4,32,128]{3,2,1,0:T(8,128)(2,1)}, bf16[2,2,1,32,128]{4,3,2,1,0:T(8,128)(2,1)}, bf16[2,2,1,32,128]{4,3,2,1,0:T(8,128)(2,1)}) conditional(s32[]{:T(128)} %clamp.8, (bf16[2,4,32,128]{3,2,1,0:T(8,128)(2,1)S(1)}, bf16[2,2,1,32,128]{4,3,2,1,0:T(8,128)(2,1)S(1)}, ...), branch_computations={%region_25.26_spmd, %region_26.27_spmd, %region_27.28_spmd, %regio... | conditional | bytes 524432 | solution.py:290
  47.2 6.4 %collective-permute-start.20 = (bf16[2,4,32,128]{3,2,1,0:T(8,128)(2,1)S(1)}, bf16[2,4,32,128]{3,2,1,0:T(8,128)(2,1)}, u32[]{:S(2)}, u32[]{:S(2)}) collective-permute-start(bf16[2,4,32,128]{3,2,1,0:T(8,128)(2,1)S(1)} %get-tuple-element.357), channel_id=1, source_target_pairs={{0,256},{64,320},{128,384},{192,448},{256,0},{320,64},{384,128},{4... | collective-permute-start | bytes 196616 | tf_op jit(solution)/shard_map/cond/branch_4_fun/ppermute | solution.py:285
  53.6 3.7 %collective-permute-start.21 = (bf16[2,2,1,32,128]{4,3,2,1,0:T(8,128)(2,1)S(1)}, bf16[2,2,1,32,128]{4,3,2,1,0:T(8,128)(2,1)}, u32[]{:S(2)}, u32[]{:S(2)}) collective-permute-start(bf16[2,2,1,32,128]{4,3,2,1,0:T(8,128)(2,1)S(1)} %get-tuple-element.358), channel_id=1, source_target_pairs={{0,1},{1,2},{2,3},{4,5},{5,6},{6,7},{8,9},{9,10},{10,11},{12,13},{... | collective-permute-start | bytes 98312 | tf_op jit(solution)/shard_map/cond/branch_4_fun/ppermute | solution.py:313
  58.6 3.6 %collective-permute-done.22 = bf16[2,2,1,32,128]{4,3,2,1,0:T(8,128)(2,1)} collective-permute-done((bf16[2,2,1,32,128]{4,3,2,1,0:T(8,128)(2,1)S(1)}, bf16[2,2,1,32,128]{4,3,2,1,0:T(8,128)(2,1)}, u32[]{:S(2)}, u32[]{:S(2)}) %collective-permute-start.22) | collective-permute-done | bytes 32800 | tf_op jit(solution)/shard_map/cond/branch_4_fun/ppermute | solution.py:313
  62.3 1.5 %all-to-all-done = bf16[32,64,128]{2,1,0:T(8,128)(2,1)S(1)} async-done(((bf16[32,64,128]{2,1,0:T(8,128)(2,1)}), bf16[32,64,128]{2,1,0:T(8,128)(2,1)S(1)}, u32[]{:S(2)}, u32[]{:S(2)}) %all-to-all-start) | async-done | bytes 524320 | tf_op jit(solution)/shard_map/all_to_all | solution.py:327
  64.5 5.8 %all-to-all-start.1 = ((bf16[8,64,128]{2,1,0:T(8,128)(2,1)}), bf16[8,64,128]{2,1,0:T(8,128)(2,1)S(1)}, u32[]{:S(2)}, u32[]{:S(2)}) async-start(bf16[8,64,128]{2,1,0:T(8,128)(2,1)} %broadcast_in_dim.7), calls=%async_computation.1 | async-start | bytes 262144 | tf_op jit(solution)/shard_map/all_to_all | solution.py:331
  70.3 2.6 %backward.1 = bf16[2,4,4,32,128]{4,3,2,1,0:T(8,128)(2,1)} custom-call(bf16[2,2,4,32,128]{4,3,2,1,0:T(8,128)(2,1)S(1)} %get-tuple-element.413.dz, bf16[2,2,1,32,128]{4,3,2,1,0:T(8,128)(2,1)} %get-tuple-element.414.low, bf16[2,2,1,32,128]{4,3,2,1,0:T(8,128)(2,1)} %get-tuple-element.415.high, bf16[27,128,128]{2,1,0:T(8,128)(2,1)S(1)} %bitcast.22), custom_call_target="tpu_custom_call" | custom-call | tf_op jit(solution)/shard_map/backward/pallas_call | solution.py:203
  72.8 5.5 %all-to-all-done.1 = bf16[8,64,128]{2,1,0:T(8,128)(2,1)S(1)} async-done(((bf16[8,64,128]{2,1,0:T(8,128)(2,1)}), bf16[8,64,128]{2,1,0:T(8,128)(2,1)S(1)}, u32[]{:S(2)}, u32[]{:S(2)}) %all-to-all-start.1) | async-done | bytes 131104 | tf_op jit(solution)/shard_map/all_to_all | solution.py:331
  79.2 4.8 %all-to-all-start.2 = ((bf16[32,64,128]{2,1,0:T(8,128)(2,1)}), bf16[32,64,128]{2,1,0:T(8,128)(2,1)S(1)}, u32[]{:S(2)}, u32[]{:S(2)}) async-start(bf16[32,64,128]{2,1,0:T(8,128)(2,1)} %broadcast_in_dim.8), calls=%async_computation.2 | async-start | bytes 1048576 | tf_op jit(solution)/shard_map/all_to_all | solution.py:334
  84.1 1.5 %conditional.7 = (bf16[2,4,32,128]{3,2,1,0:T(8,128)(2,1)}) conditional(s32[]{:T(128)} %clamp.9, bf16[2,4,32,128]{3,2,1,0:T(8,128)(2,1)} %get-tuple-element.417, bf16[2,4,32,128]{3,2,1,0:T(8,128)(2,1)} %get-tuple-element.417, bf16[2,4,32,128]{3,2,1,0:T(8,128)(2,1)} %get-tuple-element.417, ...), branch_computations={%region_34.35_spmd, %region_35.36_spmd, %region_36.37_spmd, %regio... | conditional | bytes 262192 | solution.py:290
  84.1 1.5 %collective-permute-start.32 = (bf16[2,4,32,128]{3,2,1,0:T(8,128)(2,1)}, bf16[2,4,32,128]{3,2,1,0:T(8,128)(2,1)}, u32[]{:S(2)}, u32[]{:S(2)}) collective-permute-start(bf16[2,4,32,128]{3,2,1,0:T(8,128)(2,1)} %param.32), channel_id=1, source_target_pairs={{0,0},{4,4},{8,8},{12,12},{16,16},{20,20},{24,24},{28,28},{32,32},... | collective-permute-start | bytes 196616 | tf_op jit(solution)/shard_map/cond/branch_0_fun/ppermute | solution.py:285
  85.6 11.9 %all-to-all-done.2.rows = bf16[32,64,128]{2,1,0:T(8,128)(2,1)S(1)} async-done(((bf16[32,64,128]{2,1,0:T(8,128)(2,1)}), bf16[32,64,128]{2,1,0:T(8,128)(2,1)S(1)}, u32[]{:S(2)}, u32[]{:S(2)}) %all-to-all-start.2) | async-done | bytes 524320 | tf_op jit(solution)/shard_map/all_to_all | solution.py:334
  97.5 7.4 %collective-permute-start.97 = (bf16[32,64,128]{2,1,0:T(8,128)(2,1)S(1)}, bf16[32,64,128]{2,1,0:T(8,128)(2,1)S(1)}, u32[]{:S(2)}, u32[]{:S(2)}) collective-permute-start(bf16[32,64,128]{2,1,0:T(8,128)(2,1)S(1)} %all-to-all-done.2.rows), channel_id=1, source_target_pairs={{0,4},{4,0},{1,5},{5,1},{2,6},{6,2},{3,7},{7,3},{8,12},{12,8},{9,1... | collective-permute-start | bytes 1572872 | tf_op jit(solution)/shard_map/ppermute | solution.py:294
  105.0 1.5 %own.1 = (f32[27,128,128]{2,1,0:T(8,128)}, bf16[1,2,4,32,128]{4,3,2,1,0:T(8,128)(2,1)}) custom-call(s32[1]{0:T(128)} %bitcast.4.core.first, bf16[32,64,128]{2,1,0:T(8,128)(2,1)S(1)} %all-to-all-done.2.rows, bf16[2,4,32,128]{3,2,1,0:T(8,128)(2,1)} %get-tuple-element.559.passed), custom_call_target="tpu_custom_call" | custom-call | tf_op jit(solution)/shard_map/own/pallas_call | solution.py:234
  (24 shorter events, 7.8 us)
Async XLA Ops:
  1.3 9.7 %copy-start.1 = (bf16[3,3,3,128,128]{4,3,2,1,0:T(8,128)(2,1)S(1)}, bf16[3,3,3,128,128]{4,3,2,1,0:T(8,128)(2,1)}, u32[]{:S(2)}) copy-start(bf16[3,3,3,128,128]{4,3,2,1,0:T(8,128)(2,1)} %param.57) | copy-start | bytes 2654212
  1.3 9.7 %copy-start.2 = (s32[2]{0:T(128)S(1)}, s32[2]{0:T(128)}, u32[]{:S(2)}) copy-start(s32[2]{0:T(128)} %param.55) | copy-start | bytes 28
  1.4 8.9 %collective-permute-start.48 = (bf16[2,4,32,128]{3,2,1,0:T(8,128)(2,1)}, bf16[2,4,32,128]{3,2,1,0:T(8,128)(2,1)}, u32[]{:S(2)}, u32[]{:S(2)}) collective-permute-start(bf16[2,4,32,128]{3,2,1,0:T(8,128)(2,1)} %get-tuple-element.241), channel_id=1, source_target_pairs={{0,0},{4,4},{8,8},{12,12},{16,16},{20,20},{24,24},{28,28},{32,32},... | collective-permute-start | bytes 196616 | tf_op jit(solution)/shard_map/cond/branch_0_fun/ppermute | solution.py:285
  3.8 6.5 %collective-permute-start.50 = (bf16[2,4,1,32,128]{4,3,2,1,0:T(8,128)(2,1)S(1)}, bf16[2,4,1,32,128]{4,3,2,1,0:T(8,128)(2,1)}, u32[]{:S(2)}, u32[]{:S(2)}) collective-permute-start(bf16[2,4,1,32,128]{4,3,2,1,0:T(8,128)(2,1)S(1)} %get-tuple-element.423), channel_id=1, source_target_pairs={{1,0},{2,1},{3,2},{5,4},{6,5},{7,6},{9,8},{10,9},{11,10},{13,12},{... | collective-permute-start | bytes 196616 | tf_op jit(solution)/shard_map/cond/branch_0_fun/ppermute | solution.py:313
  5.1 5.9 %collective-permute-start.49 = (bf16[2,4,1,32,128]{4,3,2,1,0:T(8,128)(2,1)S(1)}, bf16[2,4,1,32,128]{4,3,2,1,0:T(8,128)(2,1)}, u32[]{:S(2)}, u32[]{:S(2)}) collective-permute-start(bf16[2,4,1,32,128]{4,3,2,1,0:T(8,128)(2,1)S(1)} %get-tuple-element.424), channel_id=1, source_target_pairs={{0,1},{1,2},{2,3},{4,5},{5,6},{6,7},{8,9},{9,10},{10,11},{12,13},{... | collective-permute-start | bytes 196616 | tf_op jit(solution)/shard_map/cond/branch_0_fun/ppermute | solution.py:313
  11.0 12.2 %copy-start = (bf16[1,2,4,32,128]{4,3,2,1,0:T(8,128)(2,1)S(1)}, bf16[1,2,4,32,128]{4,3,2,1,0:T(8,128)(2,1)}, u32[]{:S(2)}) copy-start(bf16[1,2,4,32,128]{4,3,2,1,0:T(8,128)(2,1)} %param.58) | copy-start | bytes 196612
  11.0 11.8 %collective-permute-start.4 = (bf16[2,4,32,128]{3,2,1,0:T(8,128)(2,1)}, bf16[2,4,32,128]{3,2,1,0:T(8,128)(2,1)}, u32[]{:S(2)}, u32[]{:S(2)}) collective-permute-start(bf16[2,4,32,128]{3,2,1,0:T(8,128)(2,1)} %get-tuple-element.309), channel_id=1, source_target_pairs={{0,256},{64,320},{128,384},{192,448},{256,0},{320,64},{384,128},{4... | collective-permute-start | bytes 196616 | tf_op jit(solution)/shard_map/cond/branch_4_fun/ppermute | solution.py:285
  26.3 9.0 %collective-permute-start.96 = (bf16[27,64,128]{2,1,0:T(8,128)(2,1)S(1)}, bf16[27,64,128]{2,1,0:T(8,128)(2,1)S(1)}, u32[]{:S(2)}, u32[]{:S(2)}) collective-permute-start(bf16[27,64,128]{2,1,0:T(8,128)(2,1)S(1)} %get-tuple-element.405), channel_id=1, source_target_pairs={{0,4},{4,0},{1,5},{5,1},{2,6},{6,2},{3,7},{7,3},{8,12},{12,8},{9,1... | collective-permute-start | bytes 1327112 | tf_op jit(solution)/shard_map/ppermute | solution.py:294
  36.4 27.3 %all-to-all-start = ((bf16[32,64,128]{2,1,0:T(8,128)(2,1)}), bf16[32,64,128]{2,1,0:T(8,128)(2,1)S(1)}, u32[]{:S(2)}, u32[]{:S(2)}) async-start(bf16[32,64,128]{2,1,0:T(8,128)(2,1)} %pad.5), calls=%async_computation | async-start | bytes 1048576 | tf_op jit(solution)/shard_map/all_to_all | solution.py:327
  47.2 15.1 %collective-permute-start.20 = (bf16[2,4,32,128]{3,2,1,0:T(8,128)(2,1)S(1)}, bf16[2,4,32,128]{3,2,1,0:T(8,128)(2,1)}, u32[]{:S(2)}, u32[]{:S(2)}) collective-permute-start(bf16[2,4,32,128]{3,2,1,0:T(8,128)(2,1)S(1)} %get-tuple-element.357), channel_id=1, source_target_pairs={{0,256},{64,320},{128,384},{192,448},{256,0},{320,64},{384,128},{4... | collective-permute-start | bytes 196616 | tf_op jit(solution)/shard_map/cond/branch_4_fun/ppermute | solution.py:285
  53.6 5.0 %collective-permute-start.21 = (bf16[2,2,1,32,128]{4,3,2,1,0:T(8,128)(2,1)S(1)}, bf16[2,2,1,32,128]{4,3,2,1,0:T(8,128)(2,1)}, u32[]{:S(2)}, u32[]{:S(2)}) collective-permute-start(bf16[2,2,1,32,128]{4,3,2,1,0:T(8,128)(2,1)S(1)} %get-tuple-element.358), channel_id=1, source_target_pairs={{0,1},{1,2},{2,3},{4,5},{5,6},{6,7},{8,9},{9,10},{10,11},{12,13},{... | collective-permute-start | bytes 98312 | tf_op jit(solution)/shard_map/cond/branch_4_fun/ppermute | solution.py:313
  57.3 4.9 %collective-permute-start.22 = (bf16[2,2,1,32,128]{4,3,2,1,0:T(8,128)(2,1)S(1)}, bf16[2,2,1,32,128]{4,3,2,1,0:T(8,128)(2,1)}, u32[]{:S(2)}, u32[]{:S(2)}) collective-permute-start(bf16[2,2,1,32,128]{4,3,2,1,0:T(8,128)(2,1)S(1)} %get-tuple-element.359), channel_id=1, source_target_pairs={{1,0},{2,1},{3,2},{5,4},{6,5},{7,6},{9,8},{10,9},{11,10},{13,12},{... | collective-permute-start | bytes 98312 | tf_op jit(solution)/shard_map/cond/branch_4_fun/ppermute | solution.py:313
  64.5 13.8 %all-to-all-start.1 = ((bf16[8,64,128]{2,1,0:T(8,128)(2,1)}), bf16[8,64,128]{2,1,0:T(8,128)(2,1)S(1)}, u32[]{:S(2)}, u32[]{:S(2)}) async-start(bf16[8,64,128]{2,1,0:T(8,128)(2,1)} %broadcast_in_dim.7), calls=%async_computation.1 | async-start | bytes 262144 | tf_op jit(solution)/shard_map/all_to_all | solution.py:331
  79.2 18.3 %all-to-all-start.2 = ((bf16[32,64,128]{2,1,0:T(8,128)(2,1)}), bf16[32,64,128]{2,1,0:T(8,128)(2,1)S(1)}, u32[]{:S(2)}, u32[]{:S(2)}) async-start(bf16[32,64,128]{2,1,0:T(8,128)(2,1)} %broadcast_in_dim.8), calls=%async_computation.2 | async-start | bytes 1048576 | tf_op jit(solution)/shard_map/all_to_all | solution.py:334
  84.1 1.5 %collective-permute-start.32 = (bf16[2,4,32,128]{3,2,1,0:T(8,128)(2,1)}, bf16[2,4,32,128]{3,2,1,0:T(8,128)(2,1)}, u32[]{:S(2)}, u32[]{:S(2)}) collective-permute-start(bf16[2,4,32,128]{3,2,1,0:T(8,128)(2,1)} %param.32), channel_id=1, source_target_pairs={{0,0},{4,4},{8,8},{12,12},{16,16},{20,20},{24,24},{28,28},{32,32},... | collective-permute-start | bytes 196616 | tf_op jit(solution)/shard_map/cond/branch_0_fun/ppermute | solution.py:285
  97.5 9.0 %collective-permute-start.97 = (bf16[32,64,128]{2,1,0:T(8,128)(2,1)S(1)}, bf16[32,64,128]{2,1,0:T(8,128)(2,1)S(1)}, u32[]{:S(2)}, u32[]{:S(2)}) collective-permute-start(bf16[32,64,128]{2,1,0:T(8,128)(2,1)S(1)} %all-to-all-done.2.rows), channel_id=1, source_target_pairs={{0,4},{4,0},{1,5},{5,1},{2,6},{6,2},{3,7},{7,3},{8,12},{12,8},{9,1... | collective-permute-start | bytes 1572872 | tf_op jit(solution)/shard_map/ppermute | solution.py:294

commit v3 on v2

--- a/solution.py
+++ b/solution.py
@@ -12,7 +12,7 @@
 BF = jnp.bfloat16
 F32 = jnp.float32
 TAPS = 27
-PADDED_TAPS = 32
+HALF_TAPS = 14
 
 
 def widen(wide, block, first, mirrored):
@@ -66,8 +66,24 @@
     return block.reshape(-1, wide.shape[4])
 
 
+def half_weights(half, wide, turned, sums, rows):
+    chans = turned.shape[0]
+    first = 4 * half
+    blocks = []
+    for number in range(5):
+        offset = first + number
+        tap_t = lax.div(offset, 3)
+        block = wide[:, pl.ds(tap_t, wide.shape[1] - 2), pl.ds(offset - 3 * tap_t, rows)]
+        blocks.append(block.reshape(-1, wide.shape[4]))
+    total = jnp.dot(turned[...], jnp.concatenate(blocks, axis=1), preferred_element_type=F32)
+    for tap in range(15):
+        sums[tap] = total[:, tap * chans : (tap + 1) * chans].T
+    sums[15] = jnp.zeros((chans, chans), F32)
+    return sums[pl.ds(2 * half, HALF_TAPS)]
+
+
 def weight_kernel(core, low, high, slope_in, cot_guest_in, clips, cot_stay,
-                  dz_out, dz_first, dz_last, mine, other, edge, slope, cot_guest, wide, sums, sems):
+                  dz_out, dz_first, dz_last, other, wide, turned, edge, slope, cot_guest, sums, sems):
     slabs, frames, rows, width, chans = clips.shape
     out_frames = frames - 2
     per = rows * width
@@ -95,16 +111,42 @@
             dz_out[slab, frame] = dz
             dz_first[slab, frame] = dz[0:1]
             dz_last[slab, frame] = dz[rows - 1 : rows]
-    dz_all = jnp.concatenate(parts, axis=0)
-    for tap in range(9):
-        term = lax.dot_general(
-            window(wide, tap, rows), dz_all, (((0,), (0,)), ((), ())), preferred_element_type=F32
-        )
-        sums[3 * tap : 3 * tap + 3] = term.reshape(3, chans, chans)
-    half = chans // 2
-    own = core[0]
-    mine[...] = sums[:, pl.ds(pl.multiple_of(own * half, half), half), :]
-    other[...] = sums[:, pl.ds(pl.multiple_of((1 - own) * half, half), half), :].astype(BF)
+    turned[...] = jnp.concatenate(parts, axis=0).astype(F32).T.astype(BF)
+    other[...] = half_weights(1 - core[0], wide, turned, sums, rows).astype(BF)
+
+
+def mine_kernel(core, wide, turned, mine, sums):
+    mine[...] = half_weights(core[0], wide, turned, sums, wide.shape[2] - 2)
+
+
+def joined_kernel(mine, got, out, buffer, sems):
+    step = buffer.shape[0] // 2
+    copies = []
+    for part in range(2):
+        at = slice(part * step, part * step + step)
+        buffer[at] = (mine[at] + got[at].astype(F32)).astype(BF)
+        copies.append(pltpu.make_async_copy(buffer.at[at], out.at[at], sems.at[part]))
+        copies[-1].start()
+    for copy in copies:
+        copy.wait()
+
+
+def spread_kernel(parts, out, buffer, sems):
+    held, count = buffer.shape[0], out.shape[0]
+    total = parts[0].astype(F32)
+    for part in range(1, parts.shape[0]):
+        total = total + parts[part].astype(F32)
+    total = total.astype(BF)
+    for place in range(held):
+        buffer[place] = total
+    copies = [
+        pltpu.make_async_copy(buffer, out.at[first : first + held], sems.at[first // held])
+        for first in range(0, count, held)
+    ]
+    for copy in copies:
+        copy.start()
+    for copy in copies:
+        copy.wait()
 
 
 def backward_kernel(dz, low, high, kernel, grads, wide):
@@ -173,29 +215,70 @@
     slabs, frames, rows, width, chans = clips.shape
     one = cot_stay.shape
     edge = (slabs, frames - 2, 1, width, chans)
-    half = (TAPS, chans // 2, chans)
+    places = slabs * (frames - 2) * rows * width
     return pl.pallas_call(
         weight_kernel,
         out_shape=(
             jax.ShapeDtypeStruct((slabs,) + one, BF),
             jax.ShapeDtypeStruct(edge, BF),
             jax.ShapeDtypeStruct(edge, BF),
-            jax.ShapeDtypeStruct(half, F32),
-            jax.ShapeDtypeStruct(half, BF),
+            jax.ShapeDtypeStruct((HALF_TAPS, chans, chans), BF),
+            jax.ShapeDtypeStruct((slabs, frames, rows + 2, width, 3 * chans), BF),
+            jax.ShapeDtypeStruct((chans, places), BF),
         ),
         in_specs=smem(1) + anywhere(4) + vmem(2),
-        out_specs=tuple(vmem(5)),
+        out_specs=tuple(vmem(6)),
         scratch_shapes=[
             pltpu.VMEM((2,) + low.shape, BF),
             pltpu.VMEM(slope.shape, F32),
             pltpu.VMEM(one, BF),
-            pltpu.VMEM((slabs, frames, rows + 2, width, 3 * chans), BF),
-            pltpu.VMEM((TAPS, chans, chans), F32),
+            pltpu.VMEM((16, chans, chans), F32),
             pltpu.SemaphoreType.DMA((4,)),
         ],
         compiler_params=pltpu.CompilerParams(vmem_limit_bytes=32 * 2**20),
         name="weights",
     )(core, low, high, slope, cot_guest, clips, cot_stay)
+
+
+def mine_call(core, wide, turned):
+    chans = turned.shape[0]
+    return pl.pallas_call(
+        mine_kernel,
+        out_shape=jax.ShapeDtypeStruct((HALF_TAPS, chans, chans), F32),
+        in_specs=smem(1) + vmem(2),
+        out_specs=vmem(1)[0],
+        scratch_shapes=[pltpu.VMEM((16, chans, chans), F32)],
+        compiler_params=pltpu.CompilerParams(vmem_limit_bytes=32 * 2**20),
+        name="mine",
+    )(core, wide, turned)
+
+
+def joined_call(mine, got):
+    return pl.pallas_call(
+        joined_kernel,
+        out_shape=jax.ShapeDtypeStruct(mine.shape, BF),
+        in_specs=vmem(2),
+        out_specs=anywhere(1)[0],
+        scratch_shapes=[pltpu.VMEM(mine.shape, BF), pltpu.SemaphoreType.DMA((2,))],
+        compiler_params=pltpu.CompilerParams(vmem_limit_bytes=32 * 2**20),
+        name="joined",
+    )(mine, got)
+
+
+def spread_call(parts, count):
+    held = min(8, count)
+    return pl.pallas_call(
+        spread_kernel,
+        out_shape=jax.ShapeDtypeStruct((count,) + parts.shape[1:], BF),
+        in_specs=vmem(1),
+        out_specs=anywhere(1)[0],
+        scratch_shapes=[
+            pltpu.VMEM((held,) + parts.shape[1:], BF),
+            pltpu.SemaphoreType.DMA((count // held,)),
+        ],
+        compiler_params=pltpu.CompilerParams(vmem_limit_bytes=32 * 2**20),
+        name="spread",
+    )(parts)
 
 
 def backward_call(dz, low, high, kernel):
@@ -211,36 +294,48 @@
     )(dz, low, high, kernel)
 
 
-def half_kernel(scale, groups, first, rows, passed, out, passed_out, buffer, held, sems):
-    taps, half, _ = buffer.shape
-    step = taps // groups
-    place = pl.ds(pl.multiple_of(first[0] * half, half), half)
-    load = pltpu.make_async_copy(passed, held, sems.at[groups])
+def write_taps(scale, first, rows, out, buffer, sems):
+    pieces = ((0, 7), (7, HALF_TAPS - 1), (HALF_TAPS - 1, HALF_TAPS))
+    copies = []
+    for number, (low, high) in enumerate(pieces):
+        buffer[low:high] = rows[low:high].astype(F32) * scale
+        place = pl.ds(first[0] * HALF_TAPS + low, high - low)
+        copies.append(pltpu.make_async_copy(buffer.at[low:high], out.at[place], sems.at[number]))
+        if number < 2:
+            copies[-1].start()
+        else:
+            pl.when(first[0] == 0)(copies[-1].start)
+
+    def wait():
+        copies[0].wait()
+        copies[1].wait()
+        pl.when(first[0] == 0)(copies[2].wait)
+
+    return wait
+
+
+def half_kernel(scale, first, rows, passed, out, passed_out, buffer, held, sems):
+    load = pltpu.make_async_copy(passed, held, sems.at[3])
+    store = pltpu.make_async_copy(held, passed_out.at[0], sems.at[4])
     load.start()
-    copies = [pltpu.make_async_copy(held, passed_out.at[0], sems.at[groups + 1])]
-    for group in range(groups):
-        at = slice(group * step, group * step + step)
-        buffer[at] = rows[at].astype(F32) * scale
-        copies.append(pltpu.make_async_copy(buffer.at[at], out.at[at, place, :], sems.at[group]))
-        copies[-1].start()
+    wait = write_taps(scale, first, rows, out, buffer, sems)
     load.wait()
-    copies[0].start()
-    for copy in copies:
-        copy.wait()
+    store.start()
+    wait()
+    store.wait()
 
 
 def half_call(first, rows, scale, passed):
-    _, half, chans = rows.shape
-    return pl.pallas_call(
-        functools.partial(half_kernel, scale, 3),
+    return pl.pallas_call(
+        functools.partial(half_kernel, scale),
         out_shape=(
-            jax.ShapeDtypeStruct((TAPS, 2 * half, chans), F32),
+            jax.ShapeDtypeStruct((TAPS,) + rows.shape[1:], F32),
             jax.ShapeDtypeStruct((1,) + passed.shape, passed.dtype),
         ),
         in_specs=smem(1) + vmem(1) + anywhere(1),
         out_specs=tuple(anywhere(2)),
         scratch_shapes=[
-            pltpu.VMEM((TAPS, half, chans), F32),
+            pltpu.VMEM(rows.shape, F32),
             pltpu.VMEM(passed.shape, passed.dtype),
             pltpu.SemaphoreType.DMA((5,)),
         ],
@@ -249,28 +344,17 @@
     )(first, rows, passed)
 
 
-def rest_kernel(scale, groups, first, rows, _, out, buffer, sems):
-    taps, half, _ = buffer.shape
-    step = taps // groups
-    place = pl.ds(pl.multiple_of(first[0] * half, half), half)
-    copies = []
-    for group in range(groups):
-        at = slice(group * step, group * step + step)
-        buffer[at] = rows[at].astype(F32) * scale
-        copies.append(pltpu.make_async_copy(buffer.at[at], out.at[at, place, :], sems.at[group]))
-        copies[-1].start()
-    for copy in copies:
-        copy.wait()
+def rest_kernel(scale, first, rows, _, out, buffer, sems):
+    write_taps(scale, first, rows, out, buffer, sems)()
 
 
 def rest_call(first, rows, scale, earlier):
-    _, half, chans = rows.shape
-    return pl.pallas_call(
-        functools.partial(rest_kernel, scale, 3),
+    return pl.pallas_call(
+        functools.partial(rest_kernel, scale),
         out_shape=jax.ShapeDtypeStruct(earlier.shape, F32),
         in_specs=smem(1) + vmem(1) + anywhere(1),
         out_specs=anywhere(1)[0],
-        scratch_shapes=[pltpu.VMEM((TAPS, half, chans), F32), pltpu.SemaphoreType.DMA((3,))],
+        scratch_shapes=[pltpu.VMEM(rows.shape, F32), pltpu.SemaphoreType.DMA((3,))],
         input_output_aliases={2: 0},
         compiler_params=pltpu.CompilerParams(vmem_limit_bytes=32 * 2**20),
         name="rest",
@@ -294,44 +378,32 @@
     return lax.ppermute(value, "c", [(0, 1), (1, 0)])
 
 
-def spread(value, count):
-    return jnp.broadcast_to(value[None], (count,) + value.shape)
-
-
-def added(parts):
-    return jnp.sum(parts.astype(F32), axis=0).astype(BF)
-
-
 def shards(ny, nz, nx, scale, clips, lengths, partner, kernel, cot_stay, cot_guest):
     rows = clips.shape[2]
     chans = clips.shape[4]
-    near, far = jnp.bitwise_and(partner[0], 2 * nz - 1), partner[0] // (2 * nz)
+    near = jnp.bitwise_and(partner[0], 2 * nz - 1)
+    far = lax.shift_right_logical(partner[0], jnp.int32((2 * nz).bit_length() - 1))
     up = [(i, i + 1) for i in range(nx - 1)]
     down = [(i + 1, i) for i in range(nx - 1)]
 
     def edges(first, last):
         return lax.ppermute(last, "x", up), lax.ppermute(first, "x", down)
 
-    def clip_edges(whole):
-        return edges(whole[:, :, :1], whole[:, :, rows - 1 :])
-
     core = lax.axis_index("c").astype(jnp.int32).reshape(1)
-    cot_here, (low, high) = by_xor(cot_guest[0], ("z", "c"), 2 * nz, near, clip_edges, (clips,))
+    first, last = lax.optimization_barrier((clips[:, :, :1], clips[:, :, rows - 1 :]))
+    cot_here, (low, high) = by_xor(cot_guest[0], ("z", "c"), 2 * nz, near, edges, (first, last))
     cot_here, (y_stay, y_guest, slope) = by_xor(
         cot_here, "y", ny, far, forward_call, (lengths, low, high, clips, kernel.reshape(9, 3 * chans, chans))
     )
-    dz, dz_first, dz_last, mine, other = weight_call(core, low, high, slope, cot_here, clips, cot_stay[0])
-    half = mine + swap_cores(other).astype(F32)
-    half = jnp.pad(half, ((0, PADDED_TAPS - TAPS), (0, 0), (0, 0))).astype(BF)
-    held = half.shape
-    parts = lax.all_to_all(half.reshape((nz * nx, -1, held[2])), ("z", "x"), 0, 0)
-
+    dz, dz_first, dz_last, other, wide, turned = weight_call(core, low, high, slope, cot_here, clips, cot_stay[0])
+    half = joined_call(mine_call(core, wide, turned), swap_cores(other))
+    parts = lax.all_to_all(half.reshape(ny * nx, -1, chans), ("y", "x"), 0, 0)
     guest, (dz_low, dz_high) = by_xor(y_guest, "y", ny, far, edges, (dz_first, dz_last))
-    one, guest, dz_low, dz_high = lax.optimization_barrier((added(parts), guest, dz_low, dz_high))
-    parts = lax.all_to_all(spread(one, ny), "y", 0, 0)
+    parts, guest, dz_low, dz_high = lax.optimization_barrier((parts, guest, dz_low, dz_high))
+    parts = lax.all_to_all(spread_call(parts, nz), "z", 0, 0)
     slab_grad = backward_call(dz, dz_low, dz_high, kernel.reshape(TAPS, chans, chans))
-    one, slab_grad = lax.optimization_barrier((added(parts), slab_grad))
-    whole = lax.all_to_all(spread(one, nz * nx), ("z", "x"), 0, 0).reshape(held)
+    parts, slab_grad = lax.optimization_barrier((parts, slab_grad))
+    whole = lax.all_to_all(spread_call(parts, ny * nx), ("y", "x"), 0, 0).reshape(half.shape)
     guest = by_xor(guest, ("z", "c"), 2 * nz, near)
     whole, guest = lax.optimization_barrier((whole, guest))
     theirs = swap_cores(whole)

time: 109 us -> 108 us (level)
  Pallas kernels: 12.1 us -> 14.8 us
  local copies, waits for them, and re-layouts: 3.34 us -> 0.9 us
  starting transfers between devices: 65.2 us -> 64.1 us
    ppermute x4, starting transfers between devices: 17.2 us -> 26 us  [moved(): there = lax.ppermute(item, axes, pairs)]
    all_to_all x3, waiting for transfers between devices: 18.9 us -> 12.4 us  [the longest x1 5.35 us: shards(): lax.all_to_all(spread_call(parts, ny * nx), ('y', 'x'), 0, 0)]
    ppermute x2, starting transfers between devices: 15.1 us -> 9.31 us  [swap_cores(): return lax.ppermute(value, 'c', [(0, 1), (1, 0)])]
    ppermute x4, waiting for transfers between devices: 4.33 us -> 8.53 us  [edges(): return (lax.ppermute(last, 'x', up), lax.ppermute(first, 'x', down))]
    ppermute x4, waiting for transfers between devices: 0.01 us -> 3.72 us  [moved(): there = lax.ppermute(item, axes, pairs)]
    pallas_call x2 -> x6, Pallas kernels: 2.48 us -> 5.51 us  [the longest x2 1.55 us: spread_call(): pl.pallas_call(spread_kernel, out_shape=jax.ShapeDtypeStruct((count,) + p...]
    all_to_all x3, starting transfers between devices: 21.4 us -> 18.8 us  [the longest x1 7.88 us: shards(): parts = lax.all_to_all(half.reshape(ny * nx, -1, chans), ('y', 'x'), 0, 0)]
    broadcast_in_dim x2 -> x0, local copies, waits for them, and re-layouts: 1.59 us -> none  [spread(): return jnp.broadcast_to(value[None], (count,) + value.shape)]
  transfers between devices with their start and end apart: 13 -> 13, of which waited for: 6 -> 7; matrix products, arithmetic and copies ran while one was open for 1% -> 0% of each run, Pallas kernels for 7% -> 8%
where the time goes in v3:
time: 108 us; the launch traced here: 107 us
  starting transfers between devices  64.1 us (59%)
  waiting for transfers between devices  25.4 us (24%)
  Pallas kernels  14.8 us (14%)
  between operations  1.61 us (1%)
    ppermute x4, starting transfers between devices, moved(): there = lax.ppermute(item, axes, pairs)  26 us
    ppermute x4, starting transfers between devices, edges(): return (lax.ppermute(last, 'x', up), lax.ppermute(first, 'x', down))  9.99 us
    ppermute x2, starting transfers between devices, swap_cores(): return lax.ppermute(value, 'c', [(0, 1), (1, 0)])  9.31 us
    ppermute x4, waiting for transfers between devices, edges(): return (lax.ppermute(last, 'x', up), lax.ppermute(first, 'x', down))  8.53 us
    all_to_all x1, starting transfers between devices, shards(): parts = lax.all_to_all(half.reshape(ny * nx, -1, chans), ('y', 'x'), 0, 0)  7.88 us
    all_to_all x1, starting transfers between devices, shards(): lax.all_to_all(spread_call(parts, ny * nx), ('y', 'x'), 0, 0)  7.58 us
    all_to_all x1, waiting for transfers between devices, shards(): lax.all_to_all(spread_call(parts, ny * nx), ('y', 'x'), 0, 0)  5.35 us
    all_to_all x1, waiting for transfers between devices, shards(): parts = lax.all_to_all(spread_call(parts, nz), 'z', 0, 0)  5.18 us
  transfers between devices with their start and end apart: 13, of which 7 were waited for; matrix products, arithmetic and copies ran while one was open for 0% of the time, Pallas kernels for 8%

profile of v3, /device:TPU:1, one launch (start us, length us, event | category | flops | bytes accessed | tf_op | source)
XLA Modules:
  0.0 107.2 jit_solution(13974390892338470016)
XLA Ops:
  2.2 21.5 %conditional.4 = (bf16[2,4,32,128]{3,2,1,0:T(8,128)(2,1)}, bf16[2,4,1,32,128]{4,3,2,1,0:T(8,128)(2,1)}, bf16[2,4,1,32,128]{4,3,2,1,0:T(8,128)(2,1)}) conditional(s32[]{:T(128)} %bitcast.1, (bf16[2,4,32,128]{3,2,1,0:T(8,128)(2,1)}, bf16[2,4,1,32,128]{4,3,2,1,0:T(8,128)(2,1)S(1)}, ...), branch_computations={%region_0.0_spmd, %region_1.0_spmd, %region_2.0_spmd, %region_3.0_... | conditional | bytes 786576 | solution.py:374
  2.2 12.1 %collective-permute-start.39 = (bf16[2,4,32,128]{3,2,1,0:T(8,128)(2,1)}, bf16[2,4,32,128]{3,2,1,0:T(8,128)(2,1)}, u32[]{:S(2)}, u32[]{:S(2)}) collective-permute-start(bf16[2,4,32,128]{3,2,1,0:T(8,128)(2,1)} %get-tuple-element.312), channel_id=1, source_target_pairs={{0,52},{4,48},{8,60},{12,56},{16,36},{20,32},{24,44},{28,40},{32,2... | collective-permute-start | bytes 196616 | tf_op jit(solution)/shard_map/cond/branch_13_fun/ppermute | solution.py:369
  14.3 3.7 %collective-permute-start.40 = (bf16[2,4,1,32,128]{4,3,2,1,0:T(8,128)(2,1)S(1)}, bf16[2,4,1,32,128]{4,3,2,1,0:T(8,128)(2,1)}, u32[]{:S(2)}, u32[]{:S(2)}) collective-permute-start(bf16[2,4,1,32,128]{4,3,2,1,0:T(8,128)(2,1)S(1)} %get-tuple-element.313), channel_id=1, source_target_pairs={{0,1},{1,2},{2,3},{4,5},{5,6},{6,7},{8,9},{9,10},{10,11},{12,13},{... | collective-permute-start | bytes 196616 | tf_op jit(solution)/shard_map/cond/branch_13_fun/ppermute | solution.py:390
  19.3 4.3 %collective-permute-done.41 = bf16[2,4,1,32,128]{4,3,2,1,0:T(8,128)(2,1)} collective-permute-done((bf16[2,4,1,32,128]{4,3,2,1,0:T(8,128)(2,1)S(1)}, bf16[2,4,1,32,128]{4,3,2,1,0:T(8,128)(2,1)}, u32[]{:S(2)}, u32[]{:S(2)}) %collective-permute-start.41) | collective-permute-done | bytes 65568 | tf_op jit(solution)/shard_map/cond/branch_13_fun/ppermute | solution.py:390
  23.7 9.5 %conditional.5 = (bf16[2,4,32,128]{3,2,1,0:T(8,128)(2,1)}, bf16[2,4,32,128]{3,2,1,0:T(8,128)(2,1)}, bf16[2,4,32,128]{3,2,1,0:T(8,128)(2,1)S(1)}, f32[512,128]{1,0:T(8,128)S(1)}) conditional(s32[]{:T(128)} %bitcast, (bf16[2,4,32,128]{3,2,1,0:T(8,128)(2,1)}, s32[2]{0:T(128)}, bf16[2,4,1,32,128]{4,3,2,1,0:T(8,128)(2,1)}, ...), branch_computations={%region_16.0_spmd, %region_17.0_spmd, %region_18.0_spmd, %region_1... | conditional | bytes 262216 | solution.py:374
  23.7 5.2 %collective-permute-start.55 = (bf16[2,4,32,128]{3,2,1,0:T(8,128)(2,1)}, bf16[2,4,32,128]{3,2,1,0:T(8,128)(2,1)}, u32[]{:S(2)}, u32[]{:S(2)}) collective-permute-start(bf16[2,4,32,128]{3,2,1,0:T(8,128)(2,1)} %get-tuple-element.384), channel_id=1, source_target_pairs={{0,448},{64,384},{128,320},{192,256},{256,192},{320,128},{384,64},... | collective-permute-start | bytes 196616 | tf_op jit(solution)/shard_map/cond/branch_7_fun/ppermute | solution.py:369
  28.9 4.1 %forward.15 = (bf16[2,4,32,128]{3,2,1,0:T(8,128)(2,1)}, bf16[2,4,32,128]{3,2,1,0:T(8,128)(2,1)S(1)}, f32[512,128]{1,0:T(8,128)S(1)}) custom-call(s32[2]{0:T(128)} %get-tuple-element.385.lengths, bf16[2,4,1,32,128]{4,3,2,1,0:T(8,128)(2,1)} %get-tuple-element.386.low, bf16[2,4,1,32,128]{4,3,2,1,0:T(8,128)(2,1)} %get-tuple-element.387.high, ...), custom_call_target="tpu_custom_call" | custom-call | tf_op jit(solution)/shard_map/cond/branch_7_fun/forward/pallas_call | solution.py:194
  33.2 2.6 %weights.1 = (bf16[2,2,4,32,128]{4,3,2,1,0:T(8,128)(2,1)S(1)}, bf16[2,2,1,32,128]{4,3,2,1,0:T(8,128)(2,1)S(1)}, bf16[2,2,1,32,128]{4,3,2,1,0:T(8,128)(2,1)S(1)},...) custom-call(s32[1]{0:T(128)} %bitcast.5.core.first, ...), custom_call_target="tpu_custom_call" | custom-call | tf_op jit(solution)/shard_map/weights/pallas_call | solution.py:219
  35.9 3.1 %collective-permute-start.96 = (bf16[14,128,128]{2,1,0:T(8,128)(2,1)S(1)}, bf16[14,128,128]{2,1,0:T(8,128)(2,1)S(1)}, u32[]{:S(2)}, u32[]{:S(2)}) collective-permute-start(bf16[14,128,128]{2,1,0:T(8,128)(2,1)S(1)} %get-tuple-element.459), channel_id=1, source_target_pairs={{0,4},{4,0},{1,5},{5,1},{2,6},{6,2},{3,7},{7,3},{8,12},{12,8},{9,1... | collective-permute-start | bytes 1376264 | tf_op jit(solution)/shard_map/ppermute | solution.py:378
  41.2 7.9 %all-to-all-start = ((bf16[32,56,128]{2,1,0:T(8,128)(2,1)}), bf16[32,56,128]{2,1,0:T(8,128)(2,1)S(1)}, u32[]{:S(2)}, u32[]{:S(2)}) async-start(bf16[32,56,128]{2,1,0:T(8,128)(2,1)} %bitcast.7), calls=%async_computation | async-start | bytes 917504 | tf_op jit(solution)/shard_map/all_to_all | solution.py:400
  49.1 13.6 %conditional.6 = (bf16[2,4,32,128]{3,2,1,0:T(8,128)(2,1)}, bf16[2,2,1,32,128]{4,3,2,1,0:T(8,128)(2,1)}, bf16[2,2,1,32,128]{4,3,2,1,0:T(8,128)(2,1)}) conditional(s32[]{:T(128)} %bitcast, (bf16[2,4,32,128]{3,2,1,0:T(8,128)(2,1)S(1)}, bf16[2,2,1,32,128]{4,3,2,1,0:T(8,128)(2,1)S(1)}, ...), branch_computations={%region_24.0_spmd, %region_25.0_spmd, %region_26.0_spmd, %region_2... | conditional | bytes 524432 | solution.py:374
  49.1 4.4 %collective-permute-start.77 = (bf16[2,4,32,128]{3,2,1,0:T(8,128)(2,1)S(1)}, bf16[2,4,32,128]{3,2,1,0:T(8,128)(2,1)}, u32[]{:S(2)}, u32[]{:S(2)}) collective-permute-start(bf16[2,4,32,128]{3,2,1,0:T(8,128)(2,1)S(1)} %get-tuple-element.414), channel_id=1, source_target_pairs={{0,448},{64,384},{128,320},{192,256},{256,192},{320,128},{384,64},... | collective-permute-start | bytes 196616 | tf_op jit(solution)/shard_map/cond/branch_7_fun/ppermute | solution.py:369
  53.5 3.7 %collective-permute-start.78 = (bf16[2,2,1,32,128]{4,3,2,1,0:T(8,128)(2,1)S(1)}, bf16[2,2,1,32,128]{4,3,2,1,0:T(8,128)(2,1)}, u32[]{:S(2)}, u32[]{:S(2)}) collective-permute-start(bf16[2,2,1,32,128]{4,3,2,1,0:T(8,128)(2,1)S(1)} %get-tuple-element.415), channel_id=1, source_target_pairs={{0,1},{1,2},{2,3},{4,5},{5,6},{6,7},{8,9},{9,10},{10,11},{12,13},{... | collective-permute-start | bytes 98312 | tf_op jit(solution)/shard_map/cond/branch_7_fun/ppermute | solution.py:390
  58.5 4.2 %collective-permute-done.79 = bf16[2,2,1,32,128]{4,3,2,1,0:T(8,128)(2,1)} collective-permute-done((bf16[2,2,1,32,128]{4,3,2,1,0:T(8,128)(2,1)S(1)}, bf16[2,2,1,32,128]{4,3,2,1,0:T(8,128)(2,1)}, u32[]{:S(2)}, u32[]{:S(2)}) %collective-permute-start.79) | collective-permute-done | bytes 32800 | tf_op jit(solution)/shard_map/cond/branch_7_fun/ppermute | solution.py:390
  62.7 1.8 %all-to-all-done.parts = bf16[32,56,128]{2,1,0:T(8,128)(2,1)S(1)} async-done(((bf16[32,56,128]{2,1,0:T(8,128)(2,1)}), bf16[32,56,128]{2,1,0:T(8,128)(2,1)S(1)}, u32[]{:S(2)}, u32[]{:S(2)}) %all-to-all-start) | async-done | bytes 458784 | tf_op jit(solution)/shard_map/all_to_all | solution.py:400
  65.3 3.4 %all-to-all-start.1 = ((bf16[8,56,128]{2,1,0:T(8,128)(2,1)}), bf16[8,56,128]{2,1,0:T(8,128)(2,1)S(1)}, u32[]{:S(2)}, u32[]{:S(2)}) async-start(bf16[8,56,128]{2,1,0:T(8,128)(2,1)} %spread.2), calls=%async_computation.1 | async-start | bytes 229376 | tf_op jit(solution)/shard_map/all_to_all | solution.py:403
  68.7 2.6 %backward.1 = bf16[2,4,4,32,128]{4,3,2,1,0:T(8,128)(2,1)} custom-call(bf16[2,2,4,32,128]{4,3,2,1,0:T(8,128)(2,1)S(1)} %get-tuple-element.467.dz, bf16[2,2,1,32,128]{4,3,2,1,0:T(8,128)(2,1)} %get-tuple-element.468.low, bf16[2,2,1,32,128]{4,3,2,1,0:T(8,128)(2,1)} %get-tuple-element.469.high, bf16[27,128,128]{2,1,0:T(8,128)(2,1)S(1)} %bitcast.22), custom_call_target="tpu_custom_call" | custom-call | tf_op jit(solution)/shard_map/backward/pallas_call | solution.py:286
  71.3 5.2 %all-to-all-done.1.parts = bf16[8,56,128]{2,1,0:T(8,128)(2,1)S(1)} async-done(((bf16[8,56,128]{2,1,0:T(8,128)(2,1)}), bf16[8,56,128]{2,1,0:T(8,128)(2,1)S(1)}, u32[]{:S(2)}, u32[]{:S(2)}) %all-to-all-start.1) | async-done | bytes 114720 | tf_op jit(solution)/shard_map/all_to_all | solution.py:403
  77.3 7.6 %all-to-all-start.2 = ((bf16[32,56,128]{2,1,0:T(8,128)(2,1)}), bf16[32,56,128]{2,1,0:T(8,128)(2,1)S(1)}, u32[]{:S(2)}, u32[]{:S(2)}) async-start(bf16[32,56,128]{2,1,0:T(8,128)(2,1)} %spread.3), calls=%async_computation.2 | async-start | bytes 917504 | tf_op jit(solution)/shard_map/all_to_all | solution.py:406
  84.9 8.0 %conditional.7 = (bf16[2,4,32,128]{3,2,1,0:T(8,128)(2,1)}) conditional(s32[]{:T(128)} %bitcast.1, bf16[2,4,32,128]{3,2,1,0:T(8,128)(2,1)} %get-tuple-element.471, bf16[2,4,32,128]{3,2,1,0:T(8,128)(2,1)} %get-tuple-element.471, bf16[2,4,32,128]{3,2,1,0:T(8,128)(2,1)} %get-tuple-element.471, ...), branch_computations={%region_32.0_spmd, %region_33.0_spmd, %region_34.0_spmd, %region_3... | conditional | bytes 262192 | solution.py:374
  84.9 4.3 %collective-permute-start.93 = (bf16[2,4,32,128]{3,2,1,0:T(8,128)(2,1)}, bf16[2,4,32,128]{3,2,1,0:T(8,128)(2,1)}, u32[]{:S(2)}, u32[]{:S(2)}) collective-permute-start(bf16[2,4,32,128]{3,2,1,0:T(8,128)(2,1)} %param.45), channel_id=1, source_target_pairs={{0,52},{4,48},{8,60},{12,56},{16,36},{20,32},{24,44},{28,40},{32,2... | collective-permute-start | bytes 196616 | tf_op jit(solution)/shard_map/cond/branch_13_fun/ppermute | solution.py:369
  89.2 3.7 %collective-permute-done.93 = bf16[2,4,32,128]{3,2,1,0:T(8,128)(2,1)} collective-permute-done((bf16[2,4,32,128]{3,2,1,0:T(8,128)(2,1)}, bf16[2,4,32,128]{3,2,1,0:T(8,128)(2,1)}, u32[]{:S(2)}, u32[]{:S(2)}) %collective-permute-start.93) | collective-permute-done | bytes 65568 | tf_op jit(solution)/shard_map/cond/branch_13_fun/ppermute | solution.py:369
  92.9 5.3 %all-to-all-done.2 = bf16[32,56,128]{2,1,0:T(8,128)(2,1)S(1)} async-done(((bf16[32,56,128]{2,1,0:T(8,128)(2,1)}), bf16[32,56,128]{2,1,0:T(8,128)(2,1)S(1)}, u32[]{:S(2)}, u32[]{:S(2)}) %all-to-all-start.2) | async-done | bytes 458784 | tf_op jit(solution)/shard_map/all_to_all | solution.py:406
  98.3 6.2 %collective-permute-start.97 = (bf16[14,128,128]{2,1,0:T(8,128)(2,1)S(1)}, bf16[14,128,128]{2,1,0:T(8,128)(2,1)S(1)}, u32[]{:S(2)}, u32[]{:S(2)}) collective-permute-start(bf16[14,128,128]{2,1,0:T(8,128)(2,1)S(1)} %bitcast.11), channel_id=1, source_target_pairs={{0,4},{4,0},{1,5},{5,1},{2,6},{6,2},{3,7},{7,3},{8,12},{12,8},{9,1... | collective-permute-start | bytes 1376264 | tf_op jit(solution)/shard_map/ppermute | solution.py:378
  (20 shorter events, 9.8 us)
Async XLA Ops:
  2.2 17.1 %collective-permute-start.39 = (bf16[2,4,32,128]{3,2,1,0:T(8,128)(2,1)}, bf16[2,4,32,128]{3,2,1,0:T(8,128)(2,1)}, u32[]{:S(2)}, u32[]{:S(2)}) collective-permute-start(bf16[2,4,32,128]{3,2,1,0:T(8,128)(2,1)} %get-tuple-element.312), channel_id=1, source_target_pairs={{0,52},{4,48},{8,60},{12,56},{16,36},{20,32},{24,44},{28,40},{32,2... | collective-permute-start | bytes 196616 | tf_op jit(solution)/shard_map/cond/branch_13_fun/ppermute | solution.py:369
  14.3 5.0 %collective-permute-start.40 = (bf16[2,4,1,32,128]{4,3,2,1,0:T(8,128)(2,1)S(1)}, bf16[2,4,1,32,128]{4,3,2,1,0:T(8,128)(2,1)}, u32[]{:S(2)}, u32[]{:S(2)}) collective-permute-start(bf16[2,4,1,32,128]{4,3,2,1,0:T(8,128)(2,1)S(1)} %get-tuple-element.313), channel_id=1, source_target_pairs={{0,1},{1,2},{2,3},{4,5},{5,6},{6,7},{8,9},{9,10},{10,11},{12,13},{... | collective-permute-start | bytes 196616 | tf_op jit(solution)/shard_map/cond/branch_13_fun/ppermute | solution.py:390
  18.0 5.7 %collective-permute-start.41 = (bf16[2,4,1,32,128]{4,3,2,1,0:T(8,128)(2,1)S(1)}, bf16[2,4,1,32,128]{4,3,2,1,0:T(8,128)(2,1)}, u32[]{:S(2)}, u32[]{:S(2)}) collective-permute-start(bf16[2,4,1,32,128]{4,3,2,1,0:T(8,128)(2,1)S(1)} %get-tuple-element.314), channel_id=1, source_target_pairs={{1,0},{2,1},{3,2},{5,4},{6,5},{7,6},{9,8},{10,9},{11,10},{13,12},{... | collective-permute-start | bytes 196616 | tf_op jit(solution)/shard_map/cond/branch_13_fun/ppermute | solution.py:390
  23.7 9.5 %copy-start = (bf16[1,2,4,32,128]{4,3,2,1,0:T(8,128)(2,1)S(1)}, bf16[1,2,4,32,128]{4,3,2,1,0:T(8,128)(2,1)}, u32[]{:S(2)}) copy-start(bf16[1,2,4,32,128]{4,3,2,1,0:T(8,128)(2,1)} %param.58) | copy-start | bytes 196612
  23.7 9.3 %collective-permute-start.55 = (bf16[2,4,32,128]{3,2,1,0:T(8,128)(2,1)}, bf16[2,4,32,128]{3,2,1,0:T(8,128)(2,1)}, u32[]{:S(2)}, u32[]{:S(2)}) collective-permute-start(bf16[2,4,32,128]{3,2,1,0:T(8,128)(2,1)} %get-tuple-element.384), channel_id=1, source_target_pairs={{0,448},{64,384},{128,320},{192,256},{256,192},{320,128},{384,64},... | collective-permute-start | bytes 196616 | tf_op jit(solution)/shard_map/cond/branch_7_fun/ppermute | solution.py:369
  35.9 4.5 %collective-permute-start.96 = (bf16[14,128,128]{2,1,0:T(8,128)(2,1)S(1)}, bf16[14,128,128]{2,1,0:T(8,128)(2,1)S(1)}, u32[]{:S(2)}, u32[]{:S(2)}) collective-permute-start(bf16[14,128,128]{2,1,0:T(8,128)(2,1)S(1)} %get-tuple-element.459), channel_id=1, source_target_pairs={{0,4},{4,0},{1,5},{5,1},{2,6},{6,2},{3,7},{7,3},{8,12},{12,8},{9,1... | collective-permute-start | bytes 1376264 | tf_op jit(solution)/shard_map/ppermute | solution.py:378
  39.6 29.1 %copy-start.1 = (bf16[3,3,3,128,128]{4,3,2,1,0:T(8,128)(2,1)S(1)}, bf16[3,3,3,128,128]{4,3,2,1,0:T(8,128)(2,1)}, u32[]{:S(2)}) copy-start(bf16[3,3,3,128,128]{4,3,2,1,0:T(8,128)(2,1)} %param.57) | copy-start | bytes 2654212
  41.2 23.4 %all-to-all-start = ((bf16[32,56,128]{2,1,0:T(8,128)(2,1)}), bf16[32,56,128]{2,1,0:T(8,128)(2,1)S(1)}, u32[]{:S(2)}, u32[]{:S(2)}) async-start(bf16[32,56,128]{2,1,0:T(8,128)(2,1)} %bitcast.7), calls=%async_computation | async-start | bytes 917504 | tf_op jit(solution)/shard_map/all_to_all | solution.py:400
  49.1 13.6 %collective-permute-start.77 = (bf16[2,4,32,128]{3,2,1,0:T(8,128)(2,1)S(1)}, bf16[2,4,32,128]{3,2,1,0:T(8,128)(2,1)}, u32[]{:S(2)}, u32[]{:S(2)}) collective-permute-start(bf16[2,4,32,128]{3,2,1,0:T(8,128)(2,1)S(1)} %get-tuple-element.414), channel_id=1, source_target_pairs={{0,448},{64,384},{128,320},{192,256},{256,192},{320,128},{384,64},... | collective-permute-start | bytes 196616 | tf_op jit(solution)/shard_map/cond/branch_7_fun/ppermute | solution.py:369
  53.5 5.0 %collective-permute-start.78 = (bf16[2,2,1,32,128]{4,3,2,1,0:T(8,128)(2,1)S(1)}, bf16[2,2,1,32,128]{4,3,2,1,0:T(8,128)(2,1)}, u32[]{:S(2)}, u32[]{:S(2)}) collective-permute-start(bf16[2,2,1,32,128]{4,3,2,1,0:T(8,128)(2,1)S(1)} %get-tuple-element.415), channel_id=1, source_target_pairs={{0,1},{1,2},{2,3},{4,5},{5,6},{6,7},{8,9},{9,10},{10,11},{12,13},{... | collective-permute-start | bytes 98312 | tf_op jit(solution)/shard_map/cond/branch_7_fun/ppermute | solution.py:390
  57.2 5.5 %collective-permute-start.79 = (bf16[2,2,1,32,128]{4,3,2,1,0:T(8,128)(2,1)S(1)}, bf16[2,2,1,32,128]{4,3,2,1,0:T(8,128)(2,1)}, u32[]{:S(2)}, u32[]{:S(2)}) collective-permute-start(bf16[2,2,1,32,128]{4,3,2,1,0:T(8,128)(2,1)S(1)} %get-tuple-element.416), channel_id=1, source_target_pairs={{1,0},{2,1},{3,2},{5,4},{6,5},{7,6},{9,8},{10,9},{11,10},{13,12},{... | collective-permute-start | bytes 98312 | tf_op jit(solution)/shard_map/cond/branch_7_fun/ppermute | solution.py:390
  65.3 11.1 %all-to-all-start.1 = ((bf16[8,56,128]{2,1,0:T(8,128)(2,1)}), bf16[8,56,128]{2,1,0:T(8,128)(2,1)S(1)}, u32[]{:S(2)}, u32[]{:S(2)}) async-start(bf16[8,56,128]{2,1,0:T(8,128)(2,1)} %spread.2), calls=%async_computation.1 | async-start | bytes 229376 | tf_op jit(solution)/shard_map/all_to_all | solution.py:403
  77.3 21.0 %all-to-all-start.2 = ((bf16[32,56,128]{2,1,0:T(8,128)(2,1)}), bf16[32,56,128]{2,1,0:T(8,128)(2,1)S(1)}, u32[]{:S(2)}, u32[]{:S(2)}) async-start(bf16[32,56,128]{2,1,0:T(8,128)(2,1)} %spread.3), calls=%async_computation.2 | async-start | bytes 917504 | tf_op jit(solution)/shard_map/all_to_all | solution.py:406
  84.9 8.0 %collective-permute-start.93 = (bf16[2,4,32,128]{3,2,1,0:T(8,128)(2,1)}, bf16[2,4,32,128]{3,2,1,0:T(8,128)(2,1)}, u32[]{:S(2)}, u32[]{:S(2)}) collective-permute-start(bf16[2,4,32,128]{3,2,1,0:T(8,128)(2,1)} %param.45), channel_id=1, source_target_pairs={{0,52},{4,48},{8,60},{12,56},{16,36},{20,32},{24,44},{28,40},{32,2... | collective-permute-start | bytes 196616 | tf_op jit(solution)/shard_map/cond/branch_13_fun/ppermute | solution.py:369
  98.3 7.8 %collective-permute-start.97 = (bf16[14,128,128]{2,1,0:T(8,128)(2,1)S(1)}, bf16[14,128,128]{2,1,0:T(8,128)(2,1)S(1)}, u32[]{:S(2)}, u32[]{:S(2)}) collective-permute-start(bf16[14,128,128]{2,1,0:T(8,128)(2,1)S(1)} %bitcast.11), channel_id=1, source_target_pairs={{0,4},{4,0},{1,5},{5,1},{2,6},{6,2},{3,7},{7,3},{8,12},{12,8},{9,1... | collective-permute-start | bytes 1376264 | tf_op jit(solution)/shard_map/ppermute | solution.py:378

commit v4 on v3

--- a/solution.py
+++ b/solution.py
@@ -41,13 +41,18 @@
         load.start()
     for load in loads:
         load.wait()
-    widen(wide, held[...], 0, False)
-    places = slabs * out_frames * rows * width
-    z = jnp.zeros((places, chans), F32)
-    for tap in range(9):
-        if tap % 3 == 0:
-            weights[tap // 3].wait()
-        z = z + jnp.dot(window(wide, tap, rows), kernel[tap], preferred_element_type=F32)
+
+    def widen_frame(number, carry):
+        slab = lax.div(number, frames)
+        at = (pl.ds(slab, 1), pl.ds(number - slab * frames, 1))
+        widen(wide.at[at], held[at], 0, False)
+        return carry
+
+    lax.fori_loop(0, slabs * frames, widen_frame, 0)
+    for load in weights:
+        load.wait()
+    windows = jnp.concatenate([window(wide, tap, rows) for tap in range(9)], axis=1)
+    z = jnp.dot(windows, kernel[...].reshape(-1, chans), preferred_element_type=F32)
     sig = 1.0 / (1.0 + jnp.exp(-z))
     per = rows * width
     y = z * sig
@@ -361,8 +366,24 @@
     )(first, rows, earlier)
 
 
-def by_xor(value, axes, count, offset, beside=None, extra=()):
-    def branch(mask):
+def ring_hops(count):
+    table = 0
+    for mask in range(count):
+        hops = [min((i ^ mask) - i & count - 1, i - (i ^ mask) & count - 1) for i in range(count)]
+        table |= (sum(hops) // count) << (4 * mask)
+    return table
+
+
+def hops_of(mask, table):
+    return jnp.bitwise_and(lax.shift_right_logical(jnp.int32(table), 4 * mask), 15)
+
+
+def masks_of(axes, count):
+    return [(axes, count, mask) for mask in range(count)]
+
+
+def by_xor(value, masks, place, beside=None, extra=()):
+    def branch(axes, count, mask):
         pairs = [(source, source ^ mask) for source in range(count)]
 
         def moved(item, *others):
@@ -371,7 +392,7 @@
 
         return moved
 
-    return lax.switch(offset, [branch(mask) for mask in range(count)], value, *extra)
+    return lax.switch(place, [branch(*entry) for entry in masks], value, *extra)
 
 
 def swap_cores(value):
@@ -383,6 +404,11 @@
     chans = clips.shape[4]
     near = jnp.bitwise_and(partner[0], 2 * nz - 1)
     far = lax.shift_right_logical(partner[0], jnp.int32((2 * nz).bit_length() - 1))
+    near_masks, far_masks = masks_of(("z", "c"), 2 * nz), masks_of("y", ny)
+    far_first = hops_of(far, ring_hops(ny)) > hops_of(lax.shift_right_logical(near, jnp.int32(1)), ring_hops(nz))
+    one_way, other_way = near, 2 * nz + far
+    first_way = jnp.where(far_first, other_way, one_way)
+    second_way = jnp.where(far_first, one_way, other_way)
     up = [(i, i + 1) for i in range(nx - 1)]
     down = [(i + 1, i) for i in range(nx - 1)]
 
@@ -391,20 +417,21 @@
 
     core = lax.axis_index("c").astype(jnp.int32).reshape(1)
     first, last = lax.optimization_barrier((clips[:, :, :1], clips[:, :, rows - 1 :]))
-    cot_here, (low, high) = by_xor(cot_guest[0], ("z", "c"), 2 * nz, near, edges, (first, last))
+    cot_here, (low, high) = by_xor(cot_guest[0], near_masks + far_masks, first_way, edges, (first, last))
+    weights = kernel.reshape(9, 3 * chans, chans)
     cot_here, (y_stay, y_guest, slope) = by_xor(
-        cot_here, "y", ny, far, forward_call, (lengths, low, high, clips, kernel.reshape(9, 3 * chans, chans))
+        cot_here, near_masks + far_masks, second_way, forward_call, (lengths, low, high, clips, weights)
     )
     dz, dz_first, dz_last, other, wide, turned = weight_call(core, low, high, slope, cot_here, clips, cot_stay[0])
     half = joined_call(mine_call(core, wide, turned), swap_cores(other))
     parts = lax.all_to_all(half.reshape(ny * nx, -1, chans), ("y", "x"), 0, 0)
-    guest, (dz_low, dz_high) = by_xor(y_guest, "y", ny, far, edges, (dz_first, dz_last))
+    guest, (dz_low, dz_high) = by_xor(y_guest, far_masks, far, edges, (dz_first, dz_last))
     parts, guest, dz_low, dz_high = lax.optimization_barrier((parts, guest, dz_low, dz_high))
     parts = lax.all_to_all(spread_call(parts, nz), "z", 0, 0)
     slab_grad = backward_call(dz, dz_low, dz_high, kernel.reshape(TAPS, chans, chans))
     parts, slab_grad = lax.optimization_barrier((parts, slab_grad))
     whole = lax.all_to_all(spread_call(parts, ny * nx), ("y", "x"), 0, 0).reshape(half.shape)
-    guest = by_xor(guest, ("z", "c"), 2 * nz, near)
+    guest = by_xor(guest, near_masks, near)
     whole, guest = lax.optimization_barrier((whole, guest))
     theirs = swap_cores(whole)
     weight_grad, guest = half_call(core, whole, scale, guest)

time: 108 us -> 102 us (0.944)
  starting transfers between devices: 64.1 us -> 54.2 us
  waiting for transfers between devices: 25.4 us -> 29.9 us
    ppermute x4, starting transfers between devices: 26 us -> 10.7 us  [moved(): there = lax.ppermute(item, axes, pairs)]
    all_to_all x1, starting transfers between devices: 3.38 us -> 8.23 us  [shards(): parts = lax.all_to_all(spread_call(parts, nz), 'z', 0, 0)]
    all_to_all x1, waiting for transfers between devices: 1.84 us -> 5.81 us  [shards(): parts = lax.all_to_all(half.reshape(ny * nx, -1, chans), ('y', 'x'), 0, 0)]
    all_to_all x1, starting transfers between devices: 7.58 us -> 4.7 us  [shards(): lax.all_to_all(spread_call(parts, ny * nx), ('y', 'x'), 0, 0)]
    ppermute x2, starting transfers between devices: 9.31 us -> 11.8 us  [swap_cores(): return lax.ppermute(value, 'c', [(0, 1), (1, 0)])]
    ppermute x4, waiting for transfers between devices: 3.72 us -> 4.95 us  [moved(): there = lax.ppermute(item, axes, pairs)]
where the time goes in v4:
time: 102 us; the launch traced here: 101 us
  starting transfers between devices  54.2 us (53%)
  waiting for transfers between devices  29.9 us (29%)
  Pallas kernels  14.4 us (14%)
  between operations  1.63 us (2%)
    ppermute x2, starting transfers between devices, swap_cores(): return lax.ppermute(value, 'c', [(0, 1), (1, 0)])  11.8 us
    ppermute x4, starting transfers between devices, moved(): there = lax.ppermute(item, axes, pairs)  10.7 us
    ppermute x4, starting transfers between devices, edges(): return (lax.ppermute(last, 'x', up), lax.ppermute(first, 'x', down))  10 us
    all_to_all x1, starting transfers between devices, shards(): parts = lax.all_to_all(half.reshape(ny * nx, -1, chans), ('y', 'x'), 0, 0)  8.79 us
    all_to_all x1, starting transfers between devices, shards(): parts = lax.all_to_all(spread_call(parts, nz), 'z', 0, 0)  8.23 us
    ppermute x4, waiting for transfers between devices, edges(): return (lax.ppermute(last, 'x', up), lax.ppermute(first, 'x', down))  7.79 us
    all_to_all x1, waiting for transfers between devices, shards(): parts = lax.all_to_all(half.reshape(ny * nx, -1, chans), ('y', 'x'), 0, 0)  5.81 us
    all_to_all x1, waiting for transfers between devices, shards(): lax.all_to_all(spread_call(parts, ny * nx), ('y', 'x'), 0, 0)  5.51 us
  transfers between devices with their start and end apart: 13, of which 7 were waited for; matrix products, arithmetic and copies ran while one was open for 0% of the time, Pallas kernels for 8%

profile of v4, /device:TPU:1, one launch (start us, length us, event | category | flops | bytes accessed | tf_op | source)
XLA Modules:
  0.0 101.2 jit_solution(4255264722721498359)
XLA Ops:
  2.2 15.5 %conditional.4 = (bf16[2,4,32,128]{3,2,1,0:T(8,128)(2,1)}, bf16[2,4,1,32,128]{4,3,2,1,0:T(8,128)(2,1)}, bf16[2,4,1,32,128]{4,3,2,1,0:T(8,128)(2,1)}) conditional(s32[]{:T(128)} %clamp.16, (bf16[2,4,32,128]{3,2,1,0:T(8,128)(2,1)}, bf16[2,4,1,32,128]{4,3,2,1,0:T(8,128)(2,1)S(1)}, ...), branch_computations={%region_0.1_spmd, %region_1.2_spmd, %region_2.3_spmd, %region_3.4_... | conditional | bytes 786576 | solution.py:395
  2.2 6.6 %collective-permute-start.12 = (bf16[2,4,32,128]{3,2,1,0:T(8,128)(2,1)}, bf16[2,4,32,128]{3,2,1,0:T(8,128)(2,1)}, u32[]{:S(2)}, u32[]{:S(2)}) collective-permute-start(bf16[2,4,32,128]{3,2,1,0:T(8,128)(2,1)} %get-tuple-element.525), channel_id=1, source_target_pairs={{0,16},{4,20},{8,24},{12,28},{16,0},{20,4},{24,8},{28,12},{32,48},... | collective-permute-start | bytes 196616 | tf_op jit(solution)/shard_map/cond/branch_4_fun/ppermute | solution.py:390
  8.9 3.7 %collective-permute-start.13 = (bf16[2,4,1,32,128]{4,3,2,1,0:T(8,128)(2,1)S(1)}, bf16[2,4,1,32,128]{4,3,2,1,0:T(8,128)(2,1)}, u32[]{:S(2)}, u32[]{:S(2)}) collective-permute-start(bf16[2,4,1,32,128]{4,3,2,1,0:T(8,128)(2,1)S(1)} %get-tuple-element.526), channel_id=1, source_target_pairs={{0,1},{1,2},{2,3},{4,5},{5,6},{6,7},{8,9},{9,10},{10,11},{12,13},{... | collective-permute-start | bytes 196616 | tf_op jit(solution)/shard_map/cond/branch_4_fun/ppermute | solution.py:416
  13.9 3.8 %collective-permute-done.14 = bf16[2,4,1,32,128]{4,3,2,1,0:T(8,128)(2,1)} collective-permute-done((bf16[2,4,1,32,128]{4,3,2,1,0:T(8,128)(2,1)S(1)}, bf16[2,4,1,32,128]{4,3,2,1,0:T(8,128)(2,1)}, u32[]{:S(2)}, u32[]{:S(2)}) %collective-permute-start.14) | collective-permute-done | bytes 65568 | tf_op jit(solution)/shard_map/cond/branch_4_fun/ppermute | solution.py:416
  17.7 5.2 %conditional.5 = (bf16[2,4,32,128]{3,2,1,0:T(8,128)(2,1)}, bf16[2,4,32,128]{3,2,1,0:T(8,128)(2,1)}, bf16[2,4,32,128]{3,2,1,0:T(8,128)(2,1)S(1)}, f32[512,128]{1,0:T(8,128)S(1)}) conditional(s32[]{:T(128)} %clamp.15, (bf16[2,4,32,128]{3,2,1,0:T(8,128)(2,1)}, s32[2]{0:T(128)}, bf16[2,4,1,32,128]{4,3,2,1,0:T(8,128)(2,1)}, ...), branch_computations={%region_24.25_spmd, %region_25.26_spmd, %region_26.27_spmd, %regio... | conditional | bytes 262216 | solution.py:395
  17.7 1.5 %collective-permute-start.88 = (bf16[2,4,32,128]{3,2,1,0:T(8,128)(2,1)}, bf16[2,4,32,128]{3,2,1,0:T(8,128)(2,1)}, u32[]{:S(2)}, u32[]{:S(2)}) collective-permute-start(bf16[2,4,32,128]{3,2,1,0:T(8,128)(2,1)} %get-tuple-element.729), channel_id=1, source_target_pairs={{0,0},{64,64},{128,128},{192,192},{256,256},{320,320},{384,384},{4... | collective-permute-start | bytes 196616 | tf_op jit(solution)/shard_map/cond/branch_16_fun/ppermute | solution.py:390
  19.2 3.7 %forward.40 = (bf16[2,4,32,128]{3,2,1,0:T(8,128)(2,1)}, bf16[2,4,32,128]{3,2,1,0:T(8,128)(2,1)S(1)}, f32[512,128]{1,0:T(8,128)S(1)}) custom-call(s32[2]{0:T(128)} %get-tuple-element.730.lengths, bf16[2,4,1,32,128]{4,3,2,1,0:T(8,128)(2,1)} %get-tuple-element.731.low, bf16[2,4,1,32,128]{4,3,2,1,0:T(8,128)(2,1)} %get-tuple-element.732.high, ...), custom_call_target="tpu_custom_call" | custom-call | tf_op jit(solution)/shard_map/cond/branch_16_fun/forward/pallas_call | solution.py:199
  23.0 2.6 %weights.1 = (bf16[2,2,4,32,128]{4,3,2,1,0:T(8,128)(2,1)S(1)}, bf16[2,2,1,32,128]{4,3,2,1,0:T(8,128)(2,1)S(1)}, bf16[2,2,1,32,128]{4,3,2,1,0:T(8,128)(2,1)S(1)},...) custom-call(s32[1]{0:T(128)} %bitcast.6.core.first, ...), custom_call_target="tpu_custom_call" | custom-call | tf_op jit(solution)/shard_map/weights/pallas_call | solution.py:224
  25.6 4.6 %collective-permute-start.136 = (bf16[14,128,128]{2,1,0:T(8,128)(2,1)S(1)}, bf16[14,128,128]{2,1,0:T(8,128)(2,1)S(1)}, u32[]{:S(2)}, u32[]{:S(2)}) collective-permute-start(bf16[14,128,128]{2,1,0:T(8,128)(2,1)S(1)} %get-tuple-element.867), channel_id=1, source_target_pairs={{0,4},{4,0},{1,5},{5,1},{2,6},{6,2},{3,7},{7,3},{8,12},{12,8},{9,1... | collective-permute-start | bytes 1376264 | tf_op jit(solution)/shard_map/ppermute | solution.py:399
  32.2 8.8 %all-to-all-start = ((bf16[32,56,128]{2,1,0:T(8,128)(2,1)}), bf16[32,56,128]{2,1,0:T(8,128)(2,1)S(1)}, u32[]{:S(2)}, u32[]{:S(2)}) async-start(bf16[32,56,128]{2,1,0:T(8,128)(2,1)} %bitcast.8), calls=%async_computation | async-start | bytes 917504 | tf_op jit(solution)/shard_map/all_to_all | solution.py:427
  41.0 9.7 %conditional.6 = (bf16[2,4,32,128]{3,2,1,0:T(8,128)(2,1)}, bf16[2,2,1,32,128]{4,3,2,1,0:T(8,128)(2,1)}, bf16[2,2,1,32,128]{4,3,2,1,0:T(8,128)(2,1)}) conditional(s32[]{:T(128)} %bitcast.9, (bf16[2,4,32,128]{3,2,1,0:T(8,128)(2,1)S(1)}, bf16[2,2,1,32,128]{4,3,2,1,0:T(8,128)(2,1)S(1)}, ...), branch_computations={%region_48.49_spmd, %region_49.50_spmd, %region_50.51_spmd, %regio... | conditional | bytes 524432 | solution.py:395
  41.6 3.7 %collective-permute-start.97 = (bf16[2,2,1,32,128]{4,3,2,1,0:T(8,128)(2,1)S(1)}, bf16[2,2,1,32,128]{4,3,2,1,0:T(8,128)(2,1)}, u32[]{:S(2)}, u32[]{:S(2)}) collective-permute-start(bf16[2,2,1,32,128]{4,3,2,1,0:T(8,128)(2,1)S(1)} %get-tuple-element.802), channel_id=1, source_target_pairs={{0,1},{1,2},{2,3},{4,5},{5,6},{6,7},{8,9},{9,10},{10,11},{12,13},{... | collective-permute-start | bytes 98312 | tf_op jit(solution)/shard_map/cond/branch_0_fun/ppermute | solution.py:416
  46.7 4.0 %collective-permute-done.98 = bf16[2,2,1,32,128]{4,3,2,1,0:T(8,128)(2,1)} collective-permute-done((bf16[2,2,1,32,128]{4,3,2,1,0:T(8,128)(2,1)S(1)}, bf16[2,2,1,32,128]{4,3,2,1,0:T(8,128)(2,1)}, u32[]{:S(2)}, u32[]{:S(2)}) %collective-permute-start.98) | collective-permute-done | bytes 32800 | tf_op jit(solution)/shard_map/cond/branch_0_fun/ppermute | solution.py:416
  50.7 5.8 %all-to-all-done.parts = bf16[32,56,128]{2,1,0:T(8,128)(2,1)S(1)} async-done(((bf16[32,56,128]{2,1,0:T(8,128)(2,1)}), bf16[32,56,128]{2,1,0:T(8,128)(2,1)S(1)}, u32[]{:S(2)}, u32[]{:S(2)}) %all-to-all-start) | async-done | bytes 458784 | tf_op jit(solution)/shard_map/all_to_all | solution.py:427
  57.2 8.2 %all-to-all-start.1 = ((bf16[8,56,128]{2,1,0:T(8,128)(2,1)}), bf16[8,56,128]{2,1,0:T(8,128)(2,1)S(1)}, u32[]{:S(2)}, u32[]{:S(2)}) async-start(bf16[8,56,128]{2,1,0:T(8,128)(2,1)} %spread.2), calls=%async_computation.1 | async-start | bytes 229376 | tf_op jit(solution)/shard_map/all_to_all | solution.py:430
  65.5 2.6 %backward.1 = bf16[2,4,4,32,128]{4,3,2,1,0:T(8,128)(2,1)} custom-call(bf16[2,2,4,32,128]{4,3,2,1,0:T(8,128)(2,1)S(1)} %get-tuple-element.875.dz, bf16[2,2,1,32,128]{4,3,2,1,0:T(8,128)(2,1)} %get-tuple-element.876.low, bf16[2,2,1,32,128]{4,3,2,1,0:T(8,128)(2,1)} %get-tuple-element.877.high, bf16[27,128,128]{2,1,0:T(8,128)(2,1)S(1)} %bitcast.40), custom_call_target="tpu_custom_call" | custom-call | tf_op jit(solution)/shard_map/backward/pallas_call | solution.py:291
  68.0 5.3 %all-to-all-done.1.parts = bf16[8,56,128]{2,1,0:T(8,128)(2,1)S(1)} async-done(((bf16[8,56,128]{2,1,0:T(8,128)(2,1)}), bf16[8,56,128]{2,1,0:T(8,128)(2,1)S(1)}, u32[]{:S(2)}, u32[]{:S(2)}) %all-to-all-start.1) | async-done | bytes 114720 | tf_op jit(solution)/shard_map/all_to_all | solution.py:430
  74.1 4.7 %all-to-all-start.2 = ((bf16[32,56,128]{2,1,0:T(8,128)(2,1)}), bf16[32,56,128]{2,1,0:T(8,128)(2,1)S(1)}, u32[]{:S(2)}, u32[]{:S(2)}) async-start(bf16[32,56,128]{2,1,0:T(8,128)(2,1)} %spread.3), calls=%async_computation.2 | async-start | bytes 917504 | tf_op jit(solution)/shard_map/all_to_all | solution.py:433
  78.8 6.9 %conditional.7 = (bf16[2,4,32,128]{3,2,1,0:T(8,128)(2,1)}) conditional(s32[]{:T(128)} %clamp.19, bf16[2,4,32,128]{3,2,1,0:T(8,128)(2,1)} %get-tuple-element.879, bf16[2,4,32,128]{3,2,1,0:T(8,128)(2,1)} %get-tuple-element.879, bf16[2,4,32,128]{3,2,1,0:T(8,128)(2,1)} %get-tuple-element.879, ...), branch_computations={%region_56.57_spmd, %region_57.58_spmd, %region_58.59_spmd, %regio... | conditional | bytes 262192 | solution.py:395
  78.9 1.9 %collective-permute-start.124 = (bf16[2,4,32,128]{3,2,1,0:T(8,128)(2,1)}, bf16[2,4,32,128]{3,2,1,0:T(8,128)(2,1)}, u32[]{:S(2)}, u32[]{:S(2)}) collective-permute-start(bf16[2,4,32,128]{3,2,1,0:T(8,128)(2,1)} %param.60), channel_id=1, source_target_pairs={{0,16},{4,20},{8,24},{12,28},{16,0},{20,4},{24,8},{28,12},{32,48},... | collective-permute-start | bytes 196616 | tf_op jit(solution)/shard_map/cond/branch_4_fun/ppermute | solution.py:390
  80.8 4.9 %collective-permute-done.124 = bf16[2,4,32,128]{3,2,1,0:T(8,128)(2,1)} collective-permute-done((bf16[2,4,32,128]{3,2,1,0:T(8,128)(2,1)}, bf16[2,4,32,128]{3,2,1,0:T(8,128)(2,1)}, u32[]{:S(2)}, u32[]{:S(2)}) %collective-permute-start.124) | collective-permute-done | bytes 65568 | tf_op jit(solution)/shard_map/cond/branch_4_fun/ppermute | solution.py:390
  85.7 5.5 %all-to-all-done.2 = bf16[32,56,128]{2,1,0:T(8,128)(2,1)S(1)} async-done(((bf16[32,56,128]{2,1,0:T(8,128)(2,1)}), bf16[32,56,128]{2,1,0:T(8,128)(2,1)S(1)}, u32[]{:S(2)}, u32[]{:S(2)}) %all-to-all-start.2) | async-done | bytes 458784 | tf_op jit(solution)/shard_map/all_to_all | solution.py:433
  91.2 7.2 %collective-permute-start.137 = (bf16[14,128,128]{2,1,0:T(8,128)(2,1)S(1)}, bf16[14,128,128]{2,1,0:T(8,128)(2,1)S(1)}, u32[]{:S(2)}, u32[]{:S(2)}) collective-permute-start(bf16[14,128,128]{2,1,0:T(8,128)(2,1)S(1)} %bitcast.13), channel_id=1, source_target_pairs={{0,4},{4,0},{1,5},{5,1},{2,6},{6,2},{3,7},{7,3},{8,12},{12,8},{9,1... | collective-permute-start | bytes 1376264 | tf_op jit(solution)/shard_map/ppermute | solution.py:399
  98.5 1.5 %own.1 = (f32[27,128,128]{2,1,0:T(8,128)}, bf16[1,2,4,32,128]{4,3,2,1,0:T(8,128)(2,1)}) custom-call(s32[1]{0:T(128)} %bitcast.6.core.first, bf16[14,128,128]{2,1,0:T(8,128)(2,1)S(1)} %bitcast.14, bf16[2,4,32,128]{3,2,1,0:T(8,128)(2,1)} %get-tuple-element.1079.passed), custom_call_target="tpu_custom_call" | custom-call | tf_op jit(solution)/shard_map/own/pallas_call | solution.py:334
  (20 shorter events, 8.6 us)
Async XLA Ops:
  2.2 11.7 %collective-permute-start.12 = (bf16[2,4,32,128]{3,2,1,0:T(8,128)(2,1)}, bf16[2,4,32,128]{3,2,1,0:T(8,128)(2,1)}, u32[]{:S(2)}, u32[]{:S(2)}) collective-permute-start(bf16[2,4,32,128]{3,2,1,0:T(8,128)(2,1)} %get-tuple-element.525), channel_id=1, source_target_pairs={{0,16},{4,20},{8,24},{12,28},{16,0},{20,4},{24,8},{28,12},{32,48},... | collective-permute-start | bytes 196616 | tf_op jit(solution)/shard_map/cond/branch_4_fun/ppermute | solution.py:390
  8.9 5.0 %collective-permute-start.13 = (bf16[2,4,1,32,128]{4,3,2,1,0:T(8,128)(2,1)S(1)}, bf16[2,4,1,32,128]{4,3,2,1,0:T(8,128)(2,1)}, u32[]{:S(2)}, u32[]{:S(2)}) collective-permute-start(bf16[2,4,1,32,128]{4,3,2,1,0:T(8,128)(2,1)S(1)} %get-tuple-element.526), channel_id=1, source_target_pairs={{0,1},{1,2},{2,3},{4,5},{5,6},{6,7},{8,9},{9,10},{10,11},{12,13},{... | collective-permute-start | bytes 196616 | tf_op jit(solution)/shard_map/cond/branch_4_fun/ppermute | solution.py:416
  12.6 5.1 %collective-permute-start.14 = (bf16[2,4,1,32,128]{4,3,2,1,0:T(8,128)(2,1)S(1)}, bf16[2,4,1,32,128]{4,3,2,1,0:T(8,128)(2,1)}, u32[]{:S(2)}, u32[]{:S(2)}) collective-permute-start(bf16[2,4,1,32,128]{4,3,2,1,0:T(8,128)(2,1)S(1)} %get-tuple-element.527), channel_id=1, source_target_pairs={{1,0},{2,1},{3,2},{5,4},{6,5},{7,6},{9,8},{10,9},{11,10},{13,12},{... | collective-permute-start | bytes 196616 | tf_op jit(solution)/shard_map/cond/branch_4_fun/ppermute | solution.py:416
  17.7 5.3 %copy-start = (bf16[1,2,4,32,128]{4,3,2,1,0:T(8,128)(2,1)S(1)}, bf16[1,2,4,32,128]{4,3,2,1,0:T(8,128)(2,1)}, u32[]{:S(2)}) copy-start(bf16[1,2,4,32,128]{4,3,2,1,0:T(8,128)(2,1)} %param.82) | copy-start | bytes 196612
  17.7 5.2 %collective-permute-start.88 = (bf16[2,4,32,128]{3,2,1,0:T(8,128)(2,1)}, bf16[2,4,32,128]{3,2,1,0:T(8,128)(2,1)}, u32[]{:S(2)}, u32[]{:S(2)}) collective-permute-start(bf16[2,4,32,128]{3,2,1,0:T(8,128)(2,1)} %get-tuple-element.729), channel_id=1, source_target_pairs={{0,0},{64,64},{128,128},{192,192},{256,256},{320,320},{384,384},{4... | collective-permute-start | bytes 196616 | tf_op jit(solution)/shard_map/cond/branch_16_fun/ppermute | solution.py:390
  25.6 5.7 %collective-permute-start.136 = (bf16[14,128,128]{2,1,0:T(8,128)(2,1)S(1)}, bf16[14,128,128]{2,1,0:T(8,128)(2,1)S(1)}, u32[]{:S(2)}, u32[]{:S(2)}) collective-permute-start(bf16[14,128,128]{2,1,0:T(8,128)(2,1)S(1)} %get-tuple-element.867), channel_id=1, source_target_pairs={{0,4},{4,0},{1,5},{5,1},{2,6},{6,2},{3,7},{7,3},{8,12},{12,8},{9,1... | collective-permute-start | bytes 1376264 | tf_op jit(solution)/shard_map/ppermute | solution.py:399
  30.8 34.6 %copy-start.1 = (bf16[3,3,3,128,128]{4,3,2,1,0:T(8,128)(2,1)S(1)}, bf16[3,3,3,128,128]{4,3,2,1,0:T(8,128)(2,1)}, u32[]{:S(2)}) copy-start(bf16[3,3,3,128,128]{4,3,2,1,0:T(8,128)(2,1)} %param.81) | copy-start | bytes 2654212
  32.2 24.3 %all-to-all-start = ((bf16[32,56,128]{2,1,0:T(8,128)(2,1)}), bf16[32,56,128]{2,1,0:T(8,128)(2,1)S(1)}, u32[]{:S(2)}, u32[]{:S(2)}) async-start(bf16[32,56,128]{2,1,0:T(8,128)(2,1)} %bitcast.8), calls=%async_computation | async-start | bytes 917504 | tf_op jit(solution)/shard_map/all_to_all | solution.py:427
  41.0 9.6 %collective-permute-start.96 = (bf16[2,4,32,128]{3,2,1,0:T(8,128)(2,1)S(1)}, bf16[2,4,32,128]{3,2,1,0:T(8,128)(2,1)}, u32[]{:S(2)}, u32[]{:S(2)}) collective-permute-start(bf16[2,4,32,128]{3,2,1,0:T(8,128)(2,1)S(1)} %get-tuple-element.801), channel_id=1, source_target_pairs={{0,0},{64,64},{128,128},{192,192},{256,256},{320,320},{384,384},{4... | collective-permute-start | bytes 196616 | tf_op jit(solution)/shard_map/cond/branch_0_fun/ppermute | solution.py:390
  41.6 5.0 %collective-permute-start.97 = (bf16[2,2,1,32,128]{4,3,2,1,0:T(8,128)(2,1)S(1)}, bf16[2,2,1,32,128]{4,3,2,1,0:T(8,128)(2,1)}, u32[]{:S(2)}, u32[]{:S(2)}) collective-permute-start(bf16[2,2,1,32,128]{4,3,2,1,0:T(8,128)(2,1)S(1)} %get-tuple-element.802), channel_id=1, source_target_pairs={{0,1},{1,2},{2,3},{4,5},{5,6},{6,7},{8,9},{9,10},{10,11},{12,13},{... | collective-permute-start | bytes 98312 | tf_op jit(solution)/shard_map/cond/branch_0_fun/ppermute | solution.py:416
  45.4 5.3 %collective-permute-start.98 = (bf16[2,2,1,32,128]{4,3,2,1,0:T(8,128)(2,1)S(1)}, bf16[2,2,1,32,128]{4,3,2,1,0:T(8,128)(2,1)}, u32[]{:S(2)}, u32[]{:S(2)}) collective-permute-start(bf16[2,2,1,32,128]{4,3,2,1,0:T(8,128)(2,1)S(1)} %get-tuple-element.803), channel_id=1, source_target_pairs={{1,0},{2,1},{3,2},{5,4},{6,5},{7,6},{9,8},{10,9},{11,10},{13,12},{... | collective-permute-start | bytes 98312 | tf_op jit(solution)/shard_map/cond/branch_0_fun/ppermute | solution.py:416
  57.2 16.1 %all-to-all-start.1 = ((bf16[8,56,128]{2,1,0:T(8,128)(2,1)}), bf16[8,56,128]{2,1,0:T(8,128)(2,1)S(1)}, u32[]{:S(2)}, u32[]{:S(2)}) async-start(bf16[8,56,128]{2,1,0:T(8,128)(2,1)} %spread.2), calls=%async_computation.1 | async-start | bytes 229376 | tf_op jit(solution)/shard_map/all_to_all | solution.py:430
  74.1 17.1 %all-to-all-start.2 = ((bf16[32,56,128]{2,1,0:T(8,128)(2,1)}), bf16[32,56,128]{2,1,0:T(8,128)(2,1)S(1)}, u32[]{:S(2)}, u32[]{:S(2)}) async-start(bf16[32,56,128]{2,1,0:T(8,128)(2,1)} %spread.3), calls=%async_computation.2 | async-start | bytes 917504 | tf_op jit(solution)/shard_map/all_to_all | solution.py:433
  78.9 6.9 %collective-permute-start.124 = (bf16[2,4,32,128]{3,2,1,0:T(8,128)(2,1)}, bf16[2,4,32,128]{3,2,1,0:T(8,128)(2,1)}, u32[]{:S(2)}, u32[]{:S(2)}) collective-permute-start(bf16[2,4,32,128]{3,2,1,0:T(8,128)(2,1)} %param.60), channel_id=1, source_target_pairs={{0,16},{4,20},{8,24},{12,28},{16,0},{20,4},{24,8},{28,12},{32,48},... | collective-permute-start | bytes 196616 | tf_op jit(solution)/shard_map/cond/branch_4_fun/ppermute | solution.py:390
  91.2 8.8 %collective-permute-start.137 = (bf16[14,128,128]{2,1,0:T(8,128)(2,1)S(1)}, bf16[14,128,128]{2,1,0:T(8,128)(2,1)S(1)}, u32[]{:S(2)}, u32[]{:S(2)}) collective-permute-start(bf16[14,128,128]{2,1,0:T(8,128)(2,1)S(1)} %bitcast.13), channel_id=1, source_target_pairs={{0,4},{4,0},{1,5},{5,1},{2,6},{6,2},{3,7},{7,3},{8,12},{12,8},{9,1... | collective-permute-start | bytes 1376264 | tf_op jit(solution)/shard_map/ppermute | solution.py:399

commit v5 on v4

--- a/solution.py
+++ b/solution.py
@@ -304,7 +304,7 @@
     copies = []
     for number, (low, high) in enumerate(pieces):
         buffer[low:high] = rows[low:high].astype(F32) * scale
-        place = pl.ds(first[0] * HALF_TAPS + low, high - low)
+        place = pl.ds(jnp.minimum(first[0] * HALF_TAPS + low, TAPS - (high - low)), high - low)
         copies.append(pltpu.make_async_copy(buffer.at[low:high], out.at[place], sems.at[number]))
         if number < 2:
             copies[-1].start()
@@ -425,14 +425,14 @@
     dz, dz_first, dz_last, other, wide, turned = weight_call(core, low, high, slope, cot_here, clips, cot_stay[0])
     half = joined_call(mine_call(core, wide, turned), swap_cores(other))
     parts = lax.all_to_all(half.reshape(ny * nx, -1, chans), ("y", "x"), 0, 0)
-    guest, (dz_low, dz_high) = by_xor(y_guest, far_masks, far, edges, (dz_first, dz_last))
-    parts, guest, dz_low, dz_high = lax.optimization_barrier((parts, guest, dz_low, dz_high))
+    guest = by_xor(y_guest, far_masks, far)
+    parts, guest = lax.optimization_barrier((parts, guest))
     parts = lax.all_to_all(spread_call(parts, nz), "z", 0, 0)
+    parts, dz_first, dz_last = lax.optimization_barrier((parts, dz_first, dz_last))
+    whole = lax.all_to_all(spread_call(parts, ny * nx), ("y", "x"), 0, 0).reshape(half.shape)
+    guest, (dz_low, dz_high) = by_xor(guest, near_masks, near, edges, (dz_first, dz_last))
     slab_grad = backward_call(dz, dz_low, dz_high, kernel.reshape(TAPS, chans, chans))
-    parts, slab_grad = lax.optimization_barrier((parts, slab_grad))
-    whole = lax.all_to_all(spread_call(parts, ny * nx), ("y", "x"), 0, 0).reshape(half.shape)
-    guest = by_xor(guest, near_masks, near)
-    whole, guest = lax.optimization_barrier((whole, guest))
+    whole, guest, slab_grad = lax.optimization_barrier((whole, guest, slab_grad))
     theirs = swap_cores(whole)
     weight_grad, guest = half_call(core, whole, scale, guest)
     weight_grad = rest_call(1 - core, theirs, scale, weight_grad).reshape(kernel.shape)

time: 102 us -> 110 us (1.078)
  waiting for transfers between devices: 29.9 us -> 18.1 us
  blocking collectives: 0 us -> 11 us
  starting transfers between devices: 54.2 us -> 62.6 us
    ppermute x4, starting transfers between devices: 10.7 us -> 29.5 us  [moved(): there = lax.ppermute(item, axes, pairs)]
    all_to_all x0 -> x1, blocking collectives: none -> 11 us  [shards(): parts = lax.all_to_all(spread_call(parts, nz), 'z', 0, 0)]
    all_to_all x1 -> x0, starting transfers between devices: 8.23 us -> none  [shards(): parts = lax.all_to_all(spread_call(parts, nz), 'z', 0, 0)]
    all_to_all x1, waiting for transfers between devices: 5.51 us -> 0.01 us  [shards(): lax.all_to_all(spread_call(parts, ny * nx), ('y', 'x'), 0, 0)]
    all_to_all x1 -> x0, waiting for transfers between devices: 5.28 us -> none  [shards(): parts = lax.all_to_all(spread_call(parts, nz), 'z', 0, 0)]
    ppermute x2, starting transfers between devices: 11.8 us -> 6.87 us  [swap_cores(): return lax.ppermute(value, 'c', [(0, 1), (1, 0)])]
    all_to_all x1, waiting for transfers between devices: 5.81 us -> 1.5 us  [shards(): parts = lax.all_to_all(half.reshape(ny * nx, -1, chans), ('y', 'x'), 0, 0)]
    ppermute x4, waiting for transfers between devices: 4.95 us -> 8.07 us  [moved(): there = lax.ppermute(item, axes, pairs)]
  transfers between devices with their start and end apart: 13 -> 12, of which waited for: 7 -> 5; matrix products, arithmetic and copies ran while one was open for 0% -> 0% of each run, Pallas kernels for 8% -> 8%
where the time goes in v5:
time: 110 us; the launch traced here: 108 us
  starting transfers between devices  62.6 us (57%)
  waiting for transfers between devices  18.1 us (16%)
  Pallas kernels  13.9 us (13%)
  blocking collectives  11 us (10%)
  between operations  1.63 us (1%)
    ppermute x4, starting transfers between devices, moved(): there = lax.ppermute(item, axes, pairs)  29.5 us
    all_to_all x1, blocking collectives, shards(): parts = lax.all_to_all(spread_call(parts, nz), 'z', 0, 0)  11 us
    ppermute x4, starting transfers between devices, edges(): return (lax.ppermute(last, 'x', up), lax.ppermute(first, 'x', down))  10.3 us
    all_to_all x1, starting transfers between devices, shards(): parts = lax.all_to_all(half.reshape(ny * nx, -1, chans), ('y', 'x'), 0, 0)  8.67 us
    ppermute x4, waiting for transfers between devices, moved(): there = lax.ppermute(item, axes, pairs)  8.07 us
    ppermute x4, waiting for transfers between devices, edges(): return (lax.ppermute(last, 'x', up), lax.ppermute(first, 'x', down))  8.04 us
    all_to_all x1, starting transfers between devices, shards(): lax.all_to_all(spread_call(parts, ny * nx), ('y', 'x'), 0, 0)  7.3 us
    ppermute x2, starting transfers between devices, swap_cores(): return lax.ppermute(value, 'c', [(0, 1), (1, 0)])  6.87 us
  transfers between devices with their start and end apart: 12, of which 5 were waited for; matrix products, arithmetic and copies ran while one was open for 0% of the time, Pallas kernels for 8%

profile of v5, /device:TPU:1, one launch (start us, length us, event | category | flops | bytes accessed | tf_op | source)
XLA Modules:
  0.0 108.4 jit_solution(2535988563836223142)
XLA Ops:
  2.2 21.5 %conditional.4 = (bf16[2,4,32,128]{3,2,1,0:T(8,128)(2,1)}, bf16[2,4,1,32,128]{4,3,2,1,0:T(8,128)(2,1)}, bf16[2,4,1,32,128]{4,3,2,1,0:T(8,128)(2,1)}) conditional(s32[]{:T(128)} %clamp.16, (bf16[2,4,32,128]{3,2,1,0:T(8,128)(2,1)}, bf16[2,4,1,32,128]{4,3,2,1,0:T(8,128)(2,1)S(1)}, ...), branch_computations={%region_0.1_spmd, %region_1.2_spmd, %region_2.3_spmd, %region_3.4_... | conditional | bytes 786576 | solution.py:395
  2.2 12.0 %collective-permute-start.33 = (bf16[2,4,32,128]{3,2,1,0:T(8,128)(2,1)}, bf16[2,4,32,128]{3,2,1,0:T(8,128)(2,1)}, u32[]{:S(2)}, u32[]{:S(2)}) collective-permute-start(bf16[2,4,32,128]{3,2,1,0:T(8,128)(2,1)} %get-tuple-element.578), channel_id=1, source_target_pairs={{0,44},{4,40},{8,36},{12,32},{16,60},{20,56},{24,52},{28,48},{32,1... | collective-permute-start | bytes 196616 | tf_op jit(solution)/shard_map/cond/branch_11_fun/ppermute | solution.py:390
  14.3 3.7 %collective-permute-start.34 = (bf16[2,4,1,32,128]{4,3,2,1,0:T(8,128)(2,1)S(1)}, bf16[2,4,1,32,128]{4,3,2,1,0:T(8,128)(2,1)}, u32[]{:S(2)}, u32[]{:S(2)}) collective-permute-start(bf16[2,4,1,32,128]{4,3,2,1,0:T(8,128)(2,1)S(1)} %get-tuple-element.579), channel_id=1, source_target_pairs={{0,1},{1,2},{2,3},{4,5},{5,6},{6,7},{8,9},{9,10},{10,11},{12,13},{... | collective-permute-start | bytes 196616 | tf_op jit(solution)/shard_map/cond/branch_11_fun/ppermute | solution.py:416
  18.0 1.3 %collective-permute-start.35 = (bf16[2,4,1,32,128]{4,3,2,1,0:T(8,128)(2,1)S(1)}, bf16[2,4,1,32,128]{4,3,2,1,0:T(8,128)(2,1)}, u32[]{:S(2)}, u32[]{:S(2)}) collective-permute-start(bf16[2,4,1,32,128]{4,3,2,1,0:T(8,128)(2,1)S(1)} %get-tuple-element.580), channel_id=1, source_target_pairs={{1,0},{2,1},{3,2},{5,4},{6,5},{7,6},{9,8},{10,9},{11,10},{13,12},{... | collective-permute-start | bytes 196616 | tf_op jit(solution)/shard_map/cond/branch_11_fun/ppermute | solution.py:416
  19.3 4.3 %collective-permute-done.35 = bf16[2,4,1,32,128]{4,3,2,1,0:T(8,128)(2,1)} collective-permute-done((bf16[2,4,1,32,128]{4,3,2,1,0:T(8,128)(2,1)S(1)}, bf16[2,4,1,32,128]{4,3,2,1,0:T(8,128)(2,1)}, u32[]{:S(2)}, u32[]{:S(2)}) %collective-permute-start.35) | collective-permute-done | bytes 65568 | tf_op jit(solution)/shard_map/cond/branch_11_fun/ppermute | solution.py:416
  23.7 10.5 %conditional.5 = (bf16[2,4,32,128]{3,2,1,0:T(8,128)(2,1)}, bf16[2,4,32,128]{3,2,1,0:T(8,128)(2,1)}, bf16[2,4,32,128]{3,2,1,0:T(8,128)(2,1)S(1)}, f32[512,128]{1,0:T(8,128)S(1)}) conditional(s32[]{:T(128)} %clamp.15, (bf16[2,4,32,128]{3,2,1,0:T(8,128)(2,1)}, s32[2]{0:T(128)}, bf16[2,4,1,32,128]{4,3,2,1,0:T(8,128)(2,1)}, ...), branch_computations={%region_24.25_spmd, %region_25.26_spmd, %region_26.27_spmd, %regio... | conditional | bytes 262216 | solution.py:395
  23.7 6.8 %collective-permute-start.93 = (bf16[2,4,32,128]{3,2,1,0:T(8,128)(2,1)}, bf16[2,4,32,128]{3,2,1,0:T(8,128)(2,1)}, u32[]{:S(2)}, u32[]{:S(2)}) collective-permute-start(bf16[2,4,32,128]{3,2,1,0:T(8,128)(2,1)} %get-tuple-element.806), channel_id=1, source_target_pairs={{0,320},{64,256},{128,448},{192,384},{256,64},{320,0},{384,192},{4... | collective-permute-start | bytes 196616 | tf_op jit(solution)/shard_map/cond/branch_21_fun/ppermute | solution.py:390
  30.5 3.7 %forward.45 = (bf16[2,4,32,128]{3,2,1,0:T(8,128)(2,1)}, bf16[2,4,32,128]{3,2,1,0:T(8,128)(2,1)S(1)}, f32[512,128]{1,0:T(8,128)S(1)}) custom-call(s32[2]{0:T(128)} %get-tuple-element.807.lengths, bf16[2,4,1,32,128]{4,3,2,1,0:T(8,128)(2,1)} %get-tuple-element.808.low, bf16[2,4,1,32,128]{4,3,2,1,0:T(8,128)(2,1)} %get-tuple-element.809.high, ...), custom_call_target="tpu_custom_call" | custom-call | tf_op jit(solution)/shard_map/cond/branch_21_fun/forward/pallas_call | solution.py:199
  34.2 2.6 %weights.1 = (bf16[2,2,4,32,128]{4,3,2,1,0:T(8,128)(2,1)S(1)}, bf16[2,2,1,32,128]{4,3,2,1,0:T(8,128)(2,1)S(1)}, bf16[2,2,1,32,128]{4,3,2,1,0:T(8,128)(2,1)S(1)},...) custom-call(s32[1]{0:T(128)} %bitcast.6.core.first, ...), custom_call_target="tpu_custom_call" | custom-call | tf_op jit(solution)/shard_map/weights/pallas_call | solution.py:224
  36.9 3.3 %collective-permute-start.152 = (bf16[14,128,128]{2,1,0:T(8,128)(2,1)S(1)}, bf16[14,128,128]{2,1,0:T(8,128)(2,1)S(1)}, u32[]{:S(2)}, u32[]{:S(2)}) collective-permute-start(bf16[14,128,128]{2,1,0:T(8,128)(2,1)S(1)} %get-tuple-element.923), channel_id=1, source_target_pairs={{0,4},{4,0},{1,5},{5,1},{2,6},{6,2},{3,7},{7,3},{8,12},{12,8},{9,1... | collective-permute-start | bytes 1376264 | tf_op jit(solution)/shard_map/ppermute | solution.py:399
  42.2 8.7 %all-to-all-start = ((bf16[32,56,128]{2,1,0:T(8,128)(2,1)}), bf16[32,56,128]{2,1,0:T(8,128)(2,1)S(1)}, u32[]{:S(2)}, u32[]{:S(2)}) async-start(bf16[32,56,128]{2,1,0:T(8,128)(2,1)} %bitcast.8), calls=%async_computation | async-start | bytes 917504 | tf_op jit(solution)/shard_map/all_to_all | solution.py:427
  50.9 14.3 %conditional.6 = (bf16[2,4,32,128]{3,2,1,0:T(8,128)(2,1)}) conditional(s32[]{:T(128)} %bitcast.9, bf16[2,4,32,128]{3,2,1,0:T(8,128)(2,1)S(1)} %get-tuple-element.924, bf16[2,4,32,128]{3,2,1,0:T(8,128)(2,1)S(1)} %get-tuple-element.924, bf16[2,4,32,128]{3,2,1,0:T(8,128)(2,1)S(1)} %get-tuple-element.924, ...), branch_computations={%region_48.49_spmd, %region_49.50_spmd, %region_50.51_spmd, %regio... | conditional | bytes 262192 | solution.py:395
  50.9 6.2 %collective-permute-start.101 = (bf16[2,4,32,128]{3,2,1,0:T(8,128)(2,1)S(1)}, bf16[2,4,32,128]{3,2,1,0:T(8,128)(2,1)}, u32[]{:S(2)}, u32[]{:S(2)}) collective-permute-start(bf16[2,4,32,128]{3,2,1,0:T(8,128)(2,1)S(1)} %param.53), channel_id=1, source_target_pairs={{0,320},{64,256},{128,448},{192,384},{256,64},{320,0},{384,192},{4... | collective-permute-start | bytes 196616 | tf_op jit(solution)/shard_map/cond/branch_5_fun/ppermute | solution.py:390
  57.1 8.1 %collective-permute-done.101 = bf16[2,4,32,128]{3,2,1,0:T(8,128)(2,1)} collective-permute-done((bf16[2,4,32,128]{3,2,1,0:T(8,128)(2,1)S(1)}, bf16[2,4,32,128]{3,2,1,0:T(8,128)(2,1)}, u32[]{:S(2)}, u32[]{:S(2)}) %collective-permute-start.101) | collective-permute-done | bytes 65568 | tf_op jit(solution)/shard_map/cond/branch_5_fun/ppermute | solution.py:390
  65.2 1.5 %all-to-all-done.parts = bf16[32,56,128]{2,1,0:T(8,128)(2,1)S(1)} async-done(((bf16[32,56,128]{2,1,0:T(8,128)(2,1)}), bf16[32,56,128]{2,1,0:T(8,128)(2,1)S(1)}, u32[]{:S(2)}, u32[]{:S(2)}) %all-to-all-start) | async-done | bytes 458784 | tf_op jit(solution)/shard_map/all_to_all | solution.py:427
  66.9 11.0 %all_to_all.15.parts = bf16[8,56,128]{2,1,0:T(8,128)(2,1)S(1)} all-to-all(bf16[8,56,128]{2,1,0:T(8,128)(2,1)S(1)} %spread.2), channel_id=1, replica_groups=mesh['y'=8,'z'=8,'c'=2,'x'=4] {'z'}, dimensions={0} | all-to-all | bytes 229376 | tf_op jit(solution)/shard_map/all_to_all | solution.py:430
  78.8 7.3 %all-to-all-start.2 = ((bf16[32,56,128]{2,1,0:T(8,128)(2,1)}), bf16[32,56,128]{2,1,0:T(8,128)(2,1)S(1)}, u32[]{:S(2)}, u32[]{:S(2)}) async-start(bf16[32,56,128]{2,1,0:T(8,128)(2,1)} %spread.3), calls=%async_computation.2 | async-start | bytes 917504 | tf_op jit(solution)/shard_map/all_to_all | solution.py:432
  86.1 13.5 %conditional.7 = (bf16[2,4,32,128]{3,2,1,0:T(8,128)(2,1)}, bf16[2,2,1,32,128]{4,3,2,1,0:T(8,128)(2,1)}, bf16[2,2,1,32,128]{4,3,2,1,0:T(8,128)(2,1)}) conditional(s32[]{:T(128)} %clamp.19, (bf16[2,4,32,128]{3,2,1,0:T(8,128)(2,1)}, bf16[2,2,1,32,128]{4,3,2,1,0:T(8,128)(2,1)S(1)}, ...), branch_computations={%region_56.57_spmd, %region_57.58_spmd, %region_58.59_spmd, %regio... | conditional | bytes 524432 | solution.py:395
  86.1 4.5 %collective-permute-start.137 = (bf16[2,4,32,128]{3,2,1,0:T(8,128)(2,1)}, bf16[2,4,32,128]{3,2,1,0:T(8,128)(2,1)}, u32[]{:S(2)}, u32[]{:S(2)}) collective-permute-start(bf16[2,4,32,128]{3,2,1,0:T(8,128)(2,1)} %get-tuple-element.866), channel_id=1, source_target_pairs={{0,44},{4,40},{8,36},{12,32},{16,60},{20,56},{24,52},{28,48},{32,1... | collective-permute-start | bytes 196616 | tf_op jit(solution)/shard_map/cond/branch_11_fun/ppermute | solution.py:390
  90.6 4.0 %collective-permute-start.138 = (bf16[2,2,1,32,128]{4,3,2,1,0:T(8,128)(2,1)S(1)}, bf16[2,2,1,32,128]{4,3,2,1,0:T(8,128)(2,1)}, u32[]{:S(2)}, u32[]{:S(2)}) collective-permute-start(bf16[2,2,1,32,128]{4,3,2,1,0:T(8,128)(2,1)S(1)} %get-tuple-element.867), channel_id=1, source_target_pairs={{0,1},{1,2},{2,3},{4,5},{5,6},{6,7},{8,9},{9,10},{10,11},{12,13},{... | collective-permute-start | bytes 98312 | tf_op jit(solution)/shard_map/cond/branch_11_fun/ppermute | solution.py:416
  95.9 3.7 %collective-permute-done.139 = bf16[2,2,1,32,128]{4,3,2,1,0:T(8,128)(2,1)} collective-permute-done((bf16[2,2,1,32,128]{4,3,2,1,0:T(8,128)(2,1)S(1)}, bf16[2,2,1,32,128]{4,3,2,1,0:T(8,128)(2,1)}, u32[]{:S(2)}, u32[]{:S(2)}) %collective-permute-start.139) | collective-permute-done | bytes 32800 | tf_op jit(solution)/shard_map/cond/branch_11_fun/ppermute | solution.py:416
  99.6 2.6 %backward.1 = bf16[2,4,4,32,128]{4,3,2,1,0:T(8,128)(2,1)} custom-call(bf16[2,2,4,32,128]{4,3,2,1,0:T(8,128)(2,1)S(1)} %get-tuple-element.933.dz, bf16[2,2,1,32,128]{4,3,2,1,0:T(8,128)(2,1)} %get-tuple-element.934.low, bf16[2,2,1,32,128]{4,3,2,1,0:T(8,128)(2,1)} %get-tuple-element.935.high, bf16[27,128,128]{2,1,0:T(8,128)(2,1)S(1)} %bitcast.40), custom_call_target="tpu_custom_call" | custom-call | tf_op jit(solution)/shard_map/backward/pallas_call | solution.py:291
  102.2 3.5 %collective-permute-start.153 = (bf16[14,128,128]{2,1,0:T(8,128)(2,1)S(1)}, bf16[14,128,128]{2,1,0:T(8,128)(2,1)S(1)}, u32[]{:S(2)}, u32[]{:S(2)}) collective-permute-start(bf16[14,128,128]{2,1,0:T(8,128)(2,1)S(1)} %bitcast.13), channel_id=1, source_target_pairs={{0,4},{4,0},{1,5},{5,1},{2,6},{6,2},{3,7},{7,3},{8,12},{12,8},{9,1... | collective-permute-start | bytes 1376264 | tf_op jit(solution)/shard_map/ppermute | solution.py:399
  105.7 1.5 %own.1 = (f32[27,128,128]{2,1,0:T(8,128)}, bf16[1,2,4,32,128]{4,3,2,1,0:T(8,128)(2,1)}) custom-call(s32[1]{0:T(128)} %bitcast.6.core.first, bf16[14,128,128]{2,1,0:T(8,128)(2,1)S(1)} %bitcast.14, bf16[2,4,32,128]{3,2,1,0:T(8,128)(2,1)} %get-tuple-element.937.passed), custom_call_target="tpu_custom_call" | custom-call | tf_op jit(solution)/shard_map/own/pallas_call | solution.py:334
  (19 shorter events, 6.2 us)
Async XLA Ops:
  2.2 17.1 %collective-permute-start.33 = (bf16[2,4,32,128]{3,2,1,0:T(8,128)(2,1)}, bf16[2,4,32,128]{3,2,1,0:T(8,128)(2,1)}, u32[]{:S(2)}, u32[]{:S(2)}) collective-permute-start(bf16[2,4,32,128]{3,2,1,0:T(8,128)(2,1)} %get-tuple-element.578), channel_id=1, source_target_pairs={{0,44},{4,40},{8,36},{12,32},{16,60},{20,56},{24,52},{28,48},{32,1... | collective-permute-start | bytes 196616 | tf_op jit(solution)/shard_map/cond/branch_11_fun/ppermute | solution.py:390
  14.3 5.0 %collective-permute-start.34 = (bf16[2,4,1,32,128]{4,3,2,1,0:T(8,128)(2,1)S(1)}, bf16[2,4,1,32,128]{4,3,2,1,0:T(8,128)(2,1)}, u32[]{:S(2)}, u32[]{:S(2)}) collective-permute-start(bf16[2,4,1,32,128]{4,3,2,1,0:T(8,128)(2,1)S(1)} %get-tuple-element.579), channel_id=1, source_target_pairs={{0,1},{1,2},{2,3},{4,5},{5,6},{6,7},{8,9},{9,10},{10,11},{12,13},{... | collective-permute-start | bytes 196616 | tf_op jit(solution)/shard_map/cond/branch_11_fun/ppermute | solution.py:416
  18.0 5.7 %collective-permute-start.35 = (bf16[2,4,1,32,128]{4,3,2,1,0:T(8,128)(2,1)S(1)}, bf16[2,4,1,32,128]{4,3,2,1,0:T(8,128)(2,1)}, u32[]{:S(2)}, u32[]{:S(2)}) collective-permute-start(bf16[2,4,1,32,128]{4,3,2,1,0:T(8,128)(2,1)S(1)} %get-tuple-element.580), channel_id=1, source_target_pairs={{1,0},{2,1},{3,2},{5,4},{6,5},{7,6},{9,8},{10,9},{11,10},{13,12},{... | collective-permute-start | bytes 196616 | tf_op jit(solution)/shard_map/cond/branch_11_fun/ppermute | solution.py:416
  23.7 10.6 %copy-start = (bf16[1,2,4,32,128]{4,3,2,1,0:T(8,128)(2,1)S(1)}, bf16[1,2,4,32,128]{4,3,2,1,0:T(8,128)(2,1)}, u32[]{:S(2)}) copy-start(bf16[1,2,4,32,128]{4,3,2,1,0:T(8,128)(2,1)} %param.82) | copy-start | bytes 196612
  23.7 10.5 %collective-permute-start.93 = (bf16[2,4,32,128]{3,2,1,0:T(8,128)(2,1)}, bf16[2,4,32,128]{3,2,1,0:T(8,128)(2,1)}, u32[]{:S(2)}, u32[]{:S(2)}) collective-permute-start(bf16[2,4,32,128]{3,2,1,0:T(8,128)(2,1)} %get-tuple-element.806), channel_id=1, source_target_pairs={{0,320},{64,256},{128,448},{192,384},{256,64},{320,0},{384,192},{4... | collective-permute-start | bytes 196616 | tf_op jit(solution)/shard_map/cond/branch_21_fun/ppermute | solution.py:390
  36.9 4.5 %collective-permute-start.152 = (bf16[14,128,128]{2,1,0:T(8,128)(2,1)S(1)}, bf16[14,128,128]{2,1,0:T(8,128)(2,1)S(1)}, u32[]{:S(2)}, u32[]{:S(2)}) collective-permute-start(bf16[14,128,128]{2,1,0:T(8,128)(2,1)S(1)} %get-tuple-element.923), channel_id=1, source_target_pairs={{0,4},{4,0},{1,5},{5,1},{2,6},{6,2},{3,7},{7,3},{8,12},{12,8},{9,1... | collective-permute-start | bytes 1376264 | tf_op jit(solution)/shard_map/ppermute | solution.py:399
  42.2 57.4 %copy-start.1 = (bf16[3,3,3,128,128]{4,3,2,1,0:T(8,128)(2,1)S(1)}, bf16[3,3,3,128,128]{4,3,2,1,0:T(8,128)(2,1)}, u32[]{:S(2)}) copy-start(bf16[3,3,3,128,128]{4,3,2,1,0:T(8,128)(2,1)} %param.81) | copy-start | bytes 2654212
  42.2 24.4 %all-to-all-start = ((bf16[32,56,128]{2,1,0:T(8,128)(2,1)}), bf16[32,56,128]{2,1,0:T(8,128)(2,1)S(1)}, u32[]{:S(2)}, u32[]{:S(2)}) async-start(bf16[32,56,128]{2,1,0:T(8,128)(2,1)} %bitcast.8), calls=%async_computation | async-start | bytes 917504 | tf_op jit(solution)/shard_map/all_to_all | solution.py:427
  50.9 14.2 %collective-permute-start.101 = (bf16[2,4,32,128]{3,2,1,0:T(8,128)(2,1)S(1)}, bf16[2,4,32,128]{3,2,1,0:T(8,128)(2,1)}, u32[]{:S(2)}, u32[]{:S(2)}) collective-permute-start(bf16[2,4,32,128]{3,2,1,0:T(8,128)(2,1)S(1)} %param.53), channel_id=1, source_target_pairs={{0,320},{64,256},{128,448},{192,384},{256,64},{320,0},{384,192},{4... | collective-permute-start | bytes 196616 | tf_op jit(solution)/shard_map/cond/branch_5_fun/ppermute | solution.py:390
  78.8 23.4 %all-to-all-start.2 = ((bf16[32,56,128]{2,1,0:T(8,128)(2,1)}), bf16[32,56,128]{2,1,0:T(8,128)(2,1)S(1)}, u32[]{:S(2)}, u32[]{:S(2)}) async-start(bf16[32,56,128]{2,1,0:T(8,128)(2,1)} %spread.3), calls=%async_computation.2 | async-start | bytes 917504 | tf_op jit(solution)/shard_map/all_to_all | solution.py:432
  86.1 13.5 %collective-permute-start.137 = (bf16[2,4,32,128]{3,2,1,0:T(8,128)(2,1)}, bf16[2,4,32,128]{3,2,1,0:T(8,128)(2,1)}, u32[]{:S(2)}, u32[]{:S(2)}) collective-permute-start(bf16[2,4,32,128]{3,2,1,0:T(8,128)(2,1)} %get-tuple-element.866), channel_id=1, source_target_pairs={{0,44},{4,40},{8,36},{12,32},{16,60},{20,56},{24,52},{28,48},{32,1... | collective-permute-start | bytes 196616 | tf_op jit(solution)/shard_map/cond/branch_11_fun/ppermute | solution.py:390
  90.6 5.3 %collective-permute-start.138 = (bf16[2,2,1,32,128]{4,3,2,1,0:T(8,128)(2,1)S(1)}, bf16[2,2,1,32,128]{4,3,2,1,0:T(8,128)(2,1)}, u32[]{:S(2)}, u32[]{:S(2)}) collective-permute-start(bf16[2,2,1,32,128]{4,3,2,1,0:T(8,128)(2,1)S(1)} %get-tuple-element.867), channel_id=1, source_target_pairs={{0,1},{1,2},{2,3},{4,5},{5,6},{6,7},{8,9},{9,10},{10,11},{12,13},{... | collective-permute-start | bytes 98312 | tf_op jit(solution)/shard_map/cond/branch_11_fun/ppermute | solution.py:416
  94.6 5.0 %collective-permute-start.139 = (bf16[2,2,1,32,128]{4,3,2,1,0:T(8,128)(2,1)S(1)}, bf16[2,2,1,32,128]{4,3,2,1,0:T(8,128)(2,1)}, u32[]{:S(2)}, u32[]{:S(2)}) collective-permute-start(bf16[2,2,1,32,128]{4,3,2,1,0:T(8,128)(2,1)S(1)} %get-tuple-element.868), channel_id=1, source_target_pairs={{1,0},{2,1},{3,2},{5,4},{6,5},{7,6},{9,8},{10,9},{11,10},{13,12},{... | collective-permute-start | bytes 98312 | tf_op jit(solution)/shard_map/cond/branch_11_fun/ppermute | solution.py:416
  102.2 5.1 %collective-permute-start.153 = (bf16[14,128,128]{2,1,0:T(8,128)(2,1)S(1)}, bf16[14,128,128]{2,1,0:T(8,128)(2,1)S(1)}, u32[]{:S(2)}, u32[]{:S(2)}) collective-permute-start(bf16[14,128,128]{2,1,0:T(8,128)(2,1)S(1)} %bitcast.13), channel_id=1, source_target_pairs={{0,4},{4,0},{1,5},{5,1},{2,6},{6,2},{3,7},{7,3},{8,12},{12,8},{9,1... | collective-permute-start | bytes 1376264 | tf_op jit(solution)/shard_map/ppermute | solution.py:399
